TPU v7x, 32 devices: a whole 2x2x4 slice. The times are simulated.
32 devices in a mesh: seq: 32 (over z, y, x, core), chan: 1.
Axes of the slice: x: 2, y: 2, z: 4, core: 2. Of those that a mesh axis runs over, the one named last changes fastest.
Arguments:
- tokens: bfloat16 [1536, 16384], P('chan', 'seq'), may hold values from -6 to 6
- gate_weight: bfloat16 [1536, 1536], P('chan'), may hold values from -0.15625 to 0.15625
- value_weight: bfloat16 [1536, 1536], P('chan'), may hold values from -0.15625 to 0.15625
- first_factor: bfloat16 [64, 256, 256], P('seq'), may hold values from -0.375 to 0.375
- second_factor: bfloat16 [256, 64, 64], P('seq'), may hold values from -0.75 to 0.75
- down_latent: bfloat16 [1536, 128], P('chan'), may hold values from -0.15625 to 0.15625
- up_latent: bfloat16 [1536, 128], P('chan'), may hold values from -0.5 to 0.5
- doc_lengths: int32 [64], replicated, may hold values from 1 to 8704, 16384 in all
- cotangent: bfloat16 [1536, 16384], P('chan', 'seq'), may hold values from -6 to 6
Outputs:
- hidden: bfloat16 [1536, 16384], P('chan', 'seq')
- d_gate_weight: float32 [1536, 1536], P('chan')
- d_value_weight: float32 [1536, 1536], P('chan')
- d_first: float32 [64, 256, 256], P('seq', 'chan')
- d_second: float32 [256, 64, 64], P('seq', 'chan')
- d_down: float32 [1536, 128], P('chan')
- d_up: float32 [1536, 128], P('chan')
Inputs may be any that keep to these rules, and one draw needn't show every extreme that they name: `doc_lengths`: the documents' lengths sum to 16384; the longest is exactly 8704 tokens.
All inputs are finite; a program needn't handle non-finite values.
Results may differ from a plain program's by a relative error of at most 0.0058.
Values may be sent and summed in bfloat16 or wider, within the bound.
A program may use at most 128 MiB of HBM per device.

v0:
```python
import jax
import jax.numpy as jnp
from jax import lax
from jax.sharding import PartitionSpec as P


def body(
    tokens,
    gate_weight,
    value_weight,
    first_factor,
    second_factor,
    down_latent,
    up_latent,
    doc_lengths,
    cotangent,
):
    highest = lax.Precision.HIGHEST
    chan_rows, tok_cols = tokens.shape
    block_width = first_factor.shape[1]
    blocks_here = tok_cols // block_width
    gathered = lax.all_gather(tokens, "chan", axis=0, tiled=True)
    gate_pre = jnp.dot(gate_weight, gathered, preferred_element_type=jnp.float32)
    value_acc = jnp.dot(value_weight, gathered, preferred_element_type=jnp.float32)
    value_bf = value_acc.astype(jnp.bfloat16)
    doc_ends = jnp.cumsum(doc_lengths)
    doc_begins = doc_ends - doc_lengths
    position = lax.axis_index("seq") * tok_cols + jnp.arange(tok_cols, dtype=jnp.int32)
    member = (
        (position[None, :] >= doc_begins[:, None]) & (position[None, :] < doc_ends[:, None])
    ).astype(jnp.float32)
    len_scale = lax.rsqrt(doc_lengths.astype(jnp.float32))
    latent_part = jnp.einsum("ct,cl->lt", tokens, down_latent, preferred_element_type=jnp.float32)
    latent_full = lax.psum(latent_part, "chan")
    doc_sums = lax.psum(jnp.einsum("dt,lt->dl", member, latent_full, precision=highest), "seq")
    pooled = doc_sums * len_scale[:, None]
    up_float = up_latent.astype(jnp.float32)
    spread_rows = jnp.einsum("cl,dl->cd", up_float, pooled, precision=highest)
    summary = jnp.dot(spread_rows, member, precision=highest)
    blocked = value_bf.reshape(chan_rows, blocks_here, block_width)
    inner_mix = jnp.einsum(
        "ikj,cij->kic", first_factor, blocked, preferred_element_type=jnp.float32
    ).astype(jnp.bfloat16)
    columns = lax.all_to_all(inner_mix, "seq", split_axis=0, concat_axis=1, tiled=True)
    outer_mix = jnp.einsum(
        "kmi,kic->kmc", second_factor, columns, preferred_element_type=jnp.float32
    ).astype(jnp.bfloat16)
    mixed_back = lax.all_to_all(outer_mix, "seq", split_axis=1, concat_axis=0, tiled=True)
    mixed = (
        jnp.transpose(mixed_back, (2, 1, 0)).reshape(chan_rows, tok_cols).astype(jnp.float32)
        + summary
    )
    sig = jax.nn.sigmoid(gate_pre)
    act = gate_pre * sig
    hidden = (act * mixed).astype(jnp.bfloat16)
    upstream = cotangent.astype(jnp.float32)
    d_mixed = upstream * act
    d_mixed_bf = d_mixed.astype(jnp.bfloat16)
    d_gate_bf = (upstream * mixed * sig * (1.0 + gate_pre * (1.0 - sig))).astype(jnp.bfloat16)
    d_send = jnp.transpose(d_mixed_bf.reshape(chan_rows, blocks_here, block_width), (2, 1, 0))
    d_outer = lax.all_to_all(d_send, "seq", split_axis=0, concat_axis=1, tiled=True)
    d_inner = jnp.einsum(
        "kmi,kmc->kic", second_factor, d_outer, preferred_element_type=jnp.float32
    ).astype(jnp.bfloat16)
    d_second_part = jnp.einsum("kmc,kic->kmi", d_outer, columns, preferred_element_type=jnp.float32)
    d_rows = lax.all_to_all(d_inner, "seq", split_axis=1, concat_axis=0, tiled=True)
    d_value_bf = (
        jnp.einsum("ikj,kic->cij", first_factor, d_rows, preferred_element_type=jnp.float32)
        .astype(jnp.bfloat16)
        .reshape(chan_rows, tok_cols)
    )
    d_first_part = jnp.einsum("kic,cij->ikj", d_rows, blocked, preferred_element_type=jnp.float32)
    per_doc = jnp.einsum("ct,dt->cd", d_mixed, member, precision=highest)
    d_up_part = jnp.einsum("cd,dl->cl", per_doc, pooled, precision=highest)
    d_pooled = lax.psum(
        jnp.einsum("cd,cl->dl", per_doc, up_float, precision=highest), ("seq", "chan")
    )
    d_latent_bf = jnp.einsum(
        "dl,dt->lt", d_pooled * len_scale[:, None], member, precision=highest
    ).astype(jnp.bfloat16)
    d_down_part = jnp.einsum("ct,lt->cl", tokens, d_latent_bf, preferred_element_type=jnp.float32)
    both_grads = jnp.concatenate([d_gate_bf, d_value_bf], axis=0)
    d_proj = jnp.einsum("ot,it->oi", both_grads, gathered, preferred_element_type=jnp.float32)
    d_proj, d_down, d_up = lax.psum((d_proj, d_down_part, d_up_part), "seq")
    d_first, d_second = (
        lax.psum_scatter(d_first_part, "chan", scatter_dimension=1, tiled=True),
        lax.psum_scatter(d_second_part, "chan", scatter_dimension=1, tiled=True),
    )
    return (hidden, d_proj[:chan_rows], d_proj[chan_rows:], d_first, d_second, d_down, d_up)


def solution(mesh):
    in_specs = (
        P("chan", "seq"),
        P("chan", None),
        P("chan", None),
        P("seq", None, None),
        P("seq", None, None),
        P("chan", None),
        P("chan", None),
        P(),
        P("chan", "seq"),
    )
    out_specs = (
        P("chan", "seq"),
        P("chan", None),
        P("chan", None),
        P("seq", "chan", None),
        P("seq", "chan", None),
        P("chan", None),
        P("chan", None),
    )
    return jax.shard_map(body, mesh=mesh, in_specs=in_specs, out_specs=out_specs, check_vma=False)
```

profile of v0, /device:TPU:0, one launch (start us, length us, event | category | flops | bytes accessed | tf_op | source)
XLA Modules:
  0.0 678.4 jit_solution(18342726926857652732)
XLA Ops:
  7.2 1.4 copy-done
  8.6 5.0 convolution_convert_fusion.4
  13.6 1.1 copy-done.6
  14.7 1.9 fusion.8
  16.6 3.8 copy.44
  20.4 45.1 %all_to_all.66 = bf16[256,2,1536]{2,1,0:T(2,128)(2,1)S(1)} all-to-all(bf16[256,2,1536]{2,1,0:T(2,128)(2,1)S(1)} %copy.44), channel_id=1, replica_groups=mesh['seq'=32,'chan'=1] {'seq'}, dimensions={0} | all-to-all | bytes 3145728 | tf_op jit(solution)/shard_map/all_to_all | solution.py:44
  65.5 0.2 copy.79
  65.7 2.8 copy.46
  68.4 3.7 all_to_all.51
  72.1 0.6 fusion.10
  72.7 2.0 copy.47
  74.7 3.5 all-to-all-start.1
  78.3 0.2 all-reduce.5.cloned.1.call-start
  78.7 0.1 reduce
  78.8 2.6 copy.51
  81.5 0.4 fusion.31
  81.9 0.9 fusion.27
  82.8 4.7 fusion.30
  87.5 2.1 fusion.11
  89.6 0.7 copy-done.4
  90.4 0.9 fusion.33
  91.4 121.7 %all-reduce.5.cloned.1.call-done = (f32[64,128]{1,0:T(8,128)}, f32[64,128]{1,0:T(8,128)}) async-done(((f32[64,128]{1,0:T(8,128)}, f32[64,128]{1,0:T(8,128)}), (f32[64,128]{1,0:T(8,128)}, f32[64,128]{1,0:T(8,128)})) %all-reduce.5.cloned.1.call-update) | async-done | bytes 65552 | tf_op jit(solution)/shard_map/psum | solution.py:35
  213.1 2.1 fusion.21
  215.2 1.8 convert_bitcast_fusion
  217.0 0.2 copy.48
  217.3 1.1 copy-done.2
  218.5 1.0 copy-done.21
  219.5 4.5 fusion.2
  224.0 1.6 copy.78
  225.7 43.5 %all_to_all.67 = bf16[256,2,1536]{2,1,0:T(2,128)(2,1)S(1)} all-to-all(bf16[256,2,1536]{2,1,0:T(2,128)(2,1)S(1)} %bitcast.69), channel_id=1, replica_groups=mesh['seq'=32,'chan'=1] {'seq'}, dimensions={0} | all-to-all | bytes 3145728 | tf_op jit(solution)/shard_map/all_to_all | solution.py:61
  269.2 2.4 copy.77
  271.6 4.7 all_to_all.57
  276.2 2.0 fusion.9
  278.3 2.0 copy.55
  280.3 3.5 all-to-all-start.3
  283.9 1.1 convolution_convert_fusion.5
  285.0 3.1 fusion.19
  288.1 1.5 convolution_bitcast_fusion
  289.6 32.0 %all-to-all-done.3 = bf16[8,64,1536]{2,0,1:T(8,128)(2,1)} async-done(((bf16[8,64,1536]{2,0,1:T(8,128)(2,1)}), bf16[8,64,1536]{2,0,1:T(8,128)(2,1)}, u32[]{:S(2)}, u32[]{:S(2)}) %all-to-all-start.3) | async-done | bytes 1572896 | tf_op jit(solution)/shard_map/all_to_all | solution.py:66
  321.7 2.1 convolution_convert_fusion.1
  323.8 9.3 %fusion.3 = f32[3072,1536]{1,0:T(8,128)} fusion(bf16[1536,512]{1,0:T(8,128)(2,1)S(1)} %copy-done, bf16[1536,512]{0,1:T(8,128)(2,1)S(1)} %bitcast.76, bf16[1536,512]{0,1:T(8,128)(2,1)S(1)} %copy-done.19), kind=kOutput, calls=%fused_computation.6 | convolution fusion | flops 4838129664 | bytes 23592960 | tf_op jit(solution)/shard_map/ot,it->oi/dot_general | solution.py:83
  333.2 2.6 copy.59
  335.8 2.8 fusion.32
  338.6 2.9 fusion.13
  341.5 314.9 %all-reduce.7.cloned.1.call-done = (f32[3072,1536]{1,0:T(8,128)}, f32[1536,128]{0,1:T(8,128)}, f32[1536,128]{1,0:T(8,128)}) async-done(((f32[3072,1536]{1,0:T(8,128)}, f32[1536,128]{0,1:T(8,128)}, f32[1536,128]{1,0:T(8,128)}), (f32[3072,1536]{1,0:T(8,128)}, f32[1536,128]{0,1:T(8,128)}, f32[1536,128]{1,0:T(8,128)})) %all-reduce.7.cloned.1.call-update) | async-done | bytes 20447248 | tf_op jit(solution)/shard_map/psum | solution.py:84
  656.4 13.1 %fusion.29 = (f32[1536,1536]{1,0:T(8,128)}, f32[1536,1536]{1,0:T(8,128)}) fusion(f32[3072,1536]{1,0:T(8,128)} %get-tuple-element.30), kind=kLoop, calls=%fused_computation.47 | loop fusion | bytes 37748736 | tf_op jit(solution)/shard_map/slice | solution.py:89
  669.5 1.1 copy.60
  670.6 0.9 copy.85
  (48 shorter events, 0.4 us)
Async XLA Ops:
  7.2 1.4 copy-start
  7.2 7.5 %copy-start.8 = (bf16[2,256,256]{2,1,0:T(8,128)(2,1)S(1)}, bf16[2,256,256]{2,1,0:T(8,128)(2,1)}, u32[]{:S(2)}) copy-start(bf16[2,256,256]{2,1,0:T(8,128)(2,1)} %param.12) | copy-start | bytes 786436
  13.6 1.1 copy-start.6
  68.4 3.7 copy-start.12
  74.7 3.8 copy-start.16
  74.7 140.5 %all-to-all-start.1 = ((bf16[8,64,1536]{2,0,1:T(8,128)(2,1)}), bf16[8,64,1536]{2,0,1:T(8,128)(2,1)}, u32[]{:S(2)}, u32[]{:S(2)}) async-start(bf16[8,64,1536]{2,0,1:T(8,128)(2,1)} %copy.47), calls=%async_computation.1 | async-start | bytes 3145728 | tf_op jit(solution)/shard_map/all_to_all | solution.py:48
  78.3 134.8 %all-reduce.5.cloned.1.call-start = ((), (), s32[]{:S(2)}) async-start(), calls=%async_computation.4 | async-start | bytes 131072 | tf_op jit(solution)/shard_map/psum | solution.py:35
  78.8 8.7 %copy-start.17 = (s32[64]{0:T(128)}, s32[64]{0:T(128)S(1)}, u32[]{:S(2)}) copy-start(s32[64]{0:T(128)S(1)} %sub.6) | copy-start | bytes 772
  78.8 2.6 copy-start.15
  82.8 4.7 copy-start.1
  87.5 2.1 copy-start.20
  87.5 2.9 copy-start.3
  89.6 0.7 copy-start.4
  217.0 1.4 copy-start.2
  217.0 1.5 copy-start.14
  217.0 1.5 copy-start.18
  217.0 2.5 copy-start.21
  271.6 4.7 copy-start.13
  280.3 4.8 copy-start.5
  280.3 41.4 %all-to-all-start.3 = ((bf16[8,64,1536]{2,0,1:T(8,128)(2,1)}), bf16[8,64,1536]{2,0,1:T(8,128)(2,1)}, u32[]{:S(2)}, u32[]{:S(2)}) async-start(bf16[8,64,1536]{2,0,1:T(8,128)(2,1)} %copy.55), calls=%async_computation.3 | async-start | bytes 3145728 | tf_op jit(solution)/shard_map/all_to_all | solution.py:66
  283.8 372.6 %all-reduce.7.cloned.1.call-start = ((), (), s32[]{:S(2)}) async-start(), calls=%async_computation.5 | async-start | bytes 40894464 | tf_op jit(solution)/shard_map/psum | solution.py:84
  288.1 33.6 %copy-start.9 = (bf16[2,256,256]{2,1,0:T(8,128)(2,1)S(1)}, bf16[2,256,256]{2,1,0:T(8,128)(2,1)}, u32[]{:S(2)}) copy-start(bf16[2,256,256]{2,1,0:T(8,128)(2,1)} %param.12) | copy-start | bytes 786436
  321.7 2.2 copy-start.19
  335.8 2.8 copy-start.7
  656.4 13.1 %copy-start.11 = (f32[1536,128]{0,1:T(8,128)S(1)}, f32[1536,128]{0,1:T(8,128)}, u32[]{:S(2)}) copy-start(f32[1536,128]{0,1:T(8,128)} %get-tuple-element.31) | copy-start | bytes 2359300
  669.5 1.2 copy-start.10
Sparse Core Ops, SparseCore 0:
  91.5 121.5 all-reduce.4
  333.3 323.0 all-reduce.6
where the time goes:
time: 679 us; the launch traced here: 678 us
  waiting for transfers between devices  469 us (69%)
  blocking collectives  88.7 us (13%)
  local copies, waits for them, and re-layouts  49.2 us (7%)
  matrix products  48 us (7%)
  between operations  14.3 us (2%)
  starting transfers between devices  7.36 us (1%)
    psum x1, waiting for transfers between devices, body(): d_proj, d_down, d_up = lax.psum((d_proj, d_down_part, d_up_part), 'seq')  315 us
    psum x1, waiting for transfers between devices, body(): lax.psum(jnp.einsum('dt,lt->dl', member, latent_full, precision=highest),...  122 us
    all_to_all x1, blocking collectives, body(): lax.all_to_all(inner_mix, 'seq', split_axis=0, concat_axis=1, tiled=True)  45.1 us
    all_to_all x1, blocking collectives, body(): lax.all_to_all(d_send, 'seq', split_axis=0, concat_axis=1, tiled=True)  43.5 us
    all_to_all x1, waiting for transfers between devices, body(): lax.all_to_all(d_inner, 'seq', split_axis=1, concat_axis=0, tiled=True)  32 us
  transfers between devices with their start and end apart: 4, of which 3 were waited for; matrix products, arithmetic and copies ran while one was open for 4% of the time, Pallas kernels for 0%

commit v1 on v0

--- a/solution.py
+++ b/solution.py
@@ -1,3 +1,5 @@
+import functools
+
 import jax
 import jax.numpy as jnp
 from jax import lax
@@ -89,7 +91,188 @@
     return (hidden, d_proj[:chan_rows], d_proj[chan_rows:], d_first, d_second, d_down, d_up)
 
 
+ROWS = 8
+
+
+def swap(value, n, bit):
+    pairs = [(i, i ^ (1 << bit)) for i in range(n)]
+    return lax.ppermute(value, "seq", pairs)
+
+
+def scatter_sum(part, n, bits, index):
+    for bit in bits:
+        half = part.shape[0] // 2
+        mine = (index >> bit) & 1
+        sent = lax.dynamic_slice_in_dim(part, (1 - mine) * half, half, 0)
+        kept = lax.dynamic_slice_in_dim(part, mine * half, half, 0)
+        got = swap(sent.astype(jnp.bfloat16), n, bit)
+        part = kept + got.astype(jnp.float32)
+    return part
+
+
+def gather_all(piece, n, bits, index):
+    for bit in reversed(bits):
+        half = piece.shape[0]
+        mine = (index >> bit) & 1
+        got = swap(piece, n, bit)
+        whole = jnp.zeros((2 * half,) + piece.shape[1:], piece.dtype)
+        whole = lax.dynamic_update_slice_in_dim(whole, piece, mine * half, 0)
+        piece = lax.dynamic_update_slice_in_dim(whole, got, (1 - mine) * half, 0)
+    return piece
+
+
+def streams_of(n):
+    top = n.bit_length() - 1
+    rest = list(range(1, top))
+    orders = []
+    for s in range(min(3, max(1, len(rest)))):
+        if s == 0:
+            order = rest
+        elif s == 1:
+            order = [rest[1], rest[0]] + rest[2:]
+        else:
+            order = rest[2:] + rest[:2]
+        orders.append(order)
+    return orders
+
+
+def reduce_all(part, n, index):
+    rows, cols = part.shape
+    orders = streams_of(n)
+    unit = n // 2
+    low = 0
+    blocks = part.reshape(2, rows // (2 * ROWS), ROWS, cols)
+    mine = index & 1
+    sent = lax.dynamic_index_in_dim(blocks, 1 - mine, 0, keepdims=False)
+    kept = lax.dynamic_index_in_dim(blocks, mine, 0, keepdims=False)
+    count = sent.shape[0] // unit
+    shares = [(count * (s + 1)) // len(orders) - (count * s) // len(orders) for s in range(len(orders))]
+    shares.sort(reverse=True)
+    done = []
+    for share, order in zip(shares, orders):
+        if share == 0:
+            continue
+        at, size = low * unit, share * unit
+        low += share
+        got = swap(sent[at : at + size].astype(jnp.bfloat16), n, 0)
+        piece = kept[at : at + size] + got.astype(jnp.float32)
+        piece = scatter_sum(piece, n, order, index).astype(jnp.bfloat16)
+        done.append((at, size, gather_all(piece, n, order, index)))
+    ours = jnp.concatenate([piece for _, _, piece in done], axis=0)
+    theirs = swap(ours, n, 0)
+    first = jnp.where(mine == 0, ours, theirs)
+    second = jnp.where(mine == 0, theirs, ours)
+    return first, second
+
+
+def seq_body(
+    n,
+    tokens,
+    gate_weight,
+    value_weight,
+    first_factor,
+    second_factor,
+    down_latent,
+    up_latent,
+    doc_lengths,
+    cotangent,
+):
+    highest = lax.Precision.HIGHEST
+    f32, bf16 = jnp.float32, jnp.bfloat16
+    width, count = tokens.shape
+    here, block, _ = first_factor.shape
+    share = second_factor.shape[0]
+    index = lax.axis_index("seq")
+
+    gate_pre = jnp.einsum("ct,oc->to", tokens, gate_weight, preferred_element_type=f32)
+    sig = jax.nn.sigmoid(gate_pre)
+    act = gate_pre * sig
+    upstream = cotangent.T.astype(f32)
+    d_mixed = upstream * act
+    d_mixed_bf = d_mixed.astype(bf16)
+
+    doc_ends = jnp.cumsum(doc_lengths)
+    doc_begins = doc_ends - doc_lengths
+    position = index * count + jnp.arange(count, dtype=jnp.int32)
+    member = (
+        (position[None, :] >= doc_begins[:, None]) & (position[None, :] < doc_ends[:, None])
+    ).astype(f32)
+    len_scale = lax.rsqrt(doc_lengths.astype(f32))
+    up_float = up_latent.astype(f32)
+    latent = jnp.einsum("ct,cl->tl", tokens, down_latent, preferred_element_type=f32)
+    doc_part = jnp.dot(member, latent, precision=highest)
+    per_doc = jnp.dot(member, d_mixed, precision=highest)
+    d_pooled_part = jnp.dot(per_doc, up_float, precision=highest)
+    small = jnp.concatenate([doc_part, d_pooled_part], axis=0)
+
+    value_bf = jnp.einsum("ct,oc->to", tokens, value_weight, preferred_element_type=f32).astype(bf16)
+    blocked = value_bf.reshape(here, block, width)
+    inner_mix = jnp.einsum("ikj,ijc->ikc", first_factor, blocked, preferred_element_type=f32).astype(bf16)
+
+    def outward(rows):
+        rows = rows.reshape(here, n, share, width)
+        return jnp.transpose(rows, (1, 0, 2, 3))
+
+    def across(rows):
+        return lax.all_to_all(rows, "seq", split_axis=0, concat_axis=0, tiled=True)
+
+    inner_out = outward(inner_mix)
+    inner_out, small = lax.optimization_barrier((inner_out, small))
+    small = lax.psum(small, "seq")
+    inner_k = across(inner_out).reshape(n * here, share, width)
+    d_outer_k = across(outward(d_mixed_bf)).reshape(n * here, share, width)
+    outer_k = jnp.einsum("kmi,ikc->mkc", second_factor, inner_k, preferred_element_type=f32).astype(bf16)
+    outer_back = across(outer_k.reshape(n, here, share, width))
+    d_inner_k = jnp.einsum("kmi,mkc->ikc", second_factor, d_outer_k, preferred_element_type=f32).astype(bf16)
+    d_inner_back = across(d_inner_k.reshape(n, here, share, width))
+    d_second = jnp.einsum("mkc,ikc->kmi", d_outer_k, inner_k, preferred_element_type=f32)
+
+    docs = doc_part.shape[0]
+    pooled = small[:docs] * len_scale[:, None]
+    d_pooled = small[docs:] * len_scale[:, None]
+    spread = jnp.dot(pooled, up_float.T, precision=highest)
+    summary = jnp.einsum("dt,dc->tc", member, spread, precision=highest)
+    mixed = jnp.transpose(outer_back, (1, 0, 2, 3)).reshape(count, width).astype(f32) + summary
+    hidden = (act * mixed).astype(bf16).T
+    d_gate_bf = (upstream * mixed * sig * (1.0 + gate_pre * (1.0 - sig))).astype(bf16)
+    d_up_part = jnp.einsum("dl,dc->lc", pooled, per_doc, precision=highest)
+    d_latent_bf = jnp.einsum("dl,dt->lt", d_pooled, member, precision=highest).astype(bf16)
+    d_down_part = jnp.einsum("lt,ct->lc", d_latent_bf, tokens, preferred_element_type=f32)
+
+    d_rows = jnp.transpose(d_inner_back, (1, 0, 2, 3)).reshape(here, block, width)
+    d_value_bf = (
+        jnp.einsum("ikj,ikc->ijc", first_factor, d_rows, preferred_element_type=f32)
+        .astype(bf16)
+        .reshape(count, width)
+    )
+    d_first = jnp.einsum("ikc,ijc->ikj", d_rows, blocked, preferred_element_type=f32)
+    gate_part = jnp.einsum("to,it->oi", d_gate_bf, tokens, preferred_element_type=f32)
+    value_part = jnp.einsum("to,it->oi", d_value_bf, tokens, preferred_element_type=f32)
+    lats = d_up_part.shape[0]
+    first, second = reduce_all(
+        jnp.concatenate([gate_part, d_up_part, value_part, d_down_part], axis=0), n, index
+    )
+    first = first.reshape(-1, width)
+    second = second.reshape(-1, width)
+    return (
+        hidden,
+        first[:width].astype(f32),
+        second[:width].astype(f32),
+        d_first,
+        d_second,
+        second[width : width + lats].astype(f32).T,
+        first[width : width + lats].astype(f32).T,
+    )
+
+
+def fits(n):
+    return n >= 8 and n & (n - 1) == 0
+
+
 def solution(mesh):
+    n = mesh.shape["seq"]
+    local = mesh.shape["chan"] == 1 and fits(n)
+    run = functools.partial(seq_body, n) if local else body
     in_specs = (
         P("chan", "seq"),
         P("chan", None),
@@ -110,4 +293,4 @@
         P("chan", None),
         P("chan", None),
     )
-    return jax.shard_map(body, mesh=mesh, in_specs=in_specs, out_specs=out_specs, check_vma=False)
+    return jax.shard_map(run, mesh=mesh, in_specs=in_specs, out_specs=out_specs, check_vma=False)

time: 679 us -> 541 us (0.80); the launches traced: 678 us -> 533 us
  waiting for transfers between devices: 469 us -> 287 us
  other arithmetic: 2.02 us -> 41.3 us
  starting transfers between devices: 7.36 us -> 21.8 us
  local copies, waits for them, and re-layouts: 49.2 us -> 37 us
    psum x2 -> x1, waiting for transfers between devices: 437 us -> 128 us  [seq_body(): small = lax.psum(small, 'seq')]
    ppermute x0 -> x28, waiting for transfers between devices: none -> 136 us  [swap(): return lax.ppermute(value, 'seq', pairs)]
    ppermute x0 -> x28, starting transfers between devices: none -> 15.2 us  [swap(): return lax.ppermute(value, 'seq', pairs)]
    convert_element_type x1 -> x3, other arithmetic: 1.81 us -> 16.3 us  [the longest x1 13.4 us: seq_body(): second[:width].astype(f32)]
    all_to_all x5 -> x0, local copies, waits for them, and re-layouts: 13.6 us -> none  [the longest x2 7.01 us: body(): lax.all_to_all(d_send, 'seq', split_axis=0, concat_axis=1, tiled=True)]
    slice x1 -> x0, local copies, waits for them, and re-layouts: 13.1 us -> none  [body(): d_proj[chan_rows:]]
    concatenate x0 -> x3, other arithmetic: none -> 11.5 us  [the longest x1 8.08 us: seq_body(): jnp.concatenate([gate_part, d_up_part, value_part, d_down_part], axis=0)]
    all_to_all x2, waiting for transfers between devices: 32 us -> 22.6 us  [across(): return lax.all_to_all(rows, 'seq', split_axis=0, concat_axis=0, tiled=True)]
  transfers between devices with their start and end apart: 4 -> 31, of which waited for: 3 -> 21; matrix products, arithmetic and copies ran while one was open for 4% -> 7% of each run, Pallas kernels for 0% -> 0%
where the time goes in v1:
time: 541 us; the launch traced here: 533 us
  waiting for transfers between devices  287 us (53%)
  blocking collectives  88.3 us (16%)
  matrix products  42.1 us (8%)
  other arithmetic  41.3 us (8%)
  local copies, waits for them, and re-layouts  37 us (7%)
  starting transfers between devices  21.8 us (4%)
  between operations  15.4 us (3%)
    ppermute x28, waiting for transfers between devices, swap(): return lax.ppermute(value, 'seq', pairs)  136 us
    psum x1, waiting for transfers between devices, seq_body(): small = lax.psum(small, 'seq')  128 us
    all_to_all x2, blocking collectives, across(): return lax.all_to_all(rows, 'seq', split_axis=0, concat_axis=0, tiled=True)  88.3 us
    all_to_all x2, waiting for transfers between devices, across(): return lax.all_to_all(rows, 'seq', split_axis=0, concat_axis=0, tiled=True)  22.6 us
    unnamed x68, local copies, waits for them, and re-layouts  17.4 us
    ppermute x28, starting transfers between devices, swap(): return lax.ppermute(value, 'seq', pairs)  15.2 us
    convert_element_type x1, other arithmetic, seq_body(): second[:width].astype(f32)  13.4 us
  transfers between devices with their start and end apart: 31, of which 21 were waited for; matrix products, arithmetic and copies ran while one was open for 7% of the time, Pallas kernels for 0%

profile of v1, /device:TPU:0, one launch (start us, length us, event | category | flops | bytes accessed | tf_op | source)
XLA Modules:
  0.0 533.0 jit_solution(12113969765376970978)
XLA Ops:
  8.9 2.6 copy.46
  11.6 4.7 fusion.36
  17.0 2.7 convolution_convert_fusion.4
  21.7 2.1 fusion.13
  25.5 45.1 %all_to_all.20 = bf16[32,2,8,1536]{3,2,1,0:T(8,128)(2,1)S(1)} all-to-all(bf16[32,2,8,1536]{3,2,1,0:T(8,128)(2,1)S(1)} %bitcast.123), channel_id=1, replica_groups=mesh['seq'=32,'chan'=1] {'seq'}, dimensions={0} | all-to-all | bytes 3145728 | tf_op jit(solution)/shard_map/all_to_all | solution.py:217
  71.9 2.0 copy.62
  73.9 3.1 all-to-all-start.1
  78.4 127.6 %all-reduce.2.cloned.1.call-done = f32[128,128]{1,0:T(8,128)} async-done(((f32[128,128]{1,0:T(8,128)}), f32[128,128]{1,0:T(8,128)}) %all-reduce.2.cloned.1.call-update) | async-done | bytes 65552 | tf_op jit(solution)/shard_map/psum | solution.py:221
  206.0 2.1 fusion.29
  211.9 2.5 fusion.12
  214.6 43.2 %all_to_all.21 = bf16[32,2,8,1536]{3,2,1,0:T(8,128)(2,1)S(1)} all-to-all(bf16[32,2,8,1536]{3,2,1,0:T(8,128)(2,1)S(1)} %bitcast.124), channel_id=1, replica_groups=mesh['seq'=32,'chan'=1] {'seq'}, dimensions={0} | all-to-all | bytes 3145728 | tf_op jit(solution)/shard_map/all_to_all | solution.py:217
  259.0 2.5 fusion.9
  261.4 3.5 reshape.106
  264.9 2.9 copy.53
  267.8 3.3 all-to-all-start.3
  272.4 2.5 fusion.28
  276.5 9.7 %fusion.15 = f32[1536,1536]{1,0:T(8,128)} fusion(bf16[1536,512]{1,0:T(8,128)(2,1)S(1)} %copy-done, f32[512,1536]{1,0:T(8,128)S(1)} %copy-done.7, bf16[1536,512]{0,1:T(8,128)(2,1)} %copy.46, f32[512,1536]{1,0:T(8,128)} %copy-done.15), kind=kOutput, calls=%fused_computation.39 | convolution fusion | flops 2424569856 | bytes 18874368 | tf_op jit(solution)/shard_map/to,it->oi/dot_general | solution.py:249
  286.2 22.6 %all-to-all-done.3 = bf16[32,2,8,1536]{3,1,2,0:T(2,128)(2,1)S(1)} async-done(((bf16[32,2,8,1536]{3,1,2,0:T(2,128)(2,1)}), bf16[32,2,8,1536]{3,1,2,0:T(2,128)(2,1)S(1)}, u32[]{:S(2)}, u32[]{:S(2)}) %all-to-all-start.3) | async-done | bytes 1572896 | tf_op jit(solution)/shard_map/all_to_all | solution.py:217
  309.5 2.7 fusion.39
  313.5 8.1 %pad_maximum_fusion = f32[3328,1536]{1,0:T(8,128)} fusion(f32[128,1536]{1,0:T(8,128)S(1)} %copy-done.17, f32[1536,1536]{1,0:T(8,128)S(1)} %fusion.39, f32[128,1536]{1,0:T(8,128)S(1)} %copy-done.18, f32[1536,1536]{1,0:T(8,128)S(1)} %copy-done.8), kind=kLoop, calls=%fused_computation | loop fusion | flops 15335424 | bytes 40894464 | tf_op jit(solution)/shard_map/concatenate | solution.py:253
  321.6 4.5 dynamic-slice_convert_fusion
  326.1 1.9 slice_bitcast_fusion.4
  329.9 3.9 collective-permute-done.18
  333.8 2.0 collective-permute-done.9
  335.9 4.4 fusion.4
  341.9 2.7 fusion.2
  346.3 14.0 %collective-permute-done.10 = bf16[32,8,1536]{2,1,0:T(8,128)(2,1)S(1)} collective-permute-done((bf16[32,8,1536]{2,1,0:T(8,128)(2,1)S(1)}, bf16[32,8,1536]{2,1,0:T(8,128)(2,1)S(1)}, u32[]{:S(2)}, u32[]{:S(2)}) %collective-permute-start.10) | collective-permute-done | bytes 786464 | tf_op jit(solution)/shard_map/ppermute | solution.py:99
  362.9 14.0 %collective-permute-done.11 = bf16[16,8,1536]{2,1,0:T(8,128)(2,1)S(1)} collective-permute-done((bf16[16,8,1536]{2,1,0:T(8,128)(2,1)S(1)}, bf16[16,8,1536]{2,1,0:T(8,128)(2,1)S(1)}, u32[]{:S(2)}, u32[]{:S(2)}) %collective-permute-start.11) | collective-permute-done | bytes 393248 | tf_op jit(solution)/shard_map/ppermute | solution.py:99
  377.1 1.8 collective-permute-start.12
  378.8 2.6 collective-permute-done.20
  383.9 1.7 collective-permute-done.12
  385.9 2.5 collective-permute-done.21
  389.7 3.2 collective-permute-done.13
  393.0 5.3 collective-permute-done.22
  399.9 3.1 collective-permute-done.23
  404.1 3.5 collective-permute-done.15
  409.6 4.1 collective-permute-done.3
  414.0 18.9 %collective-permute-done.4 = bf16[5,8,1536]{2,1,0:T(8,128)(2,1)S(1)} collective-permute-done((bf16[5,8,1536]{2,1,0:T(8,128)(2,1)S(1)}, bf16[5,8,1536]{2,1,0:T(8,128)(2,1)S(1)}, u32[]{:S(2)}, u32[]{:S(2)}) %collective-permute-start.4) | collective-permute-done | bytes 122912 | tf_op jit(solution)/shard_map/ppermute | solution.py:99
  433.1 6.3 %collective-permute-done.5 = bf16[5,8,1536]{2,1,0:T(8,128)(2,1)S(1)} collective-permute-done((bf16[5,8,1536]{2,1,0:T(8,128)(2,1)S(1)}, bf16[5,8,1536]{2,1,0:T(8,128)(2,1)S(1)}, u32[]{:S(2)}, u32[]{:S(2)}) %collective-permute-start.5) | collective-permute-done | bytes 122912 | tf_op jit(solution)/shard_map/ppermute | solution.py:99
  439.7 6.6 %collective-permute-done.6 = bf16[10,8,1536]{2,1,0:T(8,128)(2,1)S(1)} collective-permute-done((bf16[10,8,1536]{2,1,0:T(8,128)(2,1)S(1)}, bf16[10,8,1536]{2,1,0:T(8,128)(2,1)S(1)}, u32[]{:S(2)}, u32[]{:S(2)}) %collective-permute-start.6) | collective-permute-done | bytes 245792 | tf_op jit(solution)/shard_map/ppermute | solution.py:99
  447.2 21.4 %collective-permute-done.7 = bf16[20,8,1536]{2,1,0:T(8,128)(2,1)S(1)} collective-permute-done((bf16[20,8,1536]{2,1,0:T(8,128)(2,1)S(1)}, bf16[20,8,1536]{2,1,0:T(8,128)(2,1)S(1)}, u32[]{:S(2)}, u32[]{:S(2)}) %collective-permute-start.7) | collective-permute-done | bytes 491552 | tf_op jit(solution)/shard_map/ppermute | solution.py:99
  469.4 21.1 %collective-permute-done.8 = bf16[40,8,1536]{2,1,0:T(8,128)(2,1)S(1)} collective-permute-done((bf16[40,8,1536]{2,1,0:T(8,128)(2,1)S(1)}, bf16[40,8,1536]{2,1,0:T(8,128)(2,1)S(1)}, u32[]{:S(2)}, u32[]{:S(2)}) %collective-permute-start.8) | collective-permute-done | bytes 983072 | tf_op jit(solution)/shard_map/ppermute | solution.py:99
  490.6 2.8 pad_maximum_fusion.1
  493.4 2.6 copy.56
  496.0 3.7 fusion.21
  502.2 3.6 broadcast_select_fusion
  505.9 2.3 copy-done.2
  510.0 13.4 %fusion = (f32[1536,1536]{1,0:T(8,128)}, f32[1536,1536]{1,0:T(8,128)}) fusion(bf16[208,8,1536]{2,1,0:T(8,128)(2,1)} %copy-done.2, bf16[208,8,1536]{2,1,0:T(8,128)(2,1)} %copy-done.3), kind=kLoop, calls=%fused_computation.6 | loop fusion | flops 4718592 | bytes 28311552 | tf_op jit(solution)/shard_map/convert_element_type | solution.py:260
  (187 shorter events, 44.2 us)
Async XLA Ops:
  7.2 4.4 copy-start
  8.9 8.0 %slice-start = ((s8[4718592]{0:T(1024)(128)(4,1)}), s8[524288]{0:T(1024)(128)(4,1)S(1)}, s32[]{:S(2)}) async-start(s8[4718592]{0:T(1024)(128)(4,1)} %bitcast.132), calls=%async_computation.5 | async-start | bytes 1048576
  11.6 4.7 copy-start.29
  11.6 5.4 %slice-start.1 = ((s8[4718592]{0:T(1024)(128)(4,1)}), s8[4194304]{0:T(1024)(128)(4,1)S(1)}, s32[]{:S(2)}) async-start(s8[4718592]{0:T(1024)(128)(4,1)} %bitcast.132), calls=%async_computation.6 | async-start | bytes 8388608
  16.3 4.8 copy-start.15
  25.5 45.1 %copy-start.27 = (bf16[8,64,64]{2,1,0:T(8,128)(2,1)S(1)}, bf16[8,64,64]{2,1,0:T(8,128)(2,1)}, u32[]{:S(2)}) copy-start(bf16[8,64,64]{2,1,0:T(8,128)(2,1)} %param.13) | copy-start | bytes 196612
  73.9 134.2 %all-to-all-start.1 = ((bf16[32,2,8,1536]{3,2,1,0:T(8,128)(2,1)}), bf16[32,2,8,1536]{3,2,1,0:T(8,128)(2,1)S(1)}, u32[]{:S(2)}, u32[]{:S(2)}) async-start(bf16[32,2,8,1536]{3,2,1,0:T(8,128)(2,1)} %bitcast.8), calls=%async_computation.1 | async-start | bytes 3145728 | tf_op jit(solution)/shard_map/all_to_all | solution.py:217
  77.0 129.0 %all-reduce.2.cloned.1.call-start = ((), (), s32[]{:S(2)}) async-start(), calls=%async_computation.4 | async-start | bytes 131072 | tf_op jit(solution)/shard_map/psum | solution.py:221
  214.5 44.4 %copy-start.28 = (bf16[8,64,64]{2,1,0:T(8,128)(2,1)S(1)}, bf16[8,64,64]{2,1,0:T(8,128)(2,1)}, u32[]{:S(2)}) copy-start(bf16[8,64,64]{2,1,0:T(8,128)(2,1)} %param.13) | copy-start | bytes 196612
  267.8 4.6 copy-start.21
  267.8 41.0 %all-to-all-start.3 = ((bf16[32,2,8,1536]{3,1,2,0:T(2,128)(2,1)}), bf16[32,2,8,1536]{3,1,2,0:T(2,128)(2,1)S(1)}, u32[]{:S(2)}, u32[]{:S(2)}) async-start(bf16[32,2,8,1536]{3,1,2,0:T(2,128)(2,1)} %copy.53), calls=%async_computation.3 | async-start | bytes 3145728 | tf_op jit(solution)/shard_map/all_to_all | solution.py:217
  271.1 5.4 %copy-start.7 = (f32[512,1536]{1,0:T(8,128)S(1)}, f32[512,1536]{1,0:T(8,128)}, u32[]{:S(2)}) copy-start(f32[512,1536]{1,0:T(8,128)} %copy-done.6) | copy-start | bytes 9437188
  276.5 32.4 %copy-start.26 = (bf16[2,256,256]{2,1,0:T(8,128)(2,1)S(1)}, bf16[2,256,256]{2,1,0:T(8,128)(2,1)}, u32[]{:S(2)}) copy-start(bf16[2,256,256]{2,1,0:T(8,128)(2,1)} %param.12) | copy-start | bytes 786436
  309.5 3.8 copy-start.17
  309.5 4.0 copy-start.18
  328.0 5.8 %collective-permute-start.18 = (bf16[64,8,1536]{2,1,0:T(8,128)(2,1)}, bf16[64,8,1536]{2,1,0:T(8,128)(2,1)S(1)}, u32[]{:S(2)}, u32[]{:S(2)}) collective-permute-start(bf16[64,8,1536]{2,1,0:T(8,128)(2,1)} %get-tuple-element.43), channel_id=1, source_target_pairs={{0,1},{1,0},{2,3},{3,2},{4,5},{5,4},{6,7},{7,6},{8,9},{9,8},{10,11... | collective-permute-start | bytes 4718600 | tf_op jit(solution)/shard_map/ppermute | solution.py:99
  328.0 7.9 %collective-permute-start.9 = (bf16[64,8,1536]{2,1,0:T(8,128)(2,1)}, bf16[64,8,1536]{2,1,0:T(8,128)(2,1)}, u32[]{:S(2)}, u32[]{:S(2)}) collective-permute-start(bf16[64,8,1536]{2,1,0:T(8,128)(2,1)} %get-tuple-element.42), channel_id=1, source_target_pairs={{0,1},{1,0},{2,3},{3,2},{4,5},{5,4},{6,7},{7,6},{8,9},{9,8},{10,11... | collective-permute-start | bytes 4718600 | tf_op jit(solution)/shard_map/ppermute | solution.py:99
  329.9 12.0 %collective-permute-start = (bf16[80,8,1536]{2,1,0:T(8,128)(2,1)}, bf16[80,8,1536]{2,1,0:T(8,128)(2,1)S(1)}, u32[]{:S(2)}, u32[]{:S(2)}) collective-permute-start(bf16[80,8,1536]{2,1,0:T(8,128)(2,1)} %slice_bitcast_fusion.2), channel_id=1, source_target_pairs={{0,1},{1,0},{2,3},{3,2},{4,5},{5,4},{6,7},{7,6},{8,9},{9,8},{10,11... | collective-permute-start | bytes 5898248 | tf_op jit(solution)/shard_map/ppermute | solution.py:99
  340.4 19.9 %collective-permute-start.10 = (bf16[32,8,1536]{2,1,0:T(8,128)(2,1)S(1)}, bf16[32,8,1536]{2,1,0:T(8,128)(2,1)S(1)}, u32[]{:S(2)}, u32[]{:S(2)}) collective-permute-start(bf16[32,8,1536]{2,1,0:T(8,128)(2,1)S(1)} %dynamic-slice_convert_fusion.3), channel_id=1, source_target_pairs={{0,4},{1,5},{2,6},{3,7},{4,0},{5,1},{6,2},{7,3},{8,12},{9,13},{10,... | collective-permute-start | bytes 2359304 | tf_op jit(solution)/shard_map/ppermute | solution.py:99
  341.8 20.0 %collective-permute-start.19 = (bf16[32,8,1536]{2,1,0:T(8,128)(2,1)S(1)}, bf16[32,8,1536]{2,1,0:T(8,128)(2,1)S(1)}, u32[]{:S(2)}, u32[]{:S(2)}) collective-permute-start(bf16[32,8,1536]{2,1,0:T(8,128)(2,1)S(1)} %dynamic-slice_convert_fusion.2), channel_id=1, source_target_pairs={{0,8},{1,9},{2,10},{3,11},{4,12},{5,13},{6,14},{7,15},{8,0},{9,1},... | collective-permute-start | bytes 2359304 | tf_op jit(solution)/shard_map/ppermute | solution.py:99
  344.7 38.4 %collective-permute-start.1 = (bf16[40,8,1536]{2,1,0:T(8,128)(2,1)S(1)}, bf16[40,8,1536]{2,1,0:T(8,128)(2,1)S(1)}, u32[]{:S(2)}, u32[]{:S(2)}) collective-permute-start(bf16[40,8,1536]{2,1,0:T(8,128)(2,1)S(1)} %dynamic-slice_convert_fusion.1), channel_id=1, source_target_pairs={{0,2},{1,3},{2,0},{3,1},{4,6},{5,7},{6,4},{7,5},{8,10},{9,11},{10,... | collective-permute-start | bytes 2949128 | tf_op jit(solution)/shard_map/ppermute | solution.py:99
  360.5 16.4 %collective-permute-start.11 = (bf16[16,8,1536]{2,1,0:T(8,128)(2,1)S(1)}, bf16[16,8,1536]{2,1,0:T(8,128)(2,1)S(1)}, u32[]{:S(2)}, u32[]{:S(2)}) collective-permute-start(bf16[16,8,1536]{2,1,0:T(8,128)(2,1)S(1)} %dynamic-slice_convert_fusion.6), channel_id=1, source_target_pairs={{0,2},{1,3},{2,0},{3,1},{4,6},{5,7},{6,4},{7,5},{8,10},{9,11},{10,... | collective-permute-start | bytes 1179656 | tf_op jit(solution)/shard_map/ppermute | solution.py:99
  362.1 19.4 %collective-permute-start.20 = (bf16[16,8,1536]{2,1,0:T(8,128)(2,1)S(1)}, bf16[16,8,1536]{2,1,0:T(8,128)(2,1)S(1)}, u32[]{:S(2)}, u32[]{:S(2)}) collective-permute-start(bf16[16,8,1536]{2,1,0:T(8,128)(2,1)S(1)} %dynamic-slice_convert_fusion.5), channel_id=1, source_target_pairs={{0,16},{1,17},{2,18},{3,19},{4,20},{5,21},{6,22},{7,23},{8,24},{9,... | collective-permute-start | bytes 1179656 | tf_op jit(solution)/shard_map/ppermute | solution.py:99
  377.1 8.5 %collective-permute-start.12 = (bf16[8,8,1536]{2,1,0:T(8,128)(2,1)S(1)}, bf16[8,8,1536]{2,1,0:T(8,128)(2,1)S(1)}, u32[]{:S(2)}, u32[]{:S(2)}) collective-permute-start(bf16[8,8,1536]{2,1,0:T(8,128)(2,1)S(1)} %dynamic-slice_convert_fusion.9), channel_id=1, source_target_pairs={{0,8},{1,9},{2,10},{3,11},{4,12},{5,13},{6,14},{7,15},{8,0},{9,1},... | collective-permute-start | bytes 589832 | tf_op jit(solution)/shard_map/ppermute | solution.py:99
  381.6 6.8 %collective-permute-start.21 = (bf16[8,8,1536]{2,1,0:T(8,128)(2,1)S(1)}, bf16[8,8,1536]{2,1,0:T(8,128)(2,1)S(1)}, u32[]{:S(2)}, u32[]{:S(2)}) collective-permute-start(bf16[8,8,1536]{2,1,0:T(8,128)(2,1)S(1)} %dynamic-slice_convert_fusion.8), channel_id=1, source_target_pairs={{0,2},{1,3},{2,0},{3,1},{4,6},{5,7},{6,4},{7,5},{8,10},{9,11},{10,... | collective-permute-start | bytes 589832 | tf_op jit(solution)/shard_map/ppermute | solution.py:99
  383.4 20.5 %collective-permute-start.2 = (bf16[20,8,1536]{2,1,0:T(8,128)(2,1)S(1)}, bf16[20,8,1536]{2,1,0:T(8,128)(2,1)S(1)}, u32[]{:S(2)}, u32[]{:S(2)}) collective-permute-start(bf16[20,8,1536]{2,1,0:T(8,128)(2,1)S(1)} %dynamic-slice_convert_fusion.4), channel_id=1, source_target_pairs={{0,4},{1,5},{2,6},{3,7},{4,0},{5,1},{6,2},{7,3},{8,12},{9,13},{10,... | collective-permute-start | bytes 1474568 | tf_op jit(solution)/shard_map/ppermute | solution.py:99
  385.6 7.2 %collective-permute-start.13 = (bf16[4,8,1536]{2,1,0:T(8,128)(2,1)S(1)}, bf16[4,8,1536]{2,1,0:T(8,128)(2,1)S(1)}, u32[]{:S(2)}, u32[]{:S(2)}) collective-permute-start(bf16[4,8,1536]{2,1,0:T(8,128)(2,1)S(1)} %dynamic-slice_convert_fusion.12), channel_id=1, source_target_pairs={{0,16},{1,17},{2,18},{3,19},{4,20},{5,21},{6,22},{7,23},{8,24},{9,... | collective-permute-start | bytes 294920 | tf_op jit(solution)/shard_map/ppermute | solution.py:99
  388.5 9.8 %collective-permute-start.22 = (bf16[4,8,1536]{2,1,0:T(8,128)(2,1)S(1)}, bf16[4,8,1536]{2,1,0:T(8,128)(2,1)S(1)}, u32[]{:S(2)}, u32[]{:S(2)}) collective-permute-start(bf16[4,8,1536]{2,1,0:T(8,128)(2,1)S(1)} %dynamic-slice_convert_fusion.11), channel_id=1, source_target_pairs={{0,4},{1,5},{2,6},{3,7},{4,0},{5,1},{6,2},{7,3},{8,12},{9,13},{10,... | collective-permute-start | bytes 294920 | tf_op jit(solution)/shard_map/ppermute | solution.py:99
  392.9 6.9 %collective-permute-start.14 = (bf16[4,8,1536]{2,1,0:T(8,128)(2,1)S(1)}, bf16[4,8,1536]{2,1,0:T(8,128)(2,1)S(1)}, u32[]{:S(2)}, u32[]{:S(2)}) collective-permute-start(bf16[4,8,1536]{2,1,0:T(8,128)(2,1)S(1)} %get-tuple-element.35), channel_id=1, source_target_pairs={{0,16},{1,17},{2,18},{3,19},{4,20},{5,21},{6,22},{7,23},{8,24},{9,... | collective-permute-start | bytes 294920 | tf_op jit(solution)/shard_map/ppermute | solution.py:99
  398.4 4.7 collective-permute-start.23
  399.8 7.8 %collective-permute-start.15 = (bf16[8,8,1536]{2,1,0:T(8,128)(2,1)S(1)}, bf16[8,8,1536]{2,1,0:T(8,128)(2,1)S(1)}, u32[]{:S(2)}, u32[]{:S(2)}) collective-permute-start(bf16[8,8,1536]{2,1,0:T(8,128)(2,1)S(1)} %constant_dynamic-update-slice_fusion.14), channel_id=1, source_target_pairs={{0,8},{1,9},{2,10},{3,11},{4,12},{5,13},{6,14},{7,15},{8,0},{9,1},... | collective-permute-start | bytes 589832 | tf_op jit(solution)/shard_map/ppermute | solution.py:99
  403.1 6.1 %collective-permute-start.24 = (bf16[8,8,1536]{2,1,0:T(8,128)(2,1)S(1)}, bf16[8,8,1536]{2,1,0:T(8,128)(2,1)S(1)}, u32[]{:S(2)}, u32[]{:S(2)}) collective-permute-start(bf16[8,8,1536]{2,1,0:T(8,128)(2,1)S(1)} %constant_dynamic-update-slice_fusion.6), channel_id=1, source_target_pairs={{0,2},{1,3},{2,0},{3,1},{4,6},{5,7},{6,4},{7,5},{8,10},{9,11},{10,... | collective-permute-start | bytes 589832 | tf_op jit(solution)/shard_map/ppermute | solution.py:99
  404.1 9.6 %collective-permute-start.3 = (bf16[10,8,1536]{2,1,0:T(8,128)(2,1)S(1)}, bf16[10,8,1536]{2,1,0:T(8,128)(2,1)S(1)}, u32[]{:S(2)}, u32[]{:S(2)}) collective-permute-start(bf16[10,8,1536]{2,1,0:T(8,128)(2,1)S(1)} %dynamic-slice_convert_fusion.7), channel_id=1, source_target_pairs={{0,8},{1,9},{2,10},{3,11},{4,12},{5,13},{6,14},{7,15},{8,0},{9,1},... | collective-permute-start | bytes 737288 | tf_op jit(solution)/shard_map/ppermute | solution.py:99
  407.7 31.8 %collective-permute-start.16 = (bf16[16,8,1536]{2,1,0:T(8,128)(2,1)S(1)}, bf16[16,8,1536]{2,1,0:T(8,128)(2,1)S(1)}, u32[]{:S(2)}, u32[]{:S(2)}) collective-permute-start(bf16[16,8,1536]{2,1,0:T(8,128)(2,1)S(1)} %constant_dynamic-update-slice_fusion.12), channel_id=1, source_target_pairs={{0,2},{1,3},{2,0},{3,1},{4,6},{5,7},{6,4},{7,5},{8,10},{9,11},{10,... | collective-permute-start | bytes 1179656 | tf_op jit(solution)/shard_map/ppermute | solution.py:99
  409.2 37.5 %collective-permute-start.25 = (bf16[16,8,1536]{2,1,0:T(8,128)(2,1)S(1)}, bf16[16,8,1536]{2,1,0:T(8,128)(2,1)S(1)}, u32[]{:S(2)}, u32[]{:S(2)}) collective-permute-start(bf16[16,8,1536]{2,1,0:T(8,128)(2,1)S(1)} %constant_dynamic-update-slice_fusion.4), channel_id=1, source_target_pairs={{0,16},{1,17},{2,18},{3,19},{4,20},{5,21},{6,22},{7,23},{8,24},{9,... | collective-permute-start | bytes 1179656 | tf_op jit(solution)/shard_map/ppermute | solution.py:99
  413.8 19.1 %collective-permute-start.4 = (bf16[5,8,1536]{2,1,0:T(8,128)(2,1)S(1)}, bf16[5,8,1536]{2,1,0:T(8,128)(2,1)S(1)}, u32[]{:S(2)}, u32[]{:S(2)}) collective-permute-start(bf16[5,8,1536]{2,1,0:T(8,128)(2,1)S(1)} %dynamic-slice_convert_fusion.10), channel_id=1, source_target_pairs={{0,16},{1,17},{2,18},{3,19},{4,20},{5,21},{6,22},{7,23},{8,24},{9,... | collective-permute-start | bytes 368648 | tf_op jit(solution)/shard_map/ppermute | solution.py:99
  432.9 6.5 %collective-permute-start.5 = (bf16[5,8,1536]{2,1,0:T(8,128)(2,1)S(1)}, bf16[5,8,1536]{2,1,0:T(8,128)(2,1)S(1)}, u32[]{:S(2)}, u32[]{:S(2)}) collective-permute-start(bf16[5,8,1536]{2,1,0:T(8,128)(2,1)S(1)} %get-tuple-element.33), channel_id=1, source_target_pairs={{0,16},{1,17},{2,18},{3,19},{4,20},{5,21},{6,22},{7,23},{8,24},{9,... | collective-permute-start | bytes 368648 | tf_op jit(solution)/shard_map/ppermute | solution.py:99
  439.4 7.0 %collective-permute-start.6 = (bf16[10,8,1536]{2,1,0:T(8,128)(2,1)S(1)}, bf16[10,8,1536]{2,1,0:T(8,128)(2,1)S(1)}, u32[]{:S(2)}, u32[]{:S(2)}) collective-permute-start(bf16[10,8,1536]{2,1,0:T(8,128)(2,1)S(1)} %constant_dynamic-update-slice_fusion.22), channel_id=1, source_target_pairs={{0,8},{1,9},{2,10},{3,11},{4,12},{5,13},{6,14},{7,15},{8,0},{9,1},... | collective-permute-start | bytes 737288 | tf_op jit(solution)/shard_map/ppermute | solution.py:99
  439.6 29.5 %collective-permute-start.17 = (bf16[32,8,1536]{2,1,0:T(8,128)(2,1)S(1)}, bf16[32,8,1536]{2,1,0:T(8,128)(2,1)S(1)}, u32[]{:S(2)}, u32[]{:S(2)}) collective-permute-start(bf16[32,8,1536]{2,1,0:T(8,128)(2,1)S(1)} %constant_dynamic-update-slice_fusion.10), channel_id=1, source_target_pairs={{0,4},{1,5},{2,6},{3,7},{4,0},{5,1},{6,2},{7,3},{8,12},{9,13},{10,... | collective-permute-start | bytes 2359304 | tf_op jit(solution)/shard_map/ppermute | solution.py:99
  446.4 22.2 %collective-permute-start.7 = (bf16[20,8,1536]{2,1,0:T(8,128)(2,1)S(1)}, bf16[20,8,1536]{2,1,0:T(8,128)(2,1)S(1)}, u32[]{:S(2)}, u32[]{:S(2)}) collective-permute-start(bf16[20,8,1536]{2,1,0:T(8,128)(2,1)S(1)} %constant_dynamic-update-slice_fusion.20), channel_id=1, source_target_pairs={{0,4},{1,5},{2,6},{3,7},{4,0},{5,1},{6,2},{7,3},{8,12},{9,13},{10,... | collective-permute-start | bytes 1474568 | tf_op jit(solution)/shard_map/ppermute | solution.py:99
  446.7 22.4 %collective-permute-start.26 = (bf16[32,8,1536]{2,1,0:T(8,128)(2,1)S(1)}, bf16[32,8,1536]{2,1,0:T(8,128)(2,1)S(1)}, u32[]{:S(2)}, u32[]{:S(2)}) collective-permute-start(bf16[32,8,1536]{2,1,0:T(8,128)(2,1)S(1)} %constant_dynamic-update-slice_fusion.2), channel_id=1, source_target_pairs={{0,8},{1,9},{2,10},{3,11},{4,12},{5,13},{6,14},{7,15},{8,0},{9,1},... | collective-permute-start | bytes 2359304 | tf_op jit(solution)/shard_map/ppermute | solution.py:99
  468.7 21.8 %collective-permute-start.8 = (bf16[40,8,1536]{2,1,0:T(8,128)(2,1)S(1)}, bf16[40,8,1536]{2,1,0:T(8,128)(2,1)S(1)}, u32[]{:S(2)}, u32[]{:S(2)}) collective-permute-start(bf16[40,8,1536]{2,1,0:T(8,128)(2,1)S(1)} %constant_dynamic-update-slice_fusion.18), channel_id=1, source_target_pairs={{0,2},{1,3},{2,0},{3,1},{4,6},{5,7},{6,4},{7,5},{8,10},{9,11},{10,... | collective-permute-start | bytes 2949128 | tf_op jit(solution)/shard_map/ppermute | solution.py:99
  469.2 21.4 %copy-start.4 = (bf16[64,8,1536]{2,1,0:T(8,128)(2,1)}, bf16[64,8,1536]{2,1,0:T(8,128)(2,1)S(1)}, u32[]{:S(2)}) copy-start(bf16[64,8,1536]{2,1,0:T(8,128)(2,1)S(1)} %constant_dynamic-update-slice_fusion) | copy-start | bytes 4718596
  493.4 8.8 %collective-permute-start.27 = (bf16[208,8,1536]{2,1,0:T(8,128)(2,1)}, bf16[208,8,1536]{2,1,0:T(8,128)(2,1)}, u32[]{:S(2)}, u32[]{:S(2)}) collective-permute-start(bf16[208,8,1536]{2,1,0:T(8,128)(2,1)} %pad_maximum_fusion.1), channel_id=1, source_target_pairs={{0,1},{1,0},{2,3},{3,2},{4,5},{5,4},{6,7},{7,6},{8,9},{9,8},{10,11... | collective-permute-start | bytes 15335432 | tf_op jit(solution)/shard_map/ppermute | solution.py:99
  496.0 3.7 copy-start.12
  496.0 3.7 copy-start.23
  505.8 3.9 copy-start.3
  510.0 15.7 %copy-start.1 = (bf16[1536,512]{1,0:T(8,128)(2,1)S(1)}, bf16[1536,512]{1,0:T(8,128)(2,1)}, u32[]{:S(2)}) copy-start(bf16[1536,512]{1,0:T(8,128)(2,1)} %param.9) | copy-start | bytes 4718596
  (15 other events, 32.7 us)
Sparse Core Ops, SparseCore 0:
  84.0 121.9 all-reduce.1

commit v2 on v0

--- a/solution.py
+++ b/solution.py
@@ -1,3 +1,5 @@
+import functools
+
 import jax
 import jax.numpy as jnp
 from jax import lax
@@ -89,7 +91,202 @@
     return (hidden, d_proj[:chan_rows], d_proj[chan_rows:], d_first, d_second, d_down, d_up)
 
 
+ROWS = 8
+
+
+def swap(value, n, bit):
+    pairs = [(i, i ^ (1 << bit)) for i in range(n)]
+    return lax.ppermute(value, "seq", pairs)
+
+
+def streams_of(n):
+    rest = list(range(1, n.bit_length() - 1))
+    return [rest[s:] + rest[:s] for s in range(min(3, len(rest)))]
+
+
+def reduce_all(part, n, index):
+    rows, cols = part.shape
+    orders = streams_of(n)
+    unit = n // 2
+    blocks = part.reshape(rows // ROWS, ROWS, cols)
+    count = blocks.shape[0] // unit
+    shares = [(count * (s + 1)) // len(orders) - (count * s) // len(orders) for s in range(len(orders))]
+    shares.sort(reverse=True)
+    pieces, low = [], 0
+    for share in shares:
+        pieces.append(blocks[low : low + share * unit])
+        low += share * unit
+    steps = len(orders[0])
+    for step in range(steps):
+        sent, kept = [], []
+        for piece, order in zip(pieces, orders):
+            half = piece.shape[0] // 2
+            mine = (index >> order[step]) & 1
+            sent.append(lax.dynamic_slice_in_dim(piece, (1 - mine) * half, half, 0).astype(jnp.bfloat16))
+            kept.append(lax.dynamic_slice_in_dim(piece, mine * half, half, 0))
+        sent = lax.optimization_barrier(tuple(sent))
+        got = [swap(value, n, order[step]) for value, order in zip(sent, orders)]
+        got = lax.optimization_barrier(tuple(got))
+        pieces = [k + g.astype(jnp.float32) for k, g in zip(kept, got)]
+    pieces = [piece.astype(jnp.bfloat16) for piece in pieces]
+    for step in reversed(range(steps)):
+        pieces = lax.optimization_barrier(tuple(pieces))
+        got = [swap(value, n, order[step]) for value, order in zip(pieces, orders)]
+        got = lax.optimization_barrier(tuple(got))
+        joined = []
+        for piece, other, order in zip(pieces, got, orders):
+            half = piece.shape[0]
+            mine = (index >> order[step]) & 1
+            whole = jnp.zeros((2 * half,) + piece.shape[1:], piece.dtype)
+            whole = lax.dynamic_update_slice_in_dim(whole, piece, mine * half, 0)
+            joined.append(lax.dynamic_update_slice_in_dim(whole, other, (1 - mine) * half, 0))
+        pieces = joined
+    return jnp.concatenate(pieces, axis=0)
+
+
+def seq_body(
+    n,
+    tokens,
+    gate_weight,
+    value_weight,
+    first_factor,
+    second_factor,
+    down_latent,
+    up_latent,
+    doc_lengths,
+    cotangent,
+):
+    highest = lax.Precision.HIGHEST
+    f32, bf16 = jnp.float32, jnp.bfloat16
+    width, count = tokens.shape
+    here, block, _ = first_factor.shape
+    lats = up_latent.shape[1]
+    docs = doc_lengths.shape[0]
+    share = second_factor.shape[0]
+    index = lax.axis_index("seq")
+    core = index & 1
+    pair_tokens = jnp.concatenate([tokens, swap(tokens, n, 0)], axis=1)
+
+    gate_pre = jnp.einsum("ct,oc->to", tokens, gate_weight, preferred_element_type=f32)
+    sig = jax.nn.sigmoid(gate_pre)
+    act = gate_pre * sig
+    upstream = cotangent.T.astype(f32)
+    d_mixed = upstream * act
+    d_mixed_bf = d_mixed.astype(bf16)
+
+    doc_ends = jnp.cumsum(doc_lengths)
+    doc_begins = doc_ends - doc_lengths
+    span = jnp.arange(count, dtype=jnp.int32)
+    position = jnp.concatenate([index * count + span, (index ^ 1) * count + span])
+    pair_member = (
+        (position[None, :] >= doc_begins[:, None]) & (position[None, :] < doc_ends[:, None])
+    ).astype(f32)
+    member = pair_member[:, :count]
+    len_scale = lax.rsqrt(doc_lengths.astype(f32))
+    up_float = up_latent.astype(f32)
+    latent = jnp.einsum("ct,cl->tl", tokens, down_latent, preferred_element_type=f32)
+    doc_part = jnp.dot(member, latent, precision=highest)
+    per_doc = jnp.dot(member, d_mixed, precision=highest)
+    d_pooled_part = jnp.dot(per_doc, up_float, precision=highest)
+    small = jnp.concatenate([doc_part, d_pooled_part], axis=0)
+
+    value_bf = jnp.einsum("ct,oc->to", tokens, value_weight, preferred_element_type=f32).astype(bf16)
+    blocked = value_bf.reshape(here, block, width)
+    inner_mix = jnp.einsum("ikj,ijc->ikc", first_factor, blocked, preferred_element_type=f32).astype(bf16)
+
+    def outward(rows):
+        rows = rows.reshape(here, n, share, width)
+        return jnp.transpose(rows, (1, 0, 2, 3))
+
+    def across(rows):
+        return lax.all_to_all(rows, "seq", split_axis=0, concat_axis=0, tiled=True)
+
+    def half_columns(rows):
+        half = rows.shape[1] // 2
+        own = lax.dynamic_slice_in_dim(rows, core * half, half, 1)
+        sent = lax.dynamic_slice_in_dim(rows, (1 - core) * half, half, 1)
+        return jnp.concatenate([own, swap(sent, n, 0)], axis=0)
+
+    def both_cores(blocks):
+        theirs = swap(blocks, n, 0)
+        place = lax.broadcasted_iota(jnp.int32, (2,) + blocks.shape, 0)
+        return jnp.where(place == core, blocks[None], theirs[None])
+
+    d_outer_out = outward(d_mixed_bf)
+    d_outer_out, small, pair_per_doc, pair_tokens = lax.optimization_barrier(
+        (d_outer_out, small, per_doc + swap(per_doc, n, 0), pair_tokens)
+    )
+    for bit in range(n.bit_length() - 1):
+        small = small + swap(small, n, bit)
+    pooled = small[:docs] * len_scale[:, None]
+    d_pooled = small[docs:] * len_scale[:, None]
+
+    d_outer_k = across(d_outer_out).reshape(n * here, share, width)
+    d_inner_k = jnp.einsum("kmi,mkc->ikc", second_factor, d_outer_k, preferred_element_type=f32).astype(bf16)
+    d_inner_k, inner_out = lax.optimization_barrier((d_inner_k, outward(inner_mix)))
+    d_inner_back = across(d_inner_k.reshape(n, here, share, width))
+    inner_out, d_inner_back = lax.optimization_barrier((inner_out, d_inner_back))
+    inner_k = across(inner_out).reshape(n * here, share, width)
+
+    d_rows = jnp.transpose(d_inner_back, (1, 0, 2, 3)).reshape(here, block, width)
+    d_value_bf = (
+        jnp.einsum("ikj,ikc->ijc", first_factor, d_rows, preferred_element_type=f32)
+        .astype(bf16)
+        .reshape(count, width)
+    )
+    half_lats = lats // 2
+    our_pooled = lax.dynamic_slice_in_dim(pooled, core * half_lats, half_lats, 1)
+    our_d_pooled = lax.dynamic_slice_in_dim(d_pooled, core * half_lats, half_lats, 1)
+    d_up_part = jnp.einsum("dl,dc->lc", our_pooled, pair_per_doc, precision=highest)
+    d_latent_bf = jnp.einsum("dl,dt->lt", our_d_pooled, pair_member, precision=highest).astype(bf16)
+    d_down_part = jnp.einsum("lt,ct->lc", d_latent_bf, pair_tokens, preferred_element_type=f32)
+    value_part = jnp.einsum(
+        "to,it->oi", half_columns(d_value_bf), pair_tokens, preferred_element_type=f32
+    )
+    value_sum = both_cores(
+        reduce_all(jnp.concatenate([value_part, d_up_part, d_down_part], axis=0), n, index)
+    )
+
+    outer_k = jnp.einsum("kmi,ikc->mkc", second_factor, inner_k, preferred_element_type=f32).astype(bf16)
+    outer_back = across(outer_k.reshape(n, here, share, width))
+    d_second = jnp.einsum("mkc,ikc->kmi", d_outer_k, inner_k, preferred_element_type=f32)
+    d_first = jnp.einsum("ikc,ijc->ikj", d_rows, blocked, preferred_element_type=f32)
+
+    spread = jnp.dot(pooled, up_float.T, precision=highest)
+    summary = jnp.einsum("dt,dc->tc", member, spread, precision=highest)
+    mixed = jnp.transpose(outer_back, (1, 0, 2, 3)).reshape(count, width).astype(f32) + summary
+    d_gate_bf = (upstream * mixed * sig * (1.0 + gate_pre * (1.0 - sig))).astype(bf16)
+    hidden = (act * mixed).astype(bf16).T
+    gate_part = jnp.einsum(
+        "to,it->oi", half_columns(d_gate_bf), pair_tokens, preferred_element_type=f32
+    )
+    gate_sum = both_cores(reduce_all(gate_part, n, index))
+
+    blocks_w = width // 2 // ROWS
+    blocks_l = half_lats // ROWS
+
+    def rows_of(blocks, extent):
+        return blocks.astype(f32).reshape(extent, width)
+
+    return (
+        hidden,
+        rows_of(gate_sum, width),
+        rows_of(value_sum[:, :blocks_w], width),
+        d_first,
+        d_second,
+        rows_of(value_sum[:, blocks_w + blocks_l :], lats).T,
+        rows_of(value_sum[:, blocks_w : blocks_w + blocks_l], lats).T,
+    )
+
+
+def fits(n):
+    return n >= 8 and n & (n - 1) == 0
+
+
 def solution(mesh):
+    n = mesh.shape["seq"]
+    local = mesh.shape["chan"] == 1 and fits(n)
+    run = functools.partial(seq_body, n) if local else body
     in_specs = (
         P("chan", "seq"),
         P("chan", None),
@@ -110,4 +307,4 @@
         P("chan", None),
         P("chan", None),
     )
-    return jax.shard_map(body, mesh=mesh, in_specs=in_specs, out_specs=out_specs, check_vma=False)
+    return jax.shard_map(run, mesh=mesh, in_specs=in_specs, out_specs=out_specs, check_vma=False)

time: 679 us -> 426 us (0.63)
  waiting for transfers between devices: 469 us -> 195 us
  blocking collectives: 88.7 us -> 0 us
  starting transfers between devices: 7.36 us -> 89.4 us
  other arithmetic: 2.02 us -> 38.2 us
  between operations: 14.3 us -> 2.49 us
    psum x2 -> x0, waiting for transfers between devices: 437 us -> none  [the longest x1 315 us: body(): d_proj, d_down, d_up = lax.psum((d_proj, d_down_part, d_up_part), 'seq')]
    ppermute x0 -> x59, waiting for transfers between devices: none -> 166 us  [swap(): return lax.ppermute(value, 'seq', pairs)]
    all_to_all x2 -> x0, blocking collectives: 88.7 us -> none  [the longest x1 45.1 us: body(): lax.all_to_all(inner_mix, 'seq', split_axis=0, concat_axis=1, tiled=True)]
    ppermute x0 -> x59, starting transfers between devices: none -> 70.6 us  [swap(): return lax.ppermute(value, 'seq', pairs)]
    add x1 -> x25, other arithmetic: 0.01 us -> 14.7 us  [the longest x18 11.5 us: reduce_all(): pieces = [k + g.astype(jnp.float32) for k, g in zip(kept, got)]]
    all_to_all x5 -> x0, local copies, waits for them, and re-layouts: 13.6 us -> none  [the longest x2 7.01 us: body(): lax.all_to_all(d_send, 'seq', split_axis=0, concat_axis=1, tiled=True)]
    reshape x1 -> x5, local copies, waits for them, and re-layouts: 1.62 us -> 13.4 us  [the longest x2 8.66 us: seq_body(): d_inner_back = across(d_inner_k.reshape(n, here, share, width))]
    all_to_all x2 -> x4, starting transfers between devices: 7.1 us -> 18.8 us  [across(): return lax.all_to_all(rows, 'seq', split_axis=0, concat_axis=0, tiled=True)]
  transfers between devices with their start and end apart: 4 -> 63, of which waited for: 3 -> 35; matrix products, arithmetic and copies ran while one was open for 4% -> 19% of each run, Pallas kernels for 0% -> 0%
where the time goes in v2:
time: 426 us; the launch traced here: 420 us
  waiting for transfers between devices  195 us (46%)
  starting transfers between devices  89.4 us (21%)
  local copies, waits for them, and re-layouts  51.6 us (12%)
  matrix products  42.6 us (10%)
  other arithmetic  38.2 us (9%)
    ppermute x59, waiting for transfers between devices, swap(): return lax.ppermute(value, 'seq', pairs)  166 us
    ppermute x59, starting transfers between devices, swap(): return lax.ppermute(value, 'seq', pairs)  70.6 us
    all_to_all x4, waiting for transfers between devices, across(): return lax.all_to_all(rows, 'seq', split_axis=0, concat_axis=0, tiled=True)  29.7 us
    all_to_all x4, starting transfers between devices, across(): return lax.all_to_all(rows, 'seq', split_axis=0, concat_axis=0, tiled=True)  18.8 us
    add x18, other arithmetic, reduce_all(): pieces = [k + g.astype(jnp.float32) for k, g in zip(kept, got)]  11.5 us
    unnamed x76, local copies, waits for them, and re-layouts  10.2 us
    reshape x2, local copies, waits for them, and re-layouts, seq_body(): d_inner_back = across(d_inner_k.reshape(n, here, share, width))  8.66 us
  transfers between devices with their start and end apart: 63, of which 35 were waited for; matrix products, arithmetic and copies ran while one was open for 19% of the time, Pallas kernels for 0%

profile of v2, /device:TPU:0, one launch (start us, length us, event | category | flops | bytes accessed | tf_op | source)
XLA Modules:
  0.0 419.5 jit_solution(2406463894788463674)
XLA Ops:
  4.7 5.5 %fusion.9 = (bf16[512,1536]{1,0:T(8,128)(2,1)S(1)}, f32[512,1536]{1,0:T(8,128)S(1)}) fusion(bf16[1536,512]{0,1:T(8,128)(2,1)S(1)} %copy.51, bf16[1536,512]{1,0:T(8,128)(2,1)S(1)} %copy-done.2, bf16[1536,1536]{1,0:T(8,128)(2,1)} %param.10), kind=kOutput, calls=%fused_computation.27 | convolution fusion | flops 2421424128 | bytes 12582912 | tf_op jit(solution)/shard_map/ct,oc->to/dot_general | solution.py:170
  18.3 7.6 %all-to-all-start = ((bf16[32,2,8,1536]{3,2,1,0:T(8,128)(2,1)}), bf16[32,2,8,1536]{3,2,1,0:T(8,128)(2,1)}, u32[]{:S(2)}, u32[]{:S(2)}) async-start(bf16[32,2,8,1536]{3,2,1,0:T(8,128)(2,1)} %bitcast.101), calls=%async_computation | async-start | bytes 3145728 | tf_op jit(solution)/shard_map/all_to_all | solution.py:202
  25.9 5.5 %convolution_convert_fusion.4 = bf16[512,1536]{1,0:T(8,128)(2,1)S(1)} fusion(bf16[1536,512]{1,0:T(8,128)(2,1)} %param.9, bf16[1536,1536]{1,0:T(8,128)(2,1)} %param.11), kind=kOutput, calls=%fused_computation.19 | convolution fusion | flops 2416705536 | bytes 7864320 | tf_op jit(solution)/shard_map/ct,oc->to/dot_general | solution.py:193
  33.9 29.7 %all-to-all-done = bf16[32,2,8,1536]{3,2,1,0:T(8,128)(2,1)} async-done(((bf16[32,2,8,1536]{3,2,1,0:T(8,128)(2,1)}), bf16[32,2,8,1536]{3,2,1,0:T(8,128)(2,1)}, u32[]{:S(2)}, u32[]{:S(2)}) %all-to-all-start) | async-done | bytes 1572896 | tf_op jit(solution)/shard_map/all_to_all | solution.py:202
  63.6 3.8 fusion.5
  67.5 4.5 %reshape.105 = bf16[32,2,8,1536]{3,1,0,2:T(2,128)(2,1)} reshape(bf16[64,8,1536]{2,0,1:T(8,128)(2,1)} %fusion.5) | data formatting | bytes 3145728 | tf_op jit(solution)/shard_map/reshape | solution.py:227
  71.9 4.2 copy.57
  76.1 4.1 all-to-all-start.1
  84.6 9.6 %collective-permute-done.3 = f32[128,128]{1,0:T(8,128)S(1)} collective-permute-done((f32[128,128]{1,0:T(8,128)S(1)}, f32[128,128]{1,0:T(8,128)S(1)}, u32[]{:S(2)}, u32[]{:S(2)}) %collective-permute-start.3) | collective-permute-done | bytes 65568 | tf_op jit(solution)/shard_map/ppermute | solution.py:99
  94.8 4.5 %collective-permute-done.4 = f32[128,128]{1,0:T(8,128)S(1)} collective-permute-done((f32[128,128]{1,0:T(8,128)S(1)}, f32[128,128]{1,0:T(8,128)S(1)}, u32[]{:S(2)}, u32[]{:S(2)}) %collective-permute-start.4) | collective-permute-done | bytes 65568 | tf_op jit(solution)/shard_map/ppermute | solution.py:99
  99.4 8.6 %collective-permute-done.5 = f32[128,128]{1,0:T(8,128)S(1)} collective-permute-done((f32[128,128]{1,0:T(8,128)S(1)}, f32[128,128]{1,0:T(8,128)S(1)}, u32[]{:S(2)}, u32[]{:S(2)}) %collective-permute-start.5) | collective-permute-done | bytes 65568 | tf_op jit(solution)/shard_map/ppermute | solution.py:99
  108.6 4.2 collective-permute-start.6
  113.3 7.4 %collective-permute-done.6 = f32[128,128]{1,0:T(8,128)} collective-permute-done((f32[128,128]{1,0:T(8,128)}, f32[128,128]{1,0:T(8,128)}, u32[]{:S(2)}, u32[]{:S(2)}) %collective-permute-start.6) | collective-permute-done | bytes 65568 | tf_op jit(solution)/shard_map/ppermute | solution.py:99
  123.0 2.0 convolution_convert_fusion.2
  127.9 2.7 fusion.16
  137.2 9.5 %collective-permute-done.35 = bf16[16,8,1536]{2,1,0:T(8,128)(2,1)} collective-permute-done((bf16[16,8,1536]{2,1,0:T(8,128)(2,1)}, bf16[16,8,1536]{2,1,0:T(8,128)(2,1)}, u32[]{:S(2)}, u32[]{:S(2)}) %collective-permute-start.35) | collective-permute-done | bytes 393248 | tf_op jit(solution)/shard_map/ppermute | solution.py:99
  157.9 2.2 collective-permute-start.39
  161.7 5.7 %collective-permute-done.38 = bf16[8,8,1536]{2,1,0:T(8,128)(2,1)} collective-permute-done((bf16[8,8,1536]{2,1,0:T(8,128)(2,1)}, bf16[8,8,1536]{2,1,0:T(8,128)(2,1)}, u32[]{:S(2)}, u32[]{:S(2)}) %collective-permute-start.38) | collective-permute-done | bytes 196640 | tf_op jit(solution)/shard_map/ppermute | solution.py:99
  176.7 2.1 collective-permute-start.40
  180.1 3.5 all-to-all-start.2
  190.0 2.5 collective-permute-start.43
  192.5 2.8 fusion.25
  197.0 27.5 %collective-permute-done.43 = bf16[3,8,1536]{2,1,0:T(8,128)(2,1)S(1)} collective-permute-done((bf16[3,8,1536]{2,1,0:T(8,128)(2,1)S(1)}, bf16[3,8,1536]{2,1,0:T(8,128)(2,1)S(1)}, u32[]{:S(2)}, u32[]{:S(2)}) %collective-permute-start.43) | collective-permute-done | bytes 73760 | tf_op jit(solution)/shard_map/ppermute | solution.py:99
  229.8 2.8 collective-permute-done.46
  232.7 2.8 fusion.7
  237.5 3.5 all-to-all-start.3
  241.1 2.7 collective-permute-start.50
  246.9 36.1 %collective-permute-done.50 = bf16[4,8,1536]{2,1,0:T(8,128)(2,1)S(1)} collective-permute-done((bf16[4,8,1536]{2,1,0:T(8,128)(2,1)S(1)}, bf16[4,8,1536]{2,1,0:T(8,128)(2,1)S(1)}, u32[]{:S(2)}, u32[]{:S(2)}) %collective-permute-start.50) | collective-permute-done | bytes 98336 | tf_op jit(solution)/shard_map/ppermute | solution.py:99
  289.3 7.2 %collective-permute-done.53 = bf16[8,8,1536]{2,1,0:T(8,128)(2,1)S(1)} collective-permute-done((bf16[8,8,1536]{2,1,0:T(8,128)(2,1)S(1)}, bf16[8,8,1536]{2,1,0:T(8,128)(2,1)S(1)}, u32[]{:S(2)}, u32[]{:S(2)}) %collective-permute-start.53) | collective-permute-done | bytes 196640 | tf_op jit(solution)/shard_map/ppermute | solution.py:99
  306.2 4.2 fusion.3
  316.2 2.7 fusion.12
  327.2 3.3 collective-permute-done.8
  336.1 3.5 fusion.20
  339.7 2.4 collective-permute-done.12
  342.1 3.7 collective-permute-done.13
  346.1 2.5 collective-permute-start.15
  358.6 2.5 slice.82
  364.7 2.9 collective-permute-done.20
  371.8 3.2 collective-permute-done.23
  375.0 3.0 collective-permute-done.24
  379.7 2.5 collective-permute-start.28
  382.2 2.9 collective-permute-done.26
  385.1 4.4 %collective-permute-done.27 = bf16[8,8,1536]{2,1,0:T(8,128)(2,1)S(1)} collective-permute-done((bf16[8,8,1536]{2,1,0:T(8,128)(2,1)S(1)}, bf16[8,8,1536]{2,1,0:T(8,128)(2,1)S(1)}, u32[]{:S(2)}, u32[]{:S(2)}) %collective-permute-start.27) | collective-permute-done | bytes 196640 | tf_op jit(solution)/shard_map/ppermute | solution.py:99
  392.2 2.1 collective-permute-start.31
  394.4 3.0 collective-permute-done.29
  403.0 7.4 %bitcast_convert_fusion = f32[1536,1536]{1,0:T(8,128)} fusion(bf16[2,96,8,1536]{3,2,1,0:T(8,128)(2,1)} %slice.82), kind=kLoop, calls=%fused_computation.1 | loop fusion | flops 2359296 | bytes 14155776 | tf_op jit(solution)/shard_map/reshape | solution.py:269
  410.4 2.6 copy.64
  413.0 6.1 %fusion = f32[1536,1536]{1,0:T(8,128)} fusion(pred[1536]{0:T(1024)(128)(4,1)S(1)} %iota.23, bf16[96,8,1536]{2,1,0:T(8,128)(2,1)} %collective-permute-done.32, bf16[96,8,1536]{2,1,0:T(8,128)(2,1)S(1)} %pad_maximum_fusion.2), kind=kLoop, calls=%fused_computation.3 | loop fusion | flops 4718592 | bytes 14157312 | tf_op jit(solution)/shard_map/convert_element_type | solution.py:269
  (334 shorter events, 137.2 us)
Async XLA Ops:
  0.6 15.9 %collective-permute-start.1 = (bf16[1536,512]{1,0:T(8,128)(2,1)}, bf16[1536,512]{1,0:T(8,128)(2,1)}, u32[]{:S(2)}, u32[]{:S(2)}) collective-permute-start(bf16[1536,512]{1,0:T(8,128)(2,1)} %param.9), channel_id=1, source_target_pairs={{0,1},{1,0},{2,3},{3,2},{4,5},{5,4},{6,7},{7,6},{8,9},{9,8},{10,11... | collective-permute-start | bytes 4718600 | tf_op jit(solution)/shard_map/ppermute | solution.py:99
  18.3 45.3 %all-to-all-start = ((bf16[32,2,8,1536]{3,2,1,0:T(8,128)(2,1)}), bf16[32,2,8,1536]{3,2,1,0:T(8,128)(2,1)}, u32[]{:S(2)}, u32[]{:S(2)}) async-start(bf16[32,2,8,1536]{3,2,1,0:T(8,128)(2,1)} %bitcast.101), calls=%async_computation | async-start | bytes 3145728 | tf_op jit(solution)/shard_map/all_to_all | solution.py:202
  76.1 46.9 %all-to-all-start.1 = ((bf16[32,2,8,1536]{3,1,2,0:T(2,128)(2,1)}), bf16[32,2,8,1536]{3,1,2,0:T(2,128)(2,1)}, u32[]{:S(2)}, u32[]{:S(2)}) async-start(bf16[32,2,8,1536]{3,1,2,0:T(2,128)(2,1)} %copy.57), calls=%async_computation.1 | async-start | bytes 3145728 | tf_op jit(solution)/shard_map/all_to_all | solution.py:202
  82.6 11.5 %collective-permute-start.3 = (f32[128,128]{1,0:T(8,128)S(1)}, f32[128,128]{1,0:T(8,128)S(1)}, u32[]{:S(2)}, u32[]{:S(2)}) collective-permute-start(f32[128,128]{1,0:T(8,128)S(1)} %add.289), channel_id=1, source_target_pairs={{0,2},{1,3},{2,0},{3,1},{4,6},{5,7},{6,4},{7,5},{8,10},{9,11},{10,... | collective-permute-start | bytes 196616 | tf_op jit(solution)/shard_map/ppermute | solution.py:99
  99.3 8.7 %collective-permute-start.5 = (f32[128,128]{1,0:T(8,128)S(1)}, f32[128,128]{1,0:T(8,128)S(1)}, u32[]{:S(2)}, u32[]{:S(2)}) collective-permute-start(f32[128,128]{1,0:T(8,128)S(1)} %add.291), channel_id=1, source_target_pairs={{0,8},{1,9},{2,10},{3,11},{4,12},{5,13},{6,14},{7,15},{8,0},{9,1},... | collective-permute-start | bytes 196616 | tf_op jit(solution)/shard_map/ppermute | solution.py:99
  108.6 12.1 %collective-permute-start.6 = (f32[128,128]{1,0:T(8,128)}, f32[128,128]{1,0:T(8,128)}, u32[]{:S(2)}, u32[]{:S(2)}) collective-permute-start(f32[128,128]{1,0:T(8,128)} %add.292), channel_id=1, source_target_pairs={{0,16},{1,17},{2,18},{3,19},{4,20},{5,21},{6,22},{7,23},{8,24},{9,... | collective-permute-start | bytes 196616 | tf_op jit(solution)/shard_map/ppermute | solution.py:99
  134.4 15.5 %collective-permute-start.34 = (bf16[24,8,1536]{2,1,0:T(8,128)(2,1)}, bf16[24,8,1536]{2,1,0:T(8,128)(2,1)}, u32[]{:S(2)}, u32[]{:S(2)}) collective-permute-start(bf16[24,8,1536]{2,1,0:T(8,128)(2,1)} %dynamic-slice_convert_fusion), channel_id=1, source_target_pairs={{0,2},{1,3},{2,0},{3,1},{4,6},{5,7},{6,4},{7,5},{8,10},{9,11},{10,... | collective-permute-start | bytes 1769480 | tf_op jit(solution)/shard_map/ppermute | solution.py:99
  135.7 11.0 %collective-permute-start.35 = (bf16[16,8,1536]{2,1,0:T(8,128)(2,1)}, bf16[16,8,1536]{2,1,0:T(8,128)(2,1)}, u32[]{:S(2)}, u32[]{:S(2)}) collective-permute-start(bf16[16,8,1536]{2,1,0:T(8,128)(2,1)} %dynamic-slice_convert_fusion.2), channel_id=1, source_target_pairs={{0,4},{1,5},{2,6},{3,7},{4,0},{5,1},{6,2},{7,3},{8,12},{9,13},{10,... | collective-permute-start | bytes 1179656 | tf_op jit(solution)/shard_map/ppermute | solution.py:99
  137.2 10.8 %collective-permute-start.36 = (bf16[16,8,1536]{2,1,0:T(8,128)(2,1)}, bf16[16,8,1536]{2,1,0:T(8,128)(2,1)}, u32[]{:S(2)}, u32[]{:S(2)}) collective-permute-start(bf16[16,8,1536]{2,1,0:T(8,128)(2,1)} %dynamic-slice_convert_fusion.1), channel_id=1, source_target_pairs={{0,8},{1,9},{2,10},{3,11},{4,12},{5,13},{6,14},{7,15},{8,0},{9,1},... | collective-permute-start | bytes 1179656 | tf_op jit(solution)/shard_map/ppermute | solution.py:99
  156.6 12.4 %collective-permute-start.37 = (bf16[12,8,1536]{2,1,0:T(8,128)(2,1)}, bf16[12,8,1536]{2,1,0:T(8,128)(2,1)}, u32[]{:S(2)}, u32[]{:S(2)}) collective-permute-start(bf16[12,8,1536]{2,1,0:T(8,128)(2,1)} %dynamic-slice_convert_fusion.6), channel_id=1, source_target_pairs={{0,4},{1,5},{2,6},{3,7},{4,0},{5,1},{6,2},{7,3},{8,12},{9,13},{10,... | collective-permute-start | bytes 884744 | tf_op jit(solution)/shard_map/ppermute | solution.py:99
  157.9 9.4 %collective-permute-start.38 = (bf16[8,8,1536]{2,1,0:T(8,128)(2,1)}, bf16[8,8,1536]{2,1,0:T(8,128)(2,1)}, u32[]{:S(2)}, u32[]{:S(2)}) collective-permute-start(bf16[8,8,1536]{2,1,0:T(8,128)(2,1)} %dynamic-slice_convert_fusion.8), channel_id=1, source_target_pairs={{0,8},{1,9},{2,10},{3,11},{4,12},{5,13},{6,14},{7,15},{8,0},{9,1},... | collective-permute-start | bytes 589832 | tf_op jit(solution)/shard_map/ppermute | solution.py:99
  157.9 11.1 %collective-permute-start.39 = (bf16[8,8,1536]{2,1,0:T(8,128)(2,1)}, bf16[8,8,1536]{2,1,0:T(8,128)(2,1)}, u32[]{:S(2)}, u32[]{:S(2)}) collective-permute-start(bf16[8,8,1536]{2,1,0:T(8,128)(2,1)} %dynamic-slice_convert_fusion.7), channel_id=1, source_target_pairs={{0,16},{1,17},{2,18},{3,19},{4,20},{5,21},{6,22},{7,23},{8,24},{9,... | collective-permute-start | bytes 589832 | tf_op jit(solution)/shard_map/ppermute | solution.py:99
  174.8 8.9 %collective-permute-start.41 = (bf16[4,8,1536]{2,1,0:T(8,128)(2,1)}, bf16[4,8,1536]{2,1,0:T(8,128)(2,1)}, u32[]{:S(2)}, u32[]{:S(2)}) collective-permute-start(bf16[4,8,1536]{2,1,0:T(8,128)(2,1)} %dynamic-slice_convert_fusion.14), channel_id=1, source_target_pairs={{0,16},{1,17},{2,18},{3,19},{4,20},{5,21},{6,22},{7,23},{8,24},{9,... | collective-permute-start | bytes 294920 | tf_op jit(solution)/shard_map/ppermute | solution.py:99
  175.1 8.5 %collective-permute-start.42 = (bf16[4,8,1536]{2,1,0:T(8,128)(2,1)}, bf16[4,8,1536]{2,1,0:T(8,128)(2,1)}, u32[]{:S(2)}, u32[]{:S(2)}) collective-permute-start(bf16[4,8,1536]{2,1,0:T(8,128)(2,1)} %dynamic-slice_convert_fusion.13), channel_id=1, source_target_pairs={{0,2},{1,3},{2,0},{3,1},{4,6},{5,7},{6,4},{7,5},{8,10},{9,11},{10,... | collective-permute-start | bytes 294920 | tf_op jit(solution)/shard_map/ppermute | solution.py:99
  176.7 7.0 %collective-permute-start.40 = (bf16[6,8,1536]{2,1,0:T(8,128)(2,1)}, bf16[6,8,1536]{2,1,0:T(8,128)(2,1)}, u32[]{:S(2)}, u32[]{:S(2)}) collective-permute-start(bf16[6,8,1536]{2,1,0:T(8,128)(2,1)} %dynamic-slice_convert_fusion.12), channel_id=1, source_target_pairs={{0,8},{1,9},{2,10},{3,11},{4,12},{5,13},{6,14},{7,15},{8,0},{9,1},... | collective-permute-start | bytes 442376 | tf_op jit(solution)/shard_map/ppermute | solution.py:99
  180.1 52.6 %all-to-all-start.2 = ((bf16[32,2,8,1536]{3,2,1,0:T(8,128)(2,1)}), bf16[32,2,8,1536]{3,2,1,0:T(8,128)(2,1)}, u32[]{:S(2)}, u32[]{:S(2)}) async-start(bf16[32,2,8,1536]{3,2,1,0:T(8,128)(2,1)} %bitcast.99), calls=%async_computation.2 | async-start | bytes 3145728 | tf_op jit(solution)/shard_map/all_to_all | solution.py:202
  186.8 10.1 %collective-permute-start.44 = (bf16[2,8,1536]{2,1,0:T(8,128)(2,1)S(1)}, bf16[2,8,1536]{2,1,0:T(8,128)(2,1)S(1)}, u32[]{:S(2)}, u32[]{:S(2)}) collective-permute-start(bf16[2,8,1536]{2,1,0:T(8,128)(2,1)S(1)} %dynamic-slice_convert_fusion.20), channel_id=1, source_target_pairs={{0,2},{1,3},{2,0},{3,1},{4,6},{5,7},{6,4},{7,5},{8,10},{9,11},{10,... | collective-permute-start | bytes 147464 | tf_op jit(solution)/shard_map/ppermute | solution.py:99
  188.5 8.5 %collective-permute-start.45 = (bf16[2,8,1536]{2,1,0:T(8,128)(2,1)S(1)}, bf16[2,8,1536]{2,1,0:T(8,128)(2,1)S(1)}, u32[]{:S(2)}, u32[]{:S(2)}) collective-permute-start(bf16[2,8,1536]{2,1,0:T(8,128)(2,1)S(1)} %dynamic-slice_convert_fusion.19), channel_id=1, source_target_pairs={{0,4},{1,5},{2,6},{3,7},{4,0},{5,1},{6,2},{7,3},{8,12},{9,13},{10,... | collective-permute-start | bytes 147464 | tf_op jit(solution)/shard_map/ppermute | solution.py:99
  190.0 34.5 %collective-permute-start.43 = (bf16[3,8,1536]{2,1,0:T(8,128)(2,1)S(1)}, bf16[3,8,1536]{2,1,0:T(8,128)(2,1)S(1)}, u32[]{:S(2)}, u32[]{:S(2)}) collective-permute-start(bf16[3,8,1536]{2,1,0:T(8,128)(2,1)S(1)} %dynamic-slice_convert_fusion.18), channel_id=1, source_target_pairs={{0,16},{1,17},{2,18},{3,19},{4,20},{5,21},{6,22},{7,23},{8,24},{9,... | collective-permute-start | bytes 221192 | tf_op jit(solution)/shard_map/ppermute | solution.py:99
  237.5 64.4 %all-to-all-start.3 = ((bf16[32,2,8,1536]{3,2,1,0:T(8,128)(2,1)}), bf16[32,2,8,1536]{3,2,1,0:T(8,128)(2,1)}, u32[]{:S(2)}, u32[]{:S(2)}) async-start(bf16[32,2,8,1536]{3,2,1,0:T(8,128)(2,1)} %bitcast.100), calls=%async_computation.3 | async-start | bytes 3145728 | tf_op jit(solution)/shard_map/all_to_all | solution.py:202
  241.1 41.9 %collective-permute-start.50 = (bf16[4,8,1536]{2,1,0:T(8,128)(2,1)S(1)}, bf16[4,8,1536]{2,1,0:T(8,128)(2,1)S(1)}, u32[]{:S(2)}, u32[]{:S(2)}) collective-permute-start(bf16[4,8,1536]{2,1,0:T(8,128)(2,1)S(1)} %constant_dynamic-update-slice_fusion.20), channel_id=1, source_target_pairs={{0,16},{1,17},{2,18},{3,19},{4,20},{5,21},{6,22},{7,23},{8,24},{9,... | collective-permute-start | bytes 294920 | tf_op jit(solution)/shard_map/ppermute | solution.py:99
  243.7 39.3 %collective-permute-start.51 = (bf16[4,8,1536]{2,1,0:T(8,128)(2,1)S(1)}, bf16[4,8,1536]{2,1,0:T(8,128)(2,1)S(1)}, u32[]{:S(2)}, u32[]{:S(2)}) collective-permute-start(bf16[4,8,1536]{2,1,0:T(8,128)(2,1)S(1)} %constant_dynamic-update-slice_fusion.18), channel_id=1, source_target_pairs={{0,2},{1,3},{2,0},{3,1},{4,6},{5,7},{6,4},{7,5},{8,10},{9,11},{10,... | collective-permute-start | bytes 294920 | tf_op jit(solution)/shard_map/ppermute | solution.py:99
  245.2 37.8 %collective-permute-start.49 = (bf16[6,8,1536]{2,1,0:T(8,128)(2,1)S(1)}, bf16[6,8,1536]{2,1,0:T(8,128)(2,1)S(1)}, u32[]{:S(2)}, u32[]{:S(2)}) collective-permute-start(bf16[6,8,1536]{2,1,0:T(8,128)(2,1)S(1)} %constant_dynamic-update-slice_fusion.22), channel_id=1, source_target_pairs={{0,8},{1,9},{2,10},{3,11},{4,12},{5,13},{6,14},{7,15},{8,0},{9,1},... | collective-permute-start | bytes 442376 | tf_op jit(solution)/shard_map/ppermute | solution.py:99
  283.1 13.5 %collective-permute-start.54 = (bf16[8,8,1536]{2,1,0:T(8,128)(2,1)S(1)}, bf16[8,8,1536]{2,1,0:T(8,128)(2,1)S(1)}, u32[]{:S(2)}, u32[]{:S(2)}) collective-permute-start(bf16[8,8,1536]{2,1,0:T(8,128)(2,1)S(1)} %constant_dynamic-update-slice_fusion.12), channel_id=1, source_target_pairs={{0,16},{1,17},{2,18},{3,19},{4,20},{5,21},{6,22},{7,23},{8,24},{9,... | collective-permute-start | bytes 589832 | tf_op jit(solution)/shard_map/ppermute | solution.py:99
  283.1 13.4 %collective-permute-start.52 = (bf16[12,8,1536]{2,1,0:T(8,128)(2,1)S(1)}, bf16[12,8,1536]{2,1,0:T(8,128)(2,1)S(1)}, u32[]{:S(2)}, u32[]{:S(2)}) collective-permute-start(bf16[12,8,1536]{2,1,0:T(8,128)(2,1)S(1)} %constant_dynamic-update-slice_fusion.16), channel_id=1, source_target_pairs={{0,4},{1,5},{2,6},{3,7},{4,0},{5,1},{6,2},{7,3},{8,12},{9,13},{10,... | collective-permute-start | bytes 884744 | tf_op jit(solution)/shard_map/ppermute | solution.py:99
  286.0 10.5 %collective-permute-start.53 = (bf16[8,8,1536]{2,1,0:T(8,128)(2,1)S(1)}, bf16[8,8,1536]{2,1,0:T(8,128)(2,1)S(1)}, u32[]{:S(2)}, u32[]{:S(2)}) collective-permute-start(bf16[8,8,1536]{2,1,0:T(8,128)(2,1)S(1)} %constant_dynamic-update-slice_fusion.14), channel_id=1, source_target_pairs={{0,8},{1,9},{2,10},{3,11},{4,12},{5,13},{6,14},{7,15},{8,0},{9,1},... | collective-permute-start | bytes 589832 | tf_op jit(solution)/shard_map/ppermute | solution.py:99
  298.0 14.9 %collective-permute-start.56 = (bf16[16,8,1536]{2,1,0:T(8,128)(2,1)}, bf16[16,8,1536]{2,1,0:T(8,128)(2,1)}, u32[]{:S(2)}, u32[]{:S(2)}) collective-permute-start(bf16[16,8,1536]{2,1,0:T(8,128)(2,1)} %constant_dynamic-update-slice_fusion.8), channel_id=1, source_target_pairs={{0,4},{1,5},{2,6},{3,7},{4,0},{5,1},{6,2},{7,3},{8,12},{9,13},{10,... | collective-permute-start | bytes 1179656 | tf_op jit(solution)/shard_map/ppermute | solution.py:99
  298.8 14.1 %collective-permute-start.57 = (bf16[16,8,1536]{2,1,0:T(8,128)(2,1)S(1)}, bf16[16,8,1536]{2,1,0:T(8,128)(2,1)}, u32[]{:S(2)}, u32[]{:S(2)}) collective-permute-start(bf16[16,8,1536]{2,1,0:T(8,128)(2,1)S(1)} %constant_dynamic-update-slice_fusion.6), channel_id=1, source_target_pairs={{0,8},{1,9},{2,10},{3,11},{4,12},{5,13},{6,14},{7,15},{8,0},{9,1},... | collective-permute-start | bytes 1179656 | tf_op jit(solution)/shard_map/ppermute | solution.py:99
  298.8 14.5 %collective-permute-start.55 = (bf16[24,8,1536]{2,1,0:T(8,128)(2,1)}, bf16[24,8,1536]{2,1,0:T(8,128)(2,1)}, u32[]{:S(2)}, u32[]{:S(2)}) collective-permute-start(bf16[24,8,1536]{2,1,0:T(8,128)(2,1)} %constant_dynamic-update-slice_fusion.10), channel_id=1, source_target_pairs={{0,2},{1,3},{2,0},{3,1},{4,6},{5,7},{6,4},{7,5},{8,10},{9,11},{10,... | collective-permute-start | bytes 1769480 | tf_op jit(solution)/shard_map/ppermute | solution.py:99
  319.3 11.2 %collective-permute-start.8 = (bf16[16,8,1536]{2,1,0:T(8,128)(2,1)S(1)}, bf16[16,8,1536]{2,1,0:T(8,128)(2,1)S(1)}, u32[]{:S(2)}, u32[]{:S(2)}) collective-permute-start(bf16[16,8,1536]{2,1,0:T(8,128)(2,1)S(1)} %dynamic-slice_convert_fusion.5), channel_id=1, source_target_pairs={{0,2},{1,3},{2,0},{3,1},{4,6},{5,7},{6,4},{7,5},{8,10},{9,11},{10,... | collective-permute-start | bytes 1179656 | tf_op jit(solution)/shard_map/ppermute | solution.py:99
  321.2 9.8 %collective-permute-start.9 = (bf16[16,8,1536]{2,1,0:T(8,128)(2,1)S(1)}, bf16[16,8,1536]{2,1,0:T(8,128)(2,1)S(1)}, u32[]{:S(2)}, u32[]{:S(2)}) collective-permute-start(bf16[16,8,1536]{2,1,0:T(8,128)(2,1)S(1)} %dynamic-slice_convert_fusion.4), channel_id=1, source_target_pairs={{0,4},{1,5},{2,6},{3,7},{4,0},{5,1},{6,2},{7,3},{8,12},{9,13},{10,... | collective-permute-start | bytes 1179656 | tf_op jit(solution)/shard_map/ppermute | solution.py:99
  322.9 9.5 %collective-permute-start.10 = (bf16[16,8,1536]{2,1,0:T(8,128)(2,1)S(1)}, bf16[16,8,1536]{2,1,0:T(8,128)(2,1)S(1)}, u32[]{:S(2)}, u32[]{:S(2)}) collective-permute-start(bf16[16,8,1536]{2,1,0:T(8,128)(2,1)S(1)} %dynamic-slice_convert_fusion.3), channel_id=1, source_target_pairs={{0,8},{1,9},{2,10},{3,11},{4,12},{5,13},{6,14},{7,15},{8,0},{9,1},... | collective-permute-start | bytes 1179656 | tf_op jit(solution)/shard_map/ppermute | solution.py:99
  327.1 23.0 %collective-permute-start.58 = (bf16[112,8,1536]{2,1,0:T(8,128)(2,1)S(1)}, bf16[112,8,1536]{2,1,0:T(8,128)(2,1)S(1)}, u32[]{:S(2)}, u32[]{:S(2)}) collective-permute-start(bf16[112,8,1536]{2,1,0:T(8,128)(2,1)S(1)} %pad_maximum_fusion.1), channel_id=1, source_target_pairs={{0,1},{1,0},{2,3},{3,2},{4,5},{5,4},{6,7},{7,6},{8,9},{9,8},{10,11... | collective-permute-start | bytes 8257544 | tf_op jit(solution)/shard_map/ppermute | solution.py:99
  332.7 6.9 %collective-permute-start.11 = (bf16[8,8,1536]{2,1,0:T(8,128)(2,1)S(1)}, bf16[8,8,1536]{2,1,0:T(8,128)(2,1)S(1)}, u32[]{:S(2)}, u32[]{:S(2)}) collective-permute-start(bf16[8,8,1536]{2,1,0:T(8,128)(2,1)S(1)} %dynamic-slice_convert_fusion.11), channel_id=1, source_target_pairs={{0,4},{1,5},{2,6},{3,7},{4,0},{5,1},{6,2},{7,3},{8,12},{9,13},{10,... | collective-permute-start | bytes 589832 | tf_op jit(solution)/shard_map/ppermute | solution.py:99
  333.4 8.7 %collective-permute-start.12 = (bf16[8,8,1536]{2,1,0:T(8,128)(2,1)S(1)}, bf16[8,8,1536]{2,1,0:T(8,128)(2,1)S(1)}, u32[]{:S(2)}, u32[]{:S(2)}) collective-permute-start(bf16[8,8,1536]{2,1,0:T(8,128)(2,1)S(1)} %dynamic-slice_convert_fusion.10), channel_id=1, source_target_pairs={{0,8},{1,9},{2,10},{3,11},{4,12},{5,13},{6,14},{7,15},{8,0},{9,1},... | collective-permute-start | bytes 589832 | tf_op jit(solution)/shard_map/ppermute | solution.py:99
  335.1 10.7 %collective-permute-start.13 = (bf16[8,8,1536]{2,1,0:T(8,128)(2,1)S(1)}, bf16[8,8,1536]{2,1,0:T(8,128)(2,1)S(1)}, u32[]{:S(2)}, u32[]{:S(2)}) collective-permute-start(bf16[8,8,1536]{2,1,0:T(8,128)(2,1)S(1)} %dynamic-slice_convert_fusion.9), channel_id=1, source_target_pairs={{0,16},{1,17},{2,18},{3,19},{4,20},{5,21},{6,22},{7,23},{8,24},{9,... | collective-permute-start | bytes 589832 | tf_op jit(solution)/shard_map/ppermute | solution.py:99
  353.8 7.3 %collective-permute-start.17 = (bf16[2,8,1536]{2,1,0:T(8,128)(2,1)S(1)}, bf16[2,8,1536]{2,1,0:T(8,128)(2,1)S(1)}, u32[]{:S(2)}, u32[]{:S(2)}) collective-permute-start(bf16[2,8,1536]{2,1,0:T(8,128)(2,1)S(1)} %dynamic-slice_convert_fusion.23), channel_id=1, source_target_pairs={{0,16},{1,17},{2,18},{3,19},{4,20},{5,21},{6,22},{7,23},{8,24},{9,... | collective-permute-start | bytes 147464 | tf_op jit(solution)/shard_map/ppermute | solution.py:99
  361.1 6.4 %collective-permute-start.20 = (bf16[2,8,1536]{2,1,0:T(8,128)(2,1)S(1)}, bf16[2,8,1536]{2,1,0:T(8,128)(2,1)S(1)}, u32[]{:S(2)}, u32[]{:S(2)}) collective-permute-start(bf16[2,8,1536]{2,1,0:T(8,128)(2,1)S(1)} %add_convert_fusion.5), channel_id=1, source_target_pairs={{0,16},{1,17},{2,18},{3,19},{4,20},{5,21},{6,22},{7,23},{8,24},{9,... | collective-permute-start | bytes 147464 | tf_op jit(solution)/shard_map/ppermute | solution.py:99
  367.7 7.4 %collective-permute-start.23 = (bf16[4,8,1536]{2,1,0:T(8,128)(2,1)S(1)}, bf16[4,8,1536]{2,1,0:T(8,128)(2,1)S(1)}, u32[]{:S(2)}, u32[]{:S(2)}) collective-permute-start(bf16[4,8,1536]{2,1,0:T(8,128)(2,1)S(1)} %constant_dynamic-update-slice_fusion.46), channel_id=1, source_target_pairs={{0,8},{1,9},{2,10},{3,11},{4,12},{5,13},{6,14},{7,15},{8,0},{9,1},... | collective-permute-start | bytes 294920 | tf_op jit(solution)/shard_map/ppermute | solution.py:99
  368.3 9.8 %collective-permute-start.24 = (bf16[4,8,1536]{2,1,0:T(8,128)(2,1)S(1)}, bf16[4,8,1536]{2,1,0:T(8,128)(2,1)S(1)}, u32[]{:S(2)}, u32[]{:S(2)}) collective-permute-start(bf16[4,8,1536]{2,1,0:T(8,128)(2,1)S(1)} %constant_dynamic-update-slice_fusion.44), channel_id=1, source_target_pairs={{0,16},{1,17},{2,18},{3,19},{4,20},{5,21},{6,22},{7,23},{8,24},{9,... | collective-permute-start | bytes 294920 | tf_op jit(solution)/shard_map/ppermute | solution.py:99
  370.3 7.7 %collective-permute-start.25 = (bf16[4,8,1536]{2,1,0:T(8,128)(2,1)S(1)}, bf16[4,8,1536]{2,1,0:T(8,128)(2,1)S(1)}, u32[]{:S(2)}, u32[]{:S(2)}) collective-permute-start(bf16[4,8,1536]{2,1,0:T(8,128)(2,1)S(1)} %constant_dynamic-update-slice_fusion.42), channel_id=1, source_target_pairs={{0,2},{1,3},{2,0},{3,1},{4,6},{5,7},{6,4},{7,5},{8,10},{9,11},{10,... | collective-permute-start | bytes 294920 | tf_op jit(solution)/shard_map/ppermute | solution.py:99
  378.1 7.0 %collective-permute-start.26 = (bf16[8,8,1536]{2,1,0:T(8,128)(2,1)S(1)}, bf16[8,8,1536]{2,1,0:T(8,128)(2,1)S(1)}, u32[]{:S(2)}, u32[]{:S(2)}) collective-permute-start(bf16[8,8,1536]{2,1,0:T(8,128)(2,1)S(1)} %constant_dynamic-update-slice_fusion.40), channel_id=1, source_target_pairs={{0,4},{1,5},{2,6},{3,7},{4,0},{5,1},{6,2},{7,3},{8,12},{9,13},{10,... | collective-permute-start | bytes 589832 | tf_op jit(solution)/shard_map/ppermute | solution.py:99
  379.5 9.9 %collective-permute-start.27 = (bf16[8,8,1536]{2,1,0:T(8,128)(2,1)S(1)}, bf16[8,8,1536]{2,1,0:T(8,128)(2,1)S(1)}, u32[]{:S(2)}, u32[]{:S(2)}) collective-permute-start(bf16[8,8,1536]{2,1,0:T(8,128)(2,1)S(1)} %constant_dynamic-update-slice_fusion.38), channel_id=1, source_target_pairs={{0,8},{1,9},{2,10},{3,11},{4,12},{5,13},{6,14},{7,15},{8,0},{9,1},... | collective-permute-start | bytes 589832 | tf_op jit(solution)/shard_map/ppermute | solution.py:99
  379.7 9.8 %collective-permute-start.28 = (bf16[8,8,1536]{2,1,0:T(8,128)(2,1)S(1)}, bf16[8,8,1536]{2,1,0:T(8,128)(2,1)S(1)}, u32[]{:S(2)}, u32[]{:S(2)}) collective-permute-start(bf16[8,8,1536]{2,1,0:T(8,128)(2,1)S(1)} %constant_dynamic-update-slice_fusion.36), channel_id=1, source_target_pairs={{0,16},{1,17},{2,18},{3,19},{4,20},{5,21},{6,22},{7,23},{8,24},{9,... | collective-permute-start | bytes 589832 | tf_op jit(solution)/shard_map/ppermute | solution.py:99
  389.6 7.8 %collective-permute-start.29 = (bf16[16,8,1536]{2,1,0:T(8,128)(2,1)S(1)}, bf16[16,8,1536]{2,1,0:T(8,128)(2,1)S(1)}, u32[]{:S(2)}, u32[]{:S(2)}) collective-permute-start(bf16[16,8,1536]{2,1,0:T(8,128)(2,1)S(1)} %constant_dynamic-update-slice_fusion.34), channel_id=1, source_target_pairs={{0,2},{1,3},{2,0},{3,1},{4,6},{5,7},{6,4},{7,5},{8,10},{9,11},{10,... | collective-permute-start | bytes 1179656 | tf_op jit(solution)/shard_map/ppermute | solution.py:99
  391.0 7.8 %collective-permute-start.30 = (bf16[16,8,1536]{2,1,0:T(8,128)(2,1)S(1)}, bf16[16,8,1536]{2,1,0:T(8,128)(2,1)S(1)}, u32[]{:S(2)}, u32[]{:S(2)}) collective-permute-start(bf16[16,8,1536]{2,1,0:T(8,128)(2,1)S(1)} %constant_dynamic-update-slice_fusion.32), channel_id=1, source_target_pairs={{0,4},{1,5},{2,6},{3,7},{4,0},{5,1},{6,2},{7,3},{8,12},{9,13},{10,... | collective-permute-start | bytes 1179656 | tf_op jit(solution)/shard_map/ppermute | solution.py:99
  392.2 7.8 %collective-permute-start.31 = (bf16[16,8,1536]{2,1,0:T(8,128)(2,1)S(1)}, bf16[16,8,1536]{2,1,0:T(8,128)(2,1)S(1)}, u32[]{:S(2)}, u32[]{:S(2)}) collective-permute-start(bf16[16,8,1536]{2,1,0:T(8,128)(2,1)S(1)} %constant_dynamic-update-slice_fusion.30), channel_id=1, source_target_pairs={{0,8},{1,9},{2,10},{3,11},{4,12},{5,13},{6,14},{7,15},{8,0},{9,1},... | collective-permute-start | bytes 1179656 | tf_op jit(solution)/shard_map/ppermute | solution.py:99
  400.4 12.6 %collective-permute-start.32 = (bf16[96,8,1536]{2,1,0:T(8,128)(2,1)S(1)}, bf16[96,8,1536]{2,1,0:T(8,128)(2,1)}, u32[]{:S(2)}, u32[]{:S(2)}) collective-permute-start(bf16[96,8,1536]{2,1,0:T(8,128)(2,1)S(1)} %pad_maximum_fusion.2), channel_id=1, source_target_pairs={{0,1},{1,0},{2,3},{3,2},{4,5},{5,4},{6,7},{7,6},{8,9},{9,8},{10,11... | collective-permute-start | bytes 7077896 | tf_op jit(solution)/shard_map/ppermute | solution.py:99
  (51 other events, 244.6 us)

commit v3 on v2

--- a/solution.py
+++ b/solution.py
@@ -99,13 +99,20 @@
     return lax.ppermute(value, "seq", pairs)
 
 
+def both(mine, other, place):
+    where = lax.broadcasted_iota(jnp.int32, (2,) + mine.shape, 0)
+    pair = jnp.where(where == place, mine[None], other[None])
+    return pair.reshape((2 * mine.shape[0],) + mine.shape[1:])
+
+
 def streams_of(n):
     rest = list(range(1, n.bit_length() - 1))
     return [rest[s:] + rest[:s] for s in range(min(3, len(rest)))]
 
 
-def reduce_all(part, n, index):
+def reduce_all(part, n, index, after=None):
     rows, cols = part.shape
+    after = after or {}
     orders = streams_of(n)
     unit = n // 2
     blocks = part.reshape(rows // ROWS, ROWS, cols)
@@ -124,22 +131,20 @@
             mine = (index >> order[step]) & 1
             sent.append(lax.dynamic_slice_in_dim(piece, (1 - mine) * half, half, 0).astype(jnp.bfloat16))
             kept.append(lax.dynamic_slice_in_dim(piece, mine * half, half, 0))
-        sent = lax.optimization_barrier(tuple(sent))
+        sent = lax.optimization_barrier(tuple(sent) + tuple(after.get(step, ())))[: len(sent)]
         got = [swap(value, n, order[step]) for value, order in zip(sent, orders)]
         got = lax.optimization_barrier(tuple(got))
         pieces = [k + g.astype(jnp.float32) for k, g in zip(kept, got)]
     pieces = [piece.astype(jnp.bfloat16) for piece in pieces]
     for step in reversed(range(steps)):
-        pieces = lax.optimization_barrier(tuple(pieces))
+        pieces = lax.optimization_barrier(
+            tuple(pieces) + tuple(after.get(2 * steps - 1 - step, ()))
+        )[: len(pieces)]
         got = [swap(value, n, order[step]) for value, order in zip(pieces, orders)]
         got = lax.optimization_barrier(tuple(got))
         joined = []
         for piece, other, order in zip(pieces, got, orders):
-            half = piece.shape[0]
-            mine = (index >> order[step]) & 1
-            whole = jnp.zeros((2 * half,) + piece.shape[1:], piece.dtype)
-            whole = lax.dynamic_update_slice_in_dim(whole, piece, mine * half, 0)
-            joined.append(lax.dynamic_update_slice_in_dim(whole, other, (1 - mine) * half, 0))
+            joined.append(both(piece, other, (index >> order[step]) & 1))
         pieces = joined
     return jnp.concatenate(pieces, axis=0)
 
@@ -208,9 +213,7 @@
         return jnp.concatenate([own, swap(sent, n, 0)], axis=0)
 
     def both_cores(blocks):
-        theirs = swap(blocks, n, 0)
-        place = lax.broadcasted_iota(jnp.int32, (2,) + blocks.shape, 0)
-        return jnp.where(place == core, blocks[None], theirs[None])
+        return both(blocks, swap(blocks, n, 0), core).reshape((2,) + blocks.shape)
 
     d_outer_out = outward(d_mixed_bf)
     d_outer_out, small, pair_per_doc, pair_tokens = lax.optimization_barrier(
@@ -221,12 +224,17 @@
     pooled = small[:docs] * len_scale[:, None]
     d_pooled = small[docs:] * len_scale[:, None]
 
-    d_outer_k = across(d_outer_out).reshape(n * here, share, width)
-    d_inner_k = jnp.einsum("kmi,mkc->ikc", second_factor, d_outer_k, preferred_element_type=f32).astype(bf16)
+    same = jnp.eye(share, dtype=bf16)
+    mixer = jnp.einsum("kmi,kq->mkiq", second_factor, same).reshape(n * here * share, n * here * share)
+    mixer = mixer.astype(bf16)
+    d_outer_rows = across(d_outer_out).reshape(n * here * share, width)
+    d_outer_k = d_outer_rows.reshape(n * here, share, width)
+    d_inner_k = jnp.einsum("pq,pc->qc", mixer, d_outer_rows, preferred_element_type=f32).astype(bf16)
     d_inner_k, inner_out = lax.optimization_barrier((d_inner_k, outward(inner_mix)))
     d_inner_back = across(d_inner_k.reshape(n, here, share, width))
     inner_out, d_inner_back = lax.optimization_barrier((inner_out, d_inner_back))
-    inner_k = across(inner_out).reshape(n * here, share, width)
+    inner_rows = across(inner_out).reshape(n * here * share, width)
+    inner_k = inner_rows.reshape(n * here, share, width)
 
     d_rows = jnp.transpose(d_inner_back, (1, 0, 2, 3)).reshape(here, block, width)
     d_value_bf = (
@@ -243,12 +251,16 @@
     value_part = jnp.einsum(
         "to,it->oi", half_columns(d_value_bf), pair_tokens, preferred_element_type=f32
     )
+    outer_k = jnp.einsum("pq,qc->pc", mixer, inner_rows, preferred_element_type=f32).astype(bf16)
+    outer_back = across(outer_k.reshape(n, here, share, width))
     value_sum = both_cores(
-        reduce_all(jnp.concatenate([value_part, d_up_part, d_down_part], axis=0), n, index)
-    )
-
-    outer_k = jnp.einsum("kmi,ikc->mkc", second_factor, inner_k, preferred_element_type=f32).astype(bf16)
-    outer_back = across(outer_k.reshape(n, here, share, width))
+        reduce_all(
+            jnp.concatenate([value_part, d_up_part, d_down_part], axis=0),
+            n,
+            index,
+            {2: (inner_rows,), 6: (outer_back,)},
+        )
+    )
     d_second = jnp.einsum("mkc,ikc->kmi", d_outer_k, inner_k, preferred_element_type=f32)
     d_first = jnp.einsum("ikc,ijc->ikj", d_rows, blocked, preferred_element_type=f32)
 

time: 426 us -> 413 us (0.969)
  waiting for transfers between devices: 195 us -> 154 us
  other arithmetic: 38.2 us -> 58.7 us
    all_to_all x4, waiting for transfers between devices: 29.7 us -> 8.81 us  [across(): return lax.all_to_all(rows, 'seq', split_axis=0, concat_axis=0, tiled=True)]
    ppermute x59, waiting for transfers between devices: 166 us -> 145 us  [swap(): return lax.ppermute(value, 'seq', pairs)]
    dynamic_update_slice x48 -> x0, local copies, waits for them, and re-layouts: 10.3 us -> none  [the longest x24 5.64 us: reduce_all(): lax.dynamic_update_slice_in_dim(whole, other, (1 - mine) * half, 0)]
    select_n x1 -> x17, other arithmetic: 0.61 us -> 10.2 us  [both(): pair = jnp.where(where == place, mine[None], other[None])]
    transpose x0 -> x1, other arithmetic: none -> 6.94 us  [seq_body(): jnp.einsum('kmi,kq->mkiq', second_factor, same)]
    unnamed x76 -> x89, local copies, waits for them, and re-layouts: 10.2 us -> 16.5 us
    iota x2 -> x34, local copies, waits for them, and re-layouts: 1.54 us -> 6.24 us  [both(): where = lax.broadcasted_iota(jnp.int32, (2,) + mine.shape, 0)]
    reshape x3 -> x1, local copies, waits for them, and re-layouts: 10.7 us -> 13.5 us  [seq_body(): jnp.einsum('kmi,kq->mkiq', second_factor, same)]
  transfers between devices with their start and end apart: 63 -> 63, of which waited for: 35 -> 32; matrix products, arithmetic and copies ran while one was open for 19% -> 23% of each run, Pallas kernels for 0% -> 0%
where the time goes in v3:
time: 413 us; the launch traced here: 406 us
  waiting for transfers between devices  154 us (37%)
  starting transfers between devices  93.4 us (23%)
  other arithmetic  58.7 us (14%)
  local copies, waits for them, and re-layouts  54.4 us (13%)
  matrix products  43.8 us (11%)
    ppermute x59, waiting for transfers between devices, swap(): return lax.ppermute(value, 'seq', pairs)  145 us
    ppermute x59, starting transfers between devices, swap(): return lax.ppermute(value, 'seq', pairs)  71.1 us
    all_to_all x4, starting transfers between devices, across(): return lax.all_to_all(rows, 'seq', split_axis=0, concat_axis=0, tiled=True)  22.3 us
    unnamed x89, local copies, waits for them, and re-layouts  16.5 us
    reshape x1, local copies, waits for them, and re-layouts, seq_body(): jnp.einsum('kmi,kq->mkiq', second_factor, same)  13.5 us
    add x18, other arithmetic, reduce_all(): pieces = [k + g.astype(jnp.float32) for k, g in zip(kept, got)]  11.5 us
    convert_element_type x24, local copies, waits for them, and re-layouts, reduce_all(): lax.dynamic_slice_in_dim(piece, (1 - mine) * half, half, 0)  11.2 us
    select_n x17, other arithmetic, both(): pair = jnp.where(where == place, mine[None], other[None])  10.2 us
  transfers between devices with their start and end apart: 63, of which 32 were waited for; matrix products, arithmetic and copies ran while one was open for 23% of the time, Pallas kernels for 0%

profile of v3, /device:TPU:0, one launch (start us, length us, event | category | flops | bytes accessed | tf_op | source)
XLA Modules:
  0.0 406.5 jit_solution(14934480348537271874)
XLA Ops:
  4.6 5.5 %fusion.7 = (bf16[512,1536]{1,0:T(8,128)(2,1)S(1)}, f32[512,1536]{1,0:T(8,128)S(1)}) fusion(bf16[1536,512]{0,1:T(8,128)(2,1)S(1)} %copy.53, bf16[1536,512]{1,0:T(8,128)(2,1)S(1)} %copy-done.2, bf16[1536,1536]{1,0:T(8,128)(2,1)} %param.10), kind=kOutput, calls=%fused_computation.26 | convolution fusion | flops 2421424128 | bytes 12582912 | tf_op jit(solution)/shard_map/ct,oc->to/dot_general | solution.py:175
  18.3 7.8 %all-to-all-start = ((bf16[32,2,8,1536]{3,2,1,0:T(8,128)(2,1)}), bf16[32,2,8,1536]{3,2,1,0:T(8,128)(2,1)}, u32[]{:S(2)}, u32[]{:S(2)}) async-start(bf16[32,2,8,1536]{3,2,1,0:T(8,128)(2,1)} %bitcast.208), calls=%async_computation | async-start | bytes 3145728 | tf_op jit(solution)/shard_map/all_to_all | solution.py:207
  27.2 5.5 %convolution_convert_fusion.4 = bf16[512,1536]{1,0:T(8,128)(2,1)S(1)} fusion(bf16[1536,512]{1,0:T(8,128)(2,1)} %param.9, bf16[1536,1536]{1,0:T(8,128)(2,1)} %param.11), kind=kOutput, calls=%fused_computation.20 | convolution fusion | flops 2416705536 | bytes 7864320 | tf_op jit(solution)/shard_map/ct,oc->to/dot_general | solution.py:198
  34.6 6.9 %multiply_bitcast_fusion = bf16[64,8,64,8]{3,2,1,0:T(8,128)(2,1)} fusion(bf16[8,64,64]{2,0,1:T(8,128)(2,1)S(1)} %copy.52, bf16[8,8]{1,0:T(8,128)(2,1)S(1)} %fusion.35), kind=kLoop, calls=%fused_computation | loop fusion | flops 262144 | bytes 589952 | tf_op jit(solution)/shard_map/kmi,kq->mkiq/transpose | solution.py:228
  41.6 13.5 %reshape.246 = bf16[512,512]{1,0:T(8,128)(2,1)} reshape(bf16[64,8,64,8]{3,2,1,0:T(8,128)(2,1)} %multiply_bitcast_fusion) | data formatting | bytes 1048576 | tf_op jit(solution)/shard_map/reshape | solution.py:228
  55.1 8.8 %all-to-all-done = bf16[32,2,8,1536]{3,2,1,0:T(8,128)(2,1)} async-done(((bf16[32,2,8,1536]{3,2,1,0:T(8,128)(2,1)}), bf16[32,2,8,1536]{3,2,1,0:T(8,128)(2,1)}, u32[]{:S(2)}, u32[]{:S(2)}) %all-to-all-start) | async-done | bytes 1572896 | tf_op jit(solution)/shard_map/all_to_all | solution.py:207
  63.9 3.7 convolution_convert_fusion.3
  67.6 4.1 %all-to-all-start.1 = ((bf16[32,2,8,1536]{3,2,1,0:T(8,128)(2,1)}), bf16[32,2,8,1536]{3,2,1,0:T(8,128)(2,1)}, u32[]{:S(2)}, u32[]{:S(2)}) async-start(bf16[32,2,8,1536]{3,2,1,0:T(8,128)(2,1)} %bitcast.211), calls=%async_computation.1 | async-start | bytes 3145728 | tf_op jit(solution)/shard_map/all_to_all | solution.py:207
  76.0 9.6 %collective-permute-done.3 = f32[128,128]{1,0:T(8,128)S(1)} collective-permute-done((f32[128,128]{1,0:T(8,128)S(1)}, f32[128,128]{1,0:T(8,128)S(1)}, u32[]{:S(2)}, u32[]{:S(2)}) %collective-permute-start.3) | collective-permute-done | bytes 65568 | tf_op jit(solution)/shard_map/ppermute | solution.py:99
  86.3 4.5 %collective-permute-done.4 = f32[128,128]{1,0:T(8,128)S(1)} collective-permute-done((f32[128,128]{1,0:T(8,128)S(1)}, f32[128,128]{1,0:T(8,128)S(1)}, u32[]{:S(2)}, u32[]{:S(2)}) %collective-permute-start.4) | collective-permute-done | bytes 65568 | tf_op jit(solution)/shard_map/ppermute | solution.py:99
  90.8 8.6 %collective-permute-done.5 = f32[128,128]{1,0:T(8,128)S(1)} collective-permute-done((f32[128,128]{1,0:T(8,128)S(1)}, f32[128,128]{1,0:T(8,128)S(1)}, u32[]{:S(2)}, u32[]{:S(2)}) %collective-permute-start.5) | collective-permute-done | bytes 65568 | tf_op jit(solution)/shard_map/ppermute | solution.py:99
  100.1 4.2 %collective-permute-start.6 = (f32[128,128]{1,0:T(8,128)}, f32[128,128]{1,0:T(8,128)}, u32[]{:S(2)}, u32[]{:S(2)}) collective-permute-start(f32[128,128]{1,0:T(8,128)} %add.244), channel_id=1, source_target_pairs={{0,16},{1,17},{2,18},{3,19},{4,20},{5,21},{6,22},{7,23},{8,24},{9,... | collective-permute-start | bytes 196616 | tf_op jit(solution)/shard_map/ppermute | solution.py:99
  104.7 7.4 %collective-permute-done.6 = f32[128,128]{1,0:T(8,128)} collective-permute-done((f32[128,128]{1,0:T(8,128)}, f32[128,128]{1,0:T(8,128)}, u32[]{:S(2)}, u32[]{:S(2)}) %collective-permute-start.6) | collective-permute-done | bytes 65568 | tf_op jit(solution)/shard_map/ppermute | solution.py:99
  119.3 2.7 fusion.14
  127.0 3.4 all-to-all-start.2
  133.6 20.6 %collective-permute-done.35 = bf16[16,8,1536]{2,1,0:T(8,128)(2,1)} collective-permute-done((bf16[16,8,1536]{2,1,0:T(8,128)(2,1)}, bf16[16,8,1536]{2,1,0:T(8,128)(2,1)}, u32[]{:S(2)}, u32[]{:S(2)}) %collective-permute-start.35) | collective-permute-done | bytes 393248 | tf_op jit(solution)/shard_map/ppermute | solution.py:99
  154.2 10.9 %collective-permute-done.36 = bf16[16,8,1536]{2,1,0:T(8,128)(2,1)} collective-permute-done((bf16[16,8,1536]{2,1,0:T(8,128)(2,1)}, bf16[16,8,1536]{2,1,0:T(8,128)(2,1)}, u32[]{:S(2)}, u32[]{:S(2)}) %collective-permute-start.36) | collective-permute-done | bytes 393248 | tf_op jit(solution)/shard_map/ppermute | solution.py:99
  173.1 2.3 collective-permute-start.37
  177.0 2.4 collective-permute-start.39
  179.4 6.7 %collective-permute-done.38 = bf16[8,8,1536]{2,1,0:T(8,128)(2,1)} collective-permute-done((bf16[8,8,1536]{2,1,0:T(8,128)(2,1)}, bf16[8,8,1536]{2,1,0:T(8,128)(2,1)}, u32[]{:S(2)}, u32[]{:S(2)}) %collective-permute-start.38) | collective-permute-done | bytes 196640 | tf_op jit(solution)/shard_map/ppermute | solution.py:99
  186.1 3.7 convolution_convert_fusion.2
  189.8 7.0 %all-to-all-start.3 = ((bf16[32,2,8,1536]{3,2,1,0:T(8,128)(2,1)}), bf16[32,2,8,1536]{3,2,1,0:T(8,128)(2,1)}, u32[]{:S(2)}, u32[]{:S(2)}) async-start(bf16[32,2,8,1536]{3,2,1,0:T(8,128)(2,1)} %bitcast.212), calls=%async_computation.3 | async-start | bytes 3145728 | tf_op jit(solution)/shard_map/all_to_all | solution.py:207
  201.1 2.7 collective-permute-start.41
  208.1 30.6 %collective-permute-done.41 = bf16[4,8,1536]{2,1,0:T(8,128)(2,1)S(1)} collective-permute-done((bf16[4,8,1536]{2,1,0:T(8,128)(2,1)S(1)}, bf16[4,8,1536]{2,1,0:T(8,128)(2,1)S(1)}, u32[]{:S(2)}, u32[]{:S(2)}) %collective-permute-start.41) | collective-permute-done | bytes 98336 | tf_op jit(solution)/shard_map/ppermute | solution.py:99
  244.5 4.1 %fusion.3 = (bf16[512,1536]{1,0:T(8,128)(2,1)S(1)}, bf16[1536,512]{0,1:T(8,128)(2,1)}) fusion(bf16[1536,512]{0,1:T(8,128)(2,1)S(1)} %copy-done.14, f32[512,1536]{1,0:T(8,128)S(1)} %copy-done.41, f32[512,1536]{1,0:T(8,128)S(1)} %bitcast.210, f32[64,1536]{1,0:T(8,128)S(1)} %copy-done.25, pred[64,1024]{1,0:T(32,128)(4,1)S(1)} %copy-done.32), kind=kOutput, calls=%fused_computation.11 | convolution fusion | flops 615776256 | bytes 11436032 | tf_op jit(solution)/shard_map/dt,dc->tc/dot_general | solution.py:268
  251.3 2.6 fusion.10
  262.5 8.1 %collective-permute-done.44 = bf16[2,8,1536]{2,1,0:T(8,128)(2,1)S(1)} collective-permute-done((bf16[2,8,1536]{2,1,0:T(8,128)(2,1)S(1)}, bf16[2,8,1536]{2,1,0:T(8,128)(2,1)S(1)}, u32[]{:S(2)}, u32[]{:S(2)}) %collective-permute-start.44) | collective-permute-done | bytes 49184 | tf_op jit(solution)/shard_map/ppermute | solution.py:99
  271.7 5.3 %collective-permute-done.43 = bf16[3,8,1536]{2,1,0:T(8,128)(2,1)} collective-permute-done((bf16[3,8,1536]{2,1,0:T(8,128)(2,1)}, bf16[3,8,1536]{2,1,0:T(8,128)(2,1)}, u32[]{:S(2)}, u32[]{:S(2)}) %collective-permute-start.43) | collective-permute-done | bytes 73760 | tf_op jit(solution)/shard_map/ppermute | solution.py:99
  281.8 2.7 collective-permute-start.13
  286.8 5.0 %collective-permute-done.12 = bf16[8,8,1536]{2,1,0:T(8,128)(2,1)S(1)} collective-permute-done((bf16[8,8,1536]{2,1,0:T(8,128)(2,1)S(1)}, bf16[8,8,1536]{2,1,0:T(8,128)(2,1)S(1)}, u32[]{:S(2)}, u32[]{:S(2)}) %collective-permute-start.12) | collective-permute-done | bytes 196640 | tf_op jit(solution)/shard_map/ppermute | solution.py:99
  293.9 2.6 collective-permute-start.15
  310.5 2.3 collective-permute-start.21
  321.2 2.1 collective-permute-start.50
  325.5 6.4 %collective-permute-done.50 = bf16[4,8,1536]{2,1,0:T(8,128)(2,1)S(1)} collective-permute-done((bf16[4,8,1536]{2,1,0:T(8,128)(2,1)S(1)}, bf16[4,8,1536]{2,1,0:T(8,128)(2,1)S(1)}, u32[]{:S(2)}, u32[]{:S(2)}) %collective-permute-start.50) | collective-permute-done | bytes 98336 | tf_op jit(solution)/shard_map/ppermute | solution.py:99
  334.5 3.1 collective-permute-start.28
  343.6 3.8 collective-permute-done.53
  353.3 2.2 collective-permute-start.31
  357.7 2.2 collective-permute-start.57
  366.0 2.2 bitcast_select_fusion.3
  368.2 2.2 bitcast_select_fusion.2
  371.1 3.0 pad_maximum_fusion.2
  374.8 3.3 fusion.21
  378.1 3.5 fusion.18
  381.7 2.8 copy.62
  384.5 6.8 %fusion = f32[1536,1536]{1,0:T(8,128)} fusion(pred[1536]{0:T(1024)(128)(4,1)S(1)} %iota.187, bf16[96,8,1536]{2,1,0:T(8,128)(2,1)} %collective-permute-done.32, bf16[96,8,1536]{2,1,0:T(8,128)(2,1)} %pad_maximum_fusion.2), kind=kLoop, calls=%fused_computation.4 | loop fusion | flops 4718592 | bytes 14157312 | tf_op jit(solution)/shard_map/convert_element_type | solution.py:281
  391.3 2.4 broadcast_select_fusion
  393.7 2.5 slice.82
  398.7 7.5 %bitcast_convert_fusion = f32[1536,1536]{1,0:T(8,128)} fusion(bf16[2,96,8,1536]{3,2,1,0:T(8,128)(2,1)} %slice.82), kind=kLoop, calls=%fused_computation.2 | loop fusion | flops 2359296 | bytes 14155776 | tf_op jit(solution)/shard_map/reshape | solution.py:281
  (327 shorter events, 132.6 us)
Async XLA Ops:
  0.7 15.9 %collective-permute-start.1 = (bf16[1536,512]{1,0:T(8,128)(2,1)}, bf16[1536,512]{1,0:T(8,128)(2,1)}, u32[]{:S(2)}, u32[]{:S(2)}) collective-permute-start(bf16[1536,512]{1,0:T(8,128)(2,1)} %param.9), channel_id=1, source_target_pairs={{0,1},{1,0},{2,3},{3,2},{4,5},{5,4},{6,7},{7,6},{8,9},{9,8},{10,11... | collective-permute-start | bytes 4718600 | tf_op jit(solution)/shard_map/ppermute | solution.py:99
  18.3 45.5 %all-to-all-start = ((bf16[32,2,8,1536]{3,2,1,0:T(8,128)(2,1)}), bf16[32,2,8,1536]{3,2,1,0:T(8,128)(2,1)}, u32[]{:S(2)}, u32[]{:S(2)}) async-start(bf16[32,2,8,1536]{3,2,1,0:T(8,128)(2,1)} %bitcast.208), calls=%async_computation | async-start | bytes 3145728 | tf_op jit(solution)/shard_map/all_to_all | solution.py:207
  67.6 46.8 %all-to-all-start.1 = ((bf16[32,2,8,1536]{3,2,1,0:T(8,128)(2,1)}), bf16[32,2,8,1536]{3,2,1,0:T(8,128)(2,1)}, u32[]{:S(2)}, u32[]{:S(2)}) async-start(bf16[32,2,8,1536]{3,2,1,0:T(8,128)(2,1)} %bitcast.211), calls=%async_computation.1 | async-start | bytes 3145728 | tf_op jit(solution)/shard_map/all_to_all | solution.py:207
  74.1 11.5 %collective-permute-start.3 = (f32[128,128]{1,0:T(8,128)S(1)}, f32[128,128]{1,0:T(8,128)S(1)}, u32[]{:S(2)}, u32[]{:S(2)}) collective-permute-start(f32[128,128]{1,0:T(8,128)S(1)} %add.241), channel_id=1, source_target_pairs={{0,2},{1,3},{2,0},{3,1},{4,6},{5,7},{6,4},{7,5},{8,10},{9,11},{10,... | collective-permute-start | bytes 196616 | tf_op jit(solution)/shard_map/ppermute | solution.py:99
  90.8 8.7 %collective-permute-start.5 = (f32[128,128]{1,0:T(8,128)S(1)}, f32[128,128]{1,0:T(8,128)S(1)}, u32[]{:S(2)}, u32[]{:S(2)}) collective-permute-start(f32[128,128]{1,0:T(8,128)S(1)} %add.243), channel_id=1, source_target_pairs={{0,8},{1,9},{2,10},{3,11},{4,12},{5,13},{6,14},{7,15},{8,0},{9,1},... | collective-permute-start | bytes 196616 | tf_op jit(solution)/shard_map/ppermute | solution.py:99
  100.1 12.1 %collective-permute-start.6 = (f32[128,128]{1,0:T(8,128)}, f32[128,128]{1,0:T(8,128)}, u32[]{:S(2)}, u32[]{:S(2)}) collective-permute-start(f32[128,128]{1,0:T(8,128)} %add.244), channel_id=1, source_target_pairs={{0,16},{1,17},{2,18},{3,19},{4,20},{5,21},{6,22},{7,23},{8,24},{9,... | collective-permute-start | bytes 196616 | tf_op jit(solution)/shard_map/ppermute | solution.py:99
  125.7 39.4 %collective-permute-start.34 = (bf16[24,8,1536]{2,1,0:T(8,128)(2,1)}, bf16[24,8,1536]{2,1,0:T(8,128)(2,1)}, u32[]{:S(2)}, u32[]{:S(2)}) collective-permute-start(bf16[24,8,1536]{2,1,0:T(8,128)(2,1)} %dynamic-slice_convert_fusion), channel_id=1, source_target_pairs={{0,2},{1,3},{2,0},{3,1},{4,6},{5,7},{6,4},{7,5},{8,10},{9,11},{10,... | collective-permute-start | bytes 1769480 | tf_op jit(solution)/shard_map/ppermute | solution.py:99
  127.0 59.2 %all-to-all-start.2 = ((bf16[32,2,8,1536]{3,2,1,0:T(8,128)(2,1)}), bf16[32,2,8,1536]{3,2,1,0:T(8,128)(2,1)}, u32[]{:S(2)}, u32[]{:S(2)}) async-start(bf16[32,2,8,1536]{3,2,1,0:T(8,128)(2,1)} %bitcast.207), calls=%async_computation.2 | async-start | bytes 3145728 | tf_op jit(solution)/shard_map/all_to_all | solution.py:207
  130.4 23.8 %collective-permute-start.35 = (bf16[16,8,1536]{2,1,0:T(8,128)(2,1)}, bf16[16,8,1536]{2,1,0:T(8,128)(2,1)}, u32[]{:S(2)}, u32[]{:S(2)}) collective-permute-start(bf16[16,8,1536]{2,1,0:T(8,128)(2,1)} %dynamic-slice_convert_fusion.2), channel_id=1, source_target_pairs={{0,4},{1,5},{2,6},{3,7},{4,0},{5,1},{6,2},{7,3},{8,12},{9,13},{10,... | collective-permute-start | bytes 1179656 | tf_op jit(solution)/shard_map/ppermute | solution.py:99
  132.0 33.0 %collective-permute-start.36 = (bf16[16,8,1536]{2,1,0:T(8,128)(2,1)}, bf16[16,8,1536]{2,1,0:T(8,128)(2,1)}, u32[]{:S(2)}, u32[]{:S(2)}) collective-permute-start(bf16[16,8,1536]{2,1,0:T(8,128)(2,1)} %dynamic-slice_convert_fusion.1), channel_id=1, source_target_pairs={{0,8},{1,9},{2,10},{3,11},{4,12},{5,13},{6,14},{7,15},{8,0},{9,1},... | collective-permute-start | bytes 1179656 | tf_op jit(solution)/shard_map/ppermute | solution.py:99
  173.1 13.0 %collective-permute-start.37 = (bf16[12,8,1536]{2,1,0:T(8,128)(2,1)}, bf16[12,8,1536]{2,1,0:T(8,128)(2,1)}, u32[]{:S(2)}, u32[]{:S(2)}) collective-permute-start(bf16[12,8,1536]{2,1,0:T(8,128)(2,1)} %dynamic-slice_convert_fusion.6), channel_id=1, source_target_pairs={{0,4},{1,5},{2,6},{3,7},{4,0},{5,1},{6,2},{7,3},{8,12},{9,13},{10,... | collective-permute-start | bytes 884744 | tf_op jit(solution)/shard_map/ppermute | solution.py:99
  175.4 10.7 %collective-permute-start.38 = (bf16[8,8,1536]{2,1,0:T(8,128)(2,1)}, bf16[8,8,1536]{2,1,0:T(8,128)(2,1)}, u32[]{:S(2)}, u32[]{:S(2)}) collective-permute-start(bf16[8,8,1536]{2,1,0:T(8,128)(2,1)} %dynamic-slice_convert_fusion.8), channel_id=1, source_target_pairs={{0,8},{1,9},{2,10},{3,11},{4,12},{5,13},{6,14},{7,15},{8,0},{9,1},... | collective-permute-start | bytes 589832 | tf_op jit(solution)/shard_map/ppermute | solution.py:99
  177.0 9.1 %collective-permute-start.39 = (bf16[8,8,1536]{2,1,0:T(8,128)(2,1)}, bf16[8,8,1536]{2,1,0:T(8,128)(2,1)}, u32[]{:S(2)}, u32[]{:S(2)}) collective-permute-start(bf16[8,8,1536]{2,1,0:T(8,128)(2,1)} %dynamic-slice_convert_fusion.7), channel_id=1, source_target_pairs={{0,16},{1,17},{2,18},{3,19},{4,20},{5,21},{6,22},{7,23},{8,24},{9,... | collective-permute-start | bytes 589832 | tf_op jit(solution)/shard_map/ppermute | solution.py:99
  189.8 50.3 %all-to-all-start.3 = ((bf16[32,2,8,1536]{3,2,1,0:T(8,128)(2,1)}), bf16[32,2,8,1536]{3,2,1,0:T(8,128)(2,1)}, u32[]{:S(2)}, u32[]{:S(2)}) async-start(bf16[32,2,8,1536]{3,2,1,0:T(8,128)(2,1)} %bitcast.212), calls=%async_computation.3 | async-start | bytes 3145728 | tf_op jit(solution)/shard_map/all_to_all | solution.py:207
  201.1 37.6 %collective-permute-start.41 = (bf16[4,8,1536]{2,1,0:T(8,128)(2,1)S(1)}, bf16[4,8,1536]{2,1,0:T(8,128)(2,1)S(1)}, u32[]{:S(2)}, u32[]{:S(2)}) collective-permute-start(bf16[4,8,1536]{2,1,0:T(8,128)(2,1)S(1)} %dynamic-slice_convert_fusion.14), channel_id=1, source_target_pairs={{0,16},{1,17},{2,18},{3,19},{4,20},{5,21},{6,22},{7,23},{8,24},{9,... | collective-permute-start | bytes 294920 | tf_op jit(solution)/shard_map/ppermute | solution.py:99
  203.8 34.9 %collective-permute-start.42 = (bf16[4,8,1536]{2,1,0:T(8,128)(2,1)S(1)}, bf16[4,8,1536]{2,1,0:T(8,128)(2,1)S(1)}, u32[]{:S(2)}, u32[]{:S(2)}) collective-permute-start(bf16[4,8,1536]{2,1,0:T(8,128)(2,1)S(1)} %dynamic-slice_convert_fusion.13), channel_id=1, source_target_pairs={{0,2},{1,3},{2,0},{3,1},{4,6},{5,7},{6,4},{7,5},{8,10},{9,11},{10,... | collective-permute-start | bytes 294920 | tf_op jit(solution)/shard_map/ppermute | solution.py:99
  205.3 33.4 %collective-permute-start.40 = (bf16[6,8,1536]{2,1,0:T(8,128)(2,1)S(1)}, bf16[6,8,1536]{2,1,0:T(8,128)(2,1)S(1)}, u32[]{:S(2)}, u32[]{:S(2)}) collective-permute-start(bf16[6,8,1536]{2,1,0:T(8,128)(2,1)S(1)} %dynamic-slice_convert_fusion.12), channel_id=1, source_target_pairs={{0,8},{1,9},{2,10},{3,11},{4,12},{5,13},{6,14},{7,15},{8,0},{9,1},... | collective-permute-start | bytes 442376 | tf_op jit(solution)/shard_map/ppermute | solution.py:99
  257.8 19.1 %collective-permute-start.8 = (bf16[16,8,1536]{2,1,0:T(8,128)(2,1)}, bf16[16,8,1536]{2,1,0:T(8,128)(2,1)S(1)}, u32[]{:S(2)}, u32[]{:S(2)}) collective-permute-start(bf16[16,8,1536]{2,1,0:T(8,128)(2,1)} %dynamic-slice_convert_fusion.5), channel_id=1, source_target_pairs={{0,2},{1,3},{2,0},{3,1},{4,6},{5,7},{6,4},{7,5},{8,10},{9,11},{10,... | collective-permute-start | bytes 1179656 | tf_op jit(solution)/shard_map/ppermute | solution.py:99
  259.1 17.9 %collective-permute-start.9 = (bf16[16,8,1536]{2,1,0:T(8,128)(2,1)}, bf16[16,8,1536]{2,1,0:T(8,128)(2,1)}, u32[]{:S(2)}, u32[]{:S(2)}) collective-permute-start(bf16[16,8,1536]{2,1,0:T(8,128)(2,1)} %dynamic-slice_convert_fusion.4), channel_id=1, source_target_pairs={{0,4},{1,5},{2,6},{3,7},{4,0},{5,1},{6,2},{7,3},{8,12},{9,13},{10,... | collective-permute-start | bytes 1179656 | tf_op jit(solution)/shard_map/ppermute | solution.py:99
  260.6 16.4 %collective-permute-start.10 = (bf16[16,8,1536]{2,1,0:T(8,128)(2,1)}, bf16[16,8,1536]{2,1,0:T(8,128)(2,1)}, u32[]{:S(2)}, u32[]{:S(2)}) collective-permute-start(bf16[16,8,1536]{2,1,0:T(8,128)(2,1)} %dynamic-slice_convert_fusion.3), channel_id=1, source_target_pairs={{0,8},{1,9},{2,10},{3,11},{4,12},{5,13},{6,14},{7,15},{8,0},{9,1},... | collective-permute-start | bytes 1179656 | tf_op jit(solution)/shard_map/ppermute | solution.py:99
  261.2 9.4 %collective-permute-start.44 = (bf16[2,8,1536]{2,1,0:T(8,128)(2,1)S(1)}, bf16[2,8,1536]{2,1,0:T(8,128)(2,1)S(1)}, u32[]{:S(2)}, u32[]{:S(2)}) collective-permute-start(bf16[2,8,1536]{2,1,0:T(8,128)(2,1)S(1)} %dynamic-slice_convert_fusion.20), channel_id=1, source_target_pairs={{0,2},{1,3},{2,0},{3,1},{4,6},{5,7},{6,4},{7,5},{8,10},{9,11},{10,... | collective-permute-start | bytes 147464 | tf_op jit(solution)/shard_map/ppermute | solution.py:99
  261.7 9.9 %collective-permute-start.45 = (bf16[2,8,1536]{2,1,0:T(8,128)(2,1)}, bf16[2,8,1536]{2,1,0:T(8,128)(2,1)}, u32[]{:S(2)}, u32[]{:S(2)}) collective-permute-start(bf16[2,8,1536]{2,1,0:T(8,128)(2,1)} %dynamic-slice_convert_fusion.19), channel_id=1, source_target_pairs={{0,4},{1,5},{2,6},{3,7},{4,0},{5,1},{6,2},{7,3},{8,12},{9,13},{10,... | collective-permute-start | bytes 147464 | tf_op jit(solution)/shard_map/ppermute | solution.py:99
  280.4 6.3 %collective-permute-start.11 = (bf16[8,8,1536]{2,1,0:T(8,128)(2,1)S(1)}, bf16[8,8,1536]{2,1,0:T(8,128)(2,1)S(1)}, u32[]{:S(2)}, u32[]{:S(2)}) collective-permute-start(bf16[8,8,1536]{2,1,0:T(8,128)(2,1)S(1)} %dynamic-slice_convert_fusion.11), channel_id=1, source_target_pairs={{0,4},{1,5},{2,6},{3,7},{4,0},{5,1},{6,2},{7,3},{8,12},{9,13},{10,... | collective-permute-start | bytes 589832 | tf_op jit(solution)/shard_map/ppermute | solution.py:99
  281.8 10.0 %collective-permute-start.12 = (bf16[8,8,1536]{2,1,0:T(8,128)(2,1)S(1)}, bf16[8,8,1536]{2,1,0:T(8,128)(2,1)S(1)}, u32[]{:S(2)}, u32[]{:S(2)}) collective-permute-start(bf16[8,8,1536]{2,1,0:T(8,128)(2,1)S(1)} %dynamic-slice_convert_fusion.10), channel_id=1, source_target_pairs={{0,8},{1,9},{2,10},{3,11},{4,12},{5,13},{6,14},{7,15},{8,0},{9,1},... | collective-permute-start | bytes 589832 | tf_op jit(solution)/shard_map/ppermute | solution.py:99
  281.8 11.5 %collective-permute-start.13 = (bf16[8,8,1536]{2,1,0:T(8,128)(2,1)S(1)}, bf16[8,8,1536]{2,1,0:T(8,128)(2,1)S(1)}, u32[]{:S(2)}, u32[]{:S(2)}) collective-permute-start(bf16[8,8,1536]{2,1,0:T(8,128)(2,1)S(1)} %dynamic-slice_convert_fusion.9), channel_id=1, source_target_pairs={{0,16},{1,17},{2,18},{3,19},{4,20},{5,21},{6,22},{7,23},{8,24},{9,... | collective-permute-start | bytes 589832 | tf_op jit(solution)/shard_map/ppermute | solution.py:99
  293.5 6.2 %collective-permute-start.14 = (bf16[4,8,1536]{2,1,0:T(8,128)(2,1)S(1)}, bf16[4,8,1536]{2,1,0:T(8,128)(2,1)S(1)}, u32[]{:S(2)}, u32[]{:S(2)}) collective-permute-start(bf16[4,8,1536]{2,1,0:T(8,128)(2,1)S(1)} %dynamic-slice_convert_fusion.17), channel_id=1, source_target_pairs={{0,8},{1,9},{2,10},{3,11},{4,12},{5,13},{6,14},{7,15},{8,0},{9,1},... | collective-permute-start | bytes 294920 | tf_op jit(solution)/shard_map/ppermute | solution.py:99
  301.3 6.2 %collective-permute-start.17 = (bf16[2,8,1536]{2,1,0:T(8,128)(2,1)S(1)}, bf16[2,8,1536]{2,1,0:T(8,128)(2,1)S(1)}, u32[]{:S(2)}, u32[]{:S(2)}) collective-permute-start(bf16[2,8,1536]{2,1,0:T(8,128)(2,1)S(1)} %dynamic-slice_convert_fusion.23), channel_id=1, source_target_pairs={{0,16},{1,17},{2,18},{3,19},{4,20},{5,21},{6,22},{7,23},{8,24},{9,... | collective-permute-start | bytes 147464 | tf_op jit(solution)/shard_map/ppermute | solution.py:99
  302.3 6.2 %collective-permute-start.18 = (bf16[2,8,1536]{2,1,0:T(8,128)(2,1)S(1)}, bf16[2,8,1536]{2,1,0:T(8,128)(2,1)S(1)}, u32[]{:S(2)}, u32[]{:S(2)}) collective-permute-start(bf16[2,8,1536]{2,1,0:T(8,128)(2,1)S(1)} %dynamic-slice_convert_fusion.22), channel_id=1, source_target_pairs={{0,2},{1,3},{2,0},{3,1},{4,6},{5,7},{6,4},{7,5},{8,10},{9,11},{10,... | collective-permute-start | bytes 147464 | tf_op jit(solution)/shard_map/ppermute | solution.py:99
  304.3 8.6 %collective-permute-start.47 = (bf16[2,8,1536]{2,1,0:T(8,128)(2,1)S(1)}, bf16[2,8,1536]{2,1,0:T(8,128)(2,1)S(1)}, u32[]{:S(2)}, u32[]{:S(2)}) collective-permute-start(bf16[2,8,1536]{2,1,0:T(8,128)(2,1)S(1)} %add_convert_fusion.2), channel_id=1, source_target_pairs={{0,2},{1,3},{2,0},{3,1},{4,6},{5,7},{6,4},{7,5},{8,10},{9,11},{10,... | collective-permute-start | bytes 147464 | tf_op jit(solution)/shard_map/ppermute | solution.py:99
  305.2 8.5 %collective-permute-start.48 = (bf16[2,8,1536]{2,1,0:T(8,128)(2,1)S(1)}, bf16[2,8,1536]{2,1,0:T(8,128)(2,1)S(1)}, u32[]{:S(2)}, u32[]{:S(2)}) collective-permute-start(bf16[2,8,1536]{2,1,0:T(8,128)(2,1)S(1)} %add_convert_fusion.1), channel_id=1, source_target_pairs={{0,4},{1,5},{2,6},{3,7},{4,0},{5,1},{6,2},{7,3},{8,12},{9,13},{10,... | collective-permute-start | bytes 147464 | tf_op jit(solution)/shard_map/ppermute | solution.py:99
  307.5 6.3 %collective-permute-start.46 = (bf16[3,8,1536]{2,1,0:T(8,128)(2,1)S(1)}, bf16[3,8,1536]{2,1,0:T(8,128)(2,1)S(1)}, u32[]{:S(2)}, u32[]{:S(2)}) collective-permute-start(bf16[3,8,1536]{2,1,0:T(8,128)(2,1)S(1)} %add_convert_fusion), channel_id=1, source_target_pairs={{0,16},{1,17},{2,18},{3,19},{4,20},{5,21},{6,22},{7,23},{8,24},{9,... | collective-permute-start | bytes 221192 | tf_op jit(solution)/shard_map/ppermute | solution.py:99
  317.2 6.0 %collective-permute-start.23 = (bf16[4,8,1536]{2,1,0:T(8,128)(2,1)S(1)}, bf16[4,8,1536]{2,1,0:T(8,128)(2,1)S(1)}, u32[]{:S(2)}, u32[]{:S(2)}) collective-permute-start(bf16[4,8,1536]{2,1,0:T(8,128)(2,1)S(1)} %bitcast_select_fusion.24), channel_id=1, source_target_pairs={{0,8},{1,9},{2,10},{3,11},{4,12},{5,13},{6,14},{7,15},{8,0},{9,1},... | collective-permute-start | bytes 294920 | tf_op jit(solution)/shard_map/ppermute | solution.py:99
  317.6 14.3 %collective-permute-start.49 = (bf16[6,8,1536]{2,1,0:T(8,128)(2,1)S(1)}, bf16[6,8,1536]{2,1,0:T(8,128)(2,1)S(1)}, u32[]{:S(2)}, u32[]{:S(2)}) collective-permute-start(bf16[6,8,1536]{2,1,0:T(8,128)(2,1)S(1)} %bitcast_select_fusion.19), channel_id=1, source_target_pairs={{0,8},{1,9},{2,10},{3,11},{4,12},{5,13},{6,14},{7,15},{8,0},{9,1},... | collective-permute-start | bytes 442376 | tf_op jit(solution)/shard_map/ppermute | solution.py:99
  321.2 10.7 %collective-permute-start.50 = (bf16[4,8,1536]{2,1,0:T(8,128)(2,1)S(1)}, bf16[4,8,1536]{2,1,0:T(8,128)(2,1)S(1)}, u32[]{:S(2)}, u32[]{:S(2)}) collective-permute-start(bf16[4,8,1536]{2,1,0:T(8,128)(2,1)S(1)} %get-tuple-element.198), channel_id=1, source_target_pairs={{0,16},{1,17},{2,18},{3,19},{4,20},{5,21},{6,22},{7,23},{8,24},{9,... | collective-permute-start | bytes 294920 | tf_op jit(solution)/shard_map/ppermute | solution.py:99
  323.3 8.6 %collective-permute-start.51 = (bf16[4,8,1536]{2,1,0:T(8,128)(2,1)S(1)}, bf16[4,8,1536]{2,1,0:T(8,128)(2,1)S(1)}, u32[]{:S(2)}, u32[]{:S(2)}) collective-permute-start(bf16[4,8,1536]{2,1,0:T(8,128)(2,1)S(1)} %get-tuple-element.199), channel_id=1, source_target_pairs={{0,2},{1,3},{2,0},{3,1},{4,6},{5,7},{6,4},{7,5},{8,10},{9,11},{10,... | collective-permute-start | bytes 294920 | tf_op jit(solution)/shard_map/ppermute | solution.py:99
  333.1 15.6 %collective-permute-start.52 = (bf16[12,8,1536]{2,1,0:T(8,128)(2,1)S(1)}, bf16[12,8,1536]{2,1,0:T(8,128)(2,1)}, u32[]{:S(2)}, u32[]{:S(2)}) collective-permute-start(bf16[12,8,1536]{2,1,0:T(8,128)(2,1)S(1)} %bitcast_select_fusion.13), channel_id=1, source_target_pairs={{0,4},{1,5},{2,6},{3,7},{4,0},{5,1},{6,2},{7,3},{8,12},{9,13},{10,... | collective-permute-start | bytes 884744 | tf_op jit(solution)/shard_map/ppermute | solution.py:99
  334.5 7.3 %collective-permute-start.27 = (bf16[8,8,1536]{2,1,0:T(8,128)(2,1)S(1)}, bf16[8,8,1536]{2,1,0:T(8,128)(2,1)S(1)}, u32[]{:S(2)}, u32[]{:S(2)}) collective-permute-start(bf16[8,8,1536]{2,1,0:T(8,128)(2,1)S(1)} %get-tuple-element.154), channel_id=1, source_target_pairs={{0,8},{1,9},{2,10},{3,11},{4,12},{5,13},{6,14},{7,15},{8,0},{9,1},... | collective-permute-start | bytes 589832 | tf_op jit(solution)/shard_map/ppermute | solution.py:99
  334.5 9.0 %collective-permute-start.28 = (bf16[8,8,1536]{2,1,0:T(8,128)(2,1)S(1)}, bf16[8,8,1536]{2,1,0:T(8,128)(2,1)S(1)}, u32[]{:S(2)}, u32[]{:S(2)}) collective-permute-start(bf16[8,8,1536]{2,1,0:T(8,128)(2,1)S(1)} %get-tuple-element.155), channel_id=1, source_target_pairs={{0,16},{1,17},{2,18},{3,19},{4,20},{5,21},{6,22},{7,23},{8,24},{9,... | collective-permute-start | bytes 589832 | tf_op jit(solution)/shard_map/ppermute | solution.py:99
  337.6 9.8 %collective-permute-start.53 = (bf16[8,8,1536]{2,1,0:T(8,128)(2,1)S(1)}, bf16[8,8,1536]{2,1,0:T(8,128)(2,1)S(1)}, u32[]{:S(2)}, u32[]{:S(2)}) collective-permute-start(bf16[8,8,1536]{2,1,0:T(8,128)(2,1)S(1)} %get-tuple-element.204), channel_id=1, source_target_pairs={{0,8},{1,9},{2,10},{3,11},{4,12},{5,13},{6,14},{7,15},{8,0},{9,1},... | collective-permute-start | bytes 589832 | tf_op jit(solution)/shard_map/ppermute | solution.py:99
  337.8 10.2 %collective-permute-start.54 = (bf16[8,8,1536]{2,1,0:T(8,128)(2,1)S(1)}, bf16[8,8,1536]{2,1,0:T(8,128)(2,1)S(1)}, u32[]{:S(2)}, u32[]{:S(2)}) collective-permute-start(bf16[8,8,1536]{2,1,0:T(8,128)(2,1)S(1)} %get-tuple-element.205), channel_id=1, source_target_pairs={{0,16},{1,17},{2,18},{3,19},{4,20},{5,21},{6,22},{7,23},{8,24},{9,... | collective-permute-start | bytes 589832 | tf_op jit(solution)/shard_map/ppermute | solution.py:99
  349.9 7.8 %collective-permute-start.29 = (bf16[16,8,1536]{2,1,0:T(8,128)(2,1)S(1)}, bf16[16,8,1536]{2,1,0:T(8,128)(2,1)S(1)}, u32[]{:S(2)}, u32[]{:S(2)}) collective-permute-start(bf16[16,8,1536]{2,1,0:T(8,128)(2,1)S(1)} %bitcast_select_fusion.12), channel_id=1, source_target_pairs={{0,2},{1,3},{2,0},{3,1},{4,6},{5,7},{6,4},{7,5},{8,10},{9,11},{10,... | collective-permute-start | bytes 1179656 | tf_op jit(solution)/shard_map/ppermute | solution.py:99
  351.2 14.6 %collective-permute-start.55 = (bf16[24,8,1536]{2,1,0:T(8,128)(2,1)S(1)}, bf16[24,8,1536]{2,1,0:T(8,128)(2,1)S(1)}, u32[]{:S(2)}, u32[]{:S(2)}) collective-permute-start(bf16[24,8,1536]{2,1,0:T(8,128)(2,1)S(1)} %bitcast_select_fusion.7), channel_id=1, source_target_pairs={{0,2},{1,3},{2,0},{3,1},{4,6},{5,7},{6,4},{7,5},{8,10},{9,11},{10,... | collective-permute-start | bytes 1769480 | tf_op jit(solution)/shard_map/ppermute | solution.py:99
  353.3 10.6 %collective-permute-start.30 = (bf16[16,8,1536]{2,1,0:T(8,128)(2,1)S(1)}, bf16[16,8,1536]{2,1,0:T(8,128)(2,1)}, u32[]{:S(2)}, u32[]{:S(2)}) collective-permute-start(bf16[16,8,1536]{2,1,0:T(8,128)(2,1)S(1)} %get-tuple-element.160), channel_id=1, source_target_pairs={{0,4},{1,5},{2,6},{3,7},{4,0},{5,1},{6,2},{7,3},{8,12},{9,13},{10,... | collective-permute-start | bytes 1179656 | tf_op jit(solution)/shard_map/ppermute | solution.py:99
  353.3 10.6 %collective-permute-start.31 = (bf16[16,8,1536]{2,1,0:T(8,128)(2,1)S(1)}, bf16[16,8,1536]{2,1,0:T(8,128)(2,1)}, u32[]{:S(2)}, u32[]{:S(2)}) collective-permute-start(bf16[16,8,1536]{2,1,0:T(8,128)(2,1)S(1)} %get-tuple-element.161), channel_id=1, source_target_pairs={{0,8},{1,9},{2,10},{3,11},{4,12},{5,13},{6,14},{7,15},{8,0},{9,1},... | collective-permute-start | bytes 1179656 | tf_op jit(solution)/shard_map/ppermute | solution.py:99
  355.5 9.9 %collective-permute-start.56 = (bf16[16,8,1536]{2,1,0:T(8,128)(2,1)S(1)}, bf16[16,8,1536]{2,1,0:T(8,128)(2,1)}, u32[]{:S(2)}, u32[]{:S(2)}) collective-permute-start(bf16[16,8,1536]{2,1,0:T(8,128)(2,1)S(1)} %get-tuple-element.210), channel_id=1, source_target_pairs={{0,4},{1,5},{2,6},{3,7},{4,0},{5,1},{6,2},{7,3},{8,12},{9,13},{10,... | collective-permute-start | bytes 1179656 | tf_op jit(solution)/shard_map/ppermute | solution.py:99
  357.7 8.1 %collective-permute-start.57 = (bf16[16,8,1536]{2,1,0:T(8,128)(2,1)S(1)}, bf16[16,8,1536]{2,1,0:T(8,128)(2,1)}, u32[]{:S(2)}, u32[]{:S(2)}) collective-permute-start(bf16[16,8,1536]{2,1,0:T(8,128)(2,1)S(1)} %get-tuple-element.211), channel_id=1, source_target_pairs={{0,8},{1,9},{2,10},{3,11},{4,12},{5,13},{6,14},{7,15},{8,0},{9,1},... | collective-permute-start | bytes 1179656 | tf_op jit(solution)/shard_map/ppermute | solution.py:99
  370.7 20.6 %collective-permute-start.58 = (bf16[112,8,1536]{2,1,0:T(8,128)(2,1)S(1)}, bf16[112,8,1536]{2,1,0:T(8,128)(2,1)}, u32[]{:S(2)}, u32[]{:S(2)}) collective-permute-start(bf16[112,8,1536]{2,1,0:T(8,128)(2,1)S(1)} %pad_maximum_fusion.1), channel_id=1, source_target_pairs={{0,1},{1,0},{2,3},{3,2},{4,5},{5,4},{6,7},{7,6},{8,9},{9,8},{10,11... | collective-permute-start | bytes 8257544 | tf_op jit(solution)/shard_map/ppermute | solution.py:99
  374.1 10.3 %collective-permute-start.32 = (bf16[96,8,1536]{2,1,0:T(8,128)(2,1)}, bf16[96,8,1536]{2,1,0:T(8,128)(2,1)}, u32[]{:S(2)}, u32[]{:S(2)}) collective-permute-start(bf16[96,8,1536]{2,1,0:T(8,128)(2,1)} %pad_maximum_fusion.2), channel_id=1, source_target_pairs={{0,1},{1,0},{2,3},{3,2},{4,5},{5,4},{6,7},{7,6},{8,9},{9,8},{10,11... | collective-permute-start | bytes 7077896 | tf_op jit(solution)/shard_map/ppermute | solution.py:99
  (57 other events, 291.8 us)

commit v4 on v3

--- a/solution.py
+++ b/solution.py
@@ -110,7 +110,7 @@
     return [rest[s:] + rest[:s] for s in range(min(3, len(rest)))]
 
 
-def reduce_all(part, n, index, after=None):
+def reduce_streams(part, n, index, after=None):
     rows, cols = part.shape
     after = after or {}
     orders = streams_of(n)
@@ -123,8 +123,7 @@
     for share in shares:
         pieces.append(blocks[low : low + share * unit])
         low += share * unit
-    steps = len(orders[0])
-    for step in range(steps):
+    for step in range(len(orders[0])):
         sent, kept = [], []
         for piece, order in zip(pieces, orders):
             half = piece.shape[0] // 2
@@ -135,18 +134,29 @@
         got = [swap(value, n, order[step]) for value, order in zip(sent, orders)]
         got = lax.optimization_barrier(tuple(got))
         pieces = [k + g.astype(jnp.float32) for k, g in zip(kept, got)]
-    pieces = [piece.astype(jnp.bfloat16) for piece in pieces]
-    for step in reversed(range(steps)):
-        pieces = lax.optimization_barrier(
-            tuple(pieces) + tuple(after.get(2 * steps - 1 - step, ()))
-        )[: len(pieces)]
+    return [piece.astype(jnp.bfloat16) for piece in pieces]
+
+
+def gather_streams(firsts, seconds, n, index):
+    orders = streams_of(n)
+    cuts = [piece.shape[0] for piece in firsts]
+    pieces = [jnp.concatenate([a, b], axis=0)[None] for a, b in zip(firsts, seconds)]
+    for step in reversed(range(len(orders[0]))):
+        pieces = lax.optimization_barrier(tuple(pieces))
         got = [swap(value, n, order[step]) for value, order in zip(pieces, orders)]
         got = lax.optimization_barrier(tuple(got))
-        joined = []
-        for piece, other, order in zip(pieces, got, orders):
-            joined.append(both(piece, other, (index >> order[step]) & 1))
-        pieces = joined
-    return jnp.concatenate(pieces, axis=0)
+        pieces = [
+            both(piece, other, (index >> order[step]) & 1)
+            for piece, other, order in zip(pieces, got, orders)
+        ]
+
+    def joined(parts):
+        return jnp.concatenate([p.reshape((-1,) + p.shape[2:]) for p in parts], axis=0)
+
+    return (
+        joined([piece[:, :cut] for piece, cut in zip(pieces, cuts)]),
+        joined([piece[:, cut:] for piece, cut in zip(pieces, cuts)]),
+    )
 
 
 def seq_body(
@@ -212,9 +222,6 @@
         sent = lax.dynamic_slice_in_dim(rows, (1 - core) * half, half, 1)
         return jnp.concatenate([own, swap(sent, n, 0)], axis=0)
 
-    def both_cores(blocks):
-        return both(blocks, swap(blocks, n, 0), core).reshape((2,) + blocks.shape)
-
     d_outer_out = outward(d_mixed_bf)
     d_outer_out, small, pair_per_doc, pair_tokens = lax.optimization_barrier(
         (d_outer_out, small, per_doc + swap(per_doc, n, 0), pair_tokens)
@@ -253,13 +260,11 @@
     )
     outer_k = jnp.einsum("pq,qc->pc", mixer, inner_rows, preferred_element_type=f32).astype(bf16)
     outer_back = across(outer_k.reshape(n, here, share, width))
-    value_sum = both_cores(
-        reduce_all(
-            jnp.concatenate([value_part, d_up_part, d_down_part], axis=0),
-            n,
-            index,
-            {2: (inner_rows,), 6: (outer_back,)},
-        )
+    value_pieces = reduce_streams(
+        jnp.concatenate([value_part, d_up_part, d_down_part], axis=0),
+        n,
+        index,
+        {2: (inner_rows,)},
     )
     d_second = jnp.einsum("mkc,ikc->kmi", d_outer_k, inner_k, preferred_element_type=f32)
     d_first = jnp.einsum("ikc,ijc->ikj", d_rows, blocked, preferred_element_type=f32)
@@ -272,22 +277,30 @@
     gate_part = jnp.einsum(
         "to,it->oi", half_columns(d_gate_bf), pair_tokens, preferred_element_type=f32
     )
-    gate_sum = both_cores(reduce_all(gate_part, n, index))
-
+    gate_part, d_second, d_first, hidden = lax.optimization_barrier(
+        (gate_part, d_second, d_first, hidden)
+    )
+    gate_pieces = reduce_streams(gate_part, n, index)
+    value_ours, gate_ours = gather_streams(value_pieces, gate_pieces, n, index)
+    value_ours, gate_ours = lax.optimization_barrier((value_ours, gate_ours))
+    value_theirs, gate_theirs = lax.optimization_barrier(
+        (swap(value_ours, n, 0), swap(gate_ours, n, 0))
+    )
     blocks_w = width // 2 // ROWS
     blocks_l = half_lats // ROWS
 
-    def rows_of(blocks, extent):
-        return blocks.astype(f32).reshape(extent, width)
+    def rows_of(ours, theirs, low, size):
+        rows = both(ours[low : low + size], theirs[low : low + size], core)
+        return rows.astype(f32).reshape(2 * size * ROWS, width)
 
     return (
         hidden,
-        rows_of(gate_sum, width),
-        rows_of(value_sum[:, :blocks_w], width),
+        rows_of(gate_ours, gate_theirs, 0, blocks_w),
+        rows_of(value_ours, value_theirs, 0, blocks_w),
         d_first,
         d_second,
-        rows_of(value_sum[:, blocks_w + blocks_l :], lats).T,
-        rows_of(value_sum[:, blocks_w : blocks_w + blocks_l], lats).T,
+        rows_of(value_ours, value_theirs, blocks_w + blocks_l, blocks_l).T,
+        rows_of(value_ours, value_theirs, blocks_w, blocks_l).T,
     )
 
 

time: 413 us -> 386 us (0.935); the launches traced: 406 us -> 385 us
  starting transfers between devices: 93.4 us -> 82.7 us
  waiting for transfers between devices: 154 us -> 145 us
  other arithmetic: 58.7 us -> 50.5 us
    ppermute x59 -> x47, waiting for transfers between devices: 145 us -> 136 us  [swap(): return lax.ppermute(value, 'seq', pairs)]
    reshape x1 -> x0, other arithmetic: 7.46 us -> none  [rows_of(): return blocks.astype(f32).reshape(extent, width)]
    ppermute x59 -> x47, starting transfers between devices: 71.1 us -> 63.7 us  [swap(): return lax.ppermute(value, 'seq', pairs)]
    slice x4 -> x12, local copies, waits for them, and re-layouts: 3.03 us -> 8.56 us  [the longest x4 5.89 us: rows_of(): rows = both(ours[low:low + size], theirs[low:low + size], core)]
    select_n x17 -> x12, other arithmetic: 10.2 us -> 6.74 us  [both(): pair = jnp.where(where == place, mine[None], other[None])]
    unnamed x89 -> x99, local copies, waits for them, and re-layouts: 16.5 us -> 18.9 us
  transfers between devices with their start and end apart: 63 -> 51, of which waited for: 32 -> 31; matrix products, arithmetic and copies ran while one was open for 23% -> 24% of each run, Pallas kernels for 0% -> 0%
where the time goes in v4:
time: 386 us; the launch traced here: 385 us
  waiting for transfers between devices  145 us (38%)
  starting transfers between devices  82.7 us (21%)
  local copies, waits for them, and re-layouts  57.2 us (15%)
  other arithmetic  50.5 us (13%)
  matrix products  47.5 us (12%)
    ppermute x47, waiting for transfers between devices, swap(): return lax.ppermute(value, 'seq', pairs)  136 us
    ppermute x47, starting transfers between devices, swap(): return lax.ppermute(value, 'seq', pairs)  63.7 us
    all_to_all x4, starting transfers between devices, across(): return lax.all_to_all(rows, 'seq', split_axis=0, concat_axis=0, tiled=True)  19 us
    unnamed x99, local copies, waits for them, and re-layouts  18.9 us
    reshape x1, local copies, waits for them, and re-layouts, seq_body(): jnp.einsum('kmi,kq->mkiq', second_factor, same)  13.5 us
    add x18, other arithmetic, reduce_streams(): pieces = [k + g.astype(jnp.float32) for k, g in zip(kept, got)]  12 us
    convert_element_type x1, other arithmetic, rows_of(): return rows.astype(f32).reshape(2 * size * ROWS, width)  9.3 us
    convert_element_type x24, local copies, waits for them, and re-layouts, reduce_streams(): lax.dynamic_slice_in_dim(piece, (1 - mine) * half, half, 0)  8.91 us
  transfers between devices with their start and end apart: 51, of which 31 were waited for; matrix products, arithmetic and copies ran while one was open for 24% of the time, Pallas kernels for 0%

profile of v4, /device:TPU:0, one launch (start us, length us, event | category | flops | bytes accessed | tf_op | source)
XLA Modules:
  0.0 384.6 jit_solution(10175863187232886109)
XLA Ops:
  4.6 5.5 %fusion.8 = (bf16[512,1536]{1,0:T(8,128)(2,1)S(1)}, f32[512,1536]{1,0:T(8,128)S(1)}) fusion(bf16[1536,512]{0,1:T(8,128)(2,1)S(1)} %copy.48, bf16[1536,512]{1,0:T(8,128)(2,1)S(1)} %copy-done.2, bf16[1536,1536]{1,0:T(8,128)(2,1)} %param.10), kind=kOutput, calls=%fused_computation.26 | convolution fusion | flops 2421424128 | bytes 12582912 | tf_op jit(solution)/shard_map/ct,oc->to/dot_general | solution.py:185
  18.4 7.5 %all-to-all-start = ((bf16[32,2,8,1536]{3,2,1,0:T(8,128)(2,1)}), bf16[32,2,8,1536]{3,2,1,0:T(8,128)(2,1)}, u32[]{:S(2)}, u32[]{:S(2)}) async-start(bf16[32,2,8,1536]{3,2,1,0:T(8,128)(2,1)} %bitcast.177), calls=%async_computation | async-start | bytes 3145728 | tf_op jit(solution)/shard_map/all_to_all | solution.py:217
  26.9 5.5 %convolution_convert_fusion.4 = bf16[512,1536]{1,0:T(8,128)(2,1)S(1)} fusion(bf16[1536,512]{1,0:T(8,128)(2,1)} %param.9, bf16[1536,1536]{1,0:T(8,128)(2,1)} %param.11), kind=kOutput, calls=%fused_computation.20 | convolution fusion | flops 2416705536 | bytes 7864320 | tf_op jit(solution)/shard_map/ct,oc->to/dot_general | solution.py:208
  34.4 6.9 %multiply_bitcast_fusion = bf16[64,8,64,8]{3,2,1,0:T(8,128)(2,1)} fusion(bf16[8,64,64]{2,0,1:T(8,128)(2,1)S(1)} %copy.49, bf16[8,8]{1,0:T(8,128)(2,1)S(1)} %fusion.36), kind=kLoop, calls=%fused_computation | loop fusion | flops 262144 | bytes 589952 | tf_op jit(solution)/shard_map/kmi,kq->mkiq/transpose | solution.py:235
  41.4 13.5 %reshape.216 = bf16[512,512]{1,0:T(8,128)(2,1)} reshape(bf16[64,8,64,8]{3,2,1,0:T(8,128)(2,1)} %multiply_bitcast_fusion) | data formatting | bytes 1048576 | tf_op jit(solution)/shard_map/reshape | solution.py:235
  54.9 8.6 %all-to-all-done = bf16[32,2,8,1536]{3,2,1,0:T(8,128)(2,1)} async-done(((bf16[32,2,8,1536]{3,2,1,0:T(8,128)(2,1)}), bf16[32,2,8,1536]{3,2,1,0:T(8,128)(2,1)}, u32[]{:S(2)}, u32[]{:S(2)}) %all-to-all-start) | async-done | bytes 1572896 | tf_op jit(solution)/shard_map/all_to_all | solution.py:217
  63.5 3.7 convolution_convert_fusion.3
  67.2 3.9 %all-to-all-start.1 = ((bf16[32,2,8,1536]{3,2,1,0:T(8,128)(2,1)}), bf16[32,2,8,1536]{3,2,1,0:T(8,128)(2,1)}, u32[]{:S(2)}, u32[]{:S(2)}) async-start(bf16[32,2,8,1536]{3,2,1,0:T(8,128)(2,1)} %bitcast.184), calls=%async_computation.1 | async-start | bytes 3145728 | tf_op jit(solution)/shard_map/all_to_all | solution.py:217
  75.2 9.8 %collective-permute-done.3 = f32[128,128]{1,0:T(8,128)S(1)} collective-permute-done((f32[128,128]{1,0:T(8,128)S(1)}, f32[128,128]{1,0:T(8,128)S(1)}, u32[]{:S(2)}, u32[]{:S(2)}) %collective-permute-start.3) | collective-permute-done | bytes 65568 | tf_op jit(solution)/shard_map/ppermute | solution.py:99
  85.7 4.6 %collective-permute-done.4 = f32[128,128]{1,0:T(8,128)S(1)} collective-permute-done((f32[128,128]{1,0:T(8,128)S(1)}, f32[128,128]{1,0:T(8,128)S(1)}, u32[]{:S(2)}, u32[]{:S(2)}) %collective-permute-start.4) | collective-permute-done | bytes 65568 | tf_op jit(solution)/shard_map/ppermute | solution.py:99
  90.3 8.5 %collective-permute-done.5 = f32[128,128]{1,0:T(8,128)S(1)} collective-permute-done((f32[128,128]{1,0:T(8,128)S(1)}, f32[128,128]{1,0:T(8,128)S(1)}, u32[]{:S(2)}, u32[]{:S(2)}) %collective-permute-start.5) | collective-permute-done | bytes 65568 | tf_op jit(solution)/shard_map/ppermute | solution.py:99
  99.4 4.2 %collective-permute-start.6 = (f32[128,128]{1,0:T(8,128)}, f32[128,128]{1,0:T(8,128)}, u32[]{:S(2)}, u32[]{:S(2)}) collective-permute-start(f32[128,128]{1,0:T(8,128)} %add.244), channel_id=1, source_target_pairs={{0,16},{1,17},{2,18},{3,19},{4,20},{5,21},{6,22},{7,23},{8,24},{9,... | collective-permute-start | bytes 196616 | tf_op jit(solution)/shard_map/ppermute | solution.py:99
  104.2 7.4 %collective-permute-done.6 = f32[128,128]{1,0:T(8,128)} collective-permute-done((f32[128,128]{1,0:T(8,128)}, f32[128,128]{1,0:T(8,128)}, u32[]{:S(2)}, u32[]{:S(2)}) %collective-permute-start.6) | collective-permute-done | bytes 65568 | tf_op jit(solution)/shard_map/ppermute | solution.py:99
  120.8 4.3 %all-to-all-start.2 = ((bf16[32,2,8,1536]{3,2,1,0:T(8,128)(2,1)}), bf16[32,2,8,1536]{3,2,1,0:T(8,128)(2,1)}, u32[]{:S(2)}, u32[]{:S(2)}) async-start(bf16[32,2,8,1536]{3,2,1,0:T(8,128)(2,1)} %bitcast.176), calls=%async_computation.2 | async-start | bytes 3145728 | tf_op jit(solution)/shard_map/all_to_all | solution.py:217
  125.1 4.0 %fusion.15 = f32[768,1536]{1,0:T(8,128)S(1)} fusion(bf16[1536,1024]{1,0:T(8,128)(2,1)S(1)} %pad_maximum_fusion, bf16[512,768]{1,0:T(8,128)(2,1)} %collective-permute-done.8, bf16[512,768]{1,0:T(8,128)(2,1)} %get-tuple-element.219), kind=kOutput, calls=%fused_computation.37 | convolution fusion | flops 2419064832 | bytes 9437184 | tf_op jit(solution)/shard_map/to,it->oi/dot_general | solution.py:258
  138.1 2.2 fusion.49
  140.3 12.3 %collective-permute-done.10 = bf16[16,8,1536]{2,1,0:T(8,128)(2,1)} collective-permute-done((bf16[16,8,1536]{2,1,0:T(8,128)(2,1)}, bf16[16,8,1536]{2,1,0:T(8,128)(2,1)}, u32[]{:S(2)}, u32[]{:S(2)}) %collective-permute-start.10) | collective-permute-done | bytes 393248 | tf_op jit(solution)/shard_map/ppermute | solution.py:99
  152.6 7.2 %collective-permute-done.11 = bf16[16,8,1536]{2,1,0:T(8,128)(2,1)} collective-permute-done((bf16[16,8,1536]{2,1,0:T(8,128)(2,1)}, bf16[16,8,1536]{2,1,0:T(8,128)(2,1)}, u32[]{:S(2)}, u32[]{:S(2)}) %collective-permute-start.11) | collective-permute-done | bytes 393248 | tf_op jit(solution)/shard_map/ppermute | solution.py:99
  166.8 2.5 collective-permute-start.13
  172.8 3.7 convolution_convert_fusion.2
  176.5 3.4 all-to-all-start.3
  179.9 3.4 fusion.20
  187.3 2.7 collective-permute-start.16
  193.0 3.5 fusion.22
  196.5 25.3 %collective-permute-done.16 = bf16[4,8,1536]{2,1,0:T(8,128)(2,1)S(1)} collective-permute-done((bf16[4,8,1536]{2,1,0:T(8,128)(2,1)S(1)}, bf16[4,8,1536]{2,1,0:T(8,128)(2,1)S(1)}, u32[]{:S(2)}, u32[]{:S(2)}) %collective-permute-start.16) | collective-permute-done | bytes 98336 | tf_op jit(solution)/shard_map/ppermute | solution.py:99
  227.5 3.9 %fusion.9 = (bf16[1536,512]{0,1:T(8,128)(2,1)}, bf16[512,1536]{1,0:T(8,128)(2,1)S(1)}) fusion(f32[512,1536]{1,0:T(8,128)S(1)} %copy-done.46, bf16[1536,512]{0,1:T(8,128)(2,1)S(1)} %copy-done.23, f32[512,1536]{1,0:T(8,128)S(1)} %bitcast.179, f32[64,1536]{1,0:T(8,128)S(1)} %copy-done.31, pred[64,1024]{1,0:T(32,128)(4,1)S(1)} %copy-done.37), kind=kOutput, calls=%fused_computation.28 | convolution fusion | flops 615776256 | bytes 11436032 | tf_op jit(solution)/shard_map/dt,dc->tc/dot_general | solution.py:273
  233.9 2.7 fusion.11
  246.0 6.8 %collective-permute-done.19 = bf16[2,8,1536]{2,1,0:T(8,128)(2,1)S(1)} collective-permute-done((bf16[2,8,1536]{2,1,0:T(8,128)(2,1)S(1)}, bf16[2,8,1536]{2,1,0:T(8,128)(2,1)S(1)}, u32[]{:S(2)}, u32[]{:S(2)}) %collective-permute-start.19) | collective-permute-done | bytes 49184 | tf_op jit(solution)/shard_map/ppermute | solution.py:99
  253.7 4.4 %collective-permute-done.18 = bf16[3,8,1536]{2,1,0:T(8,128)(2,1)} collective-permute-done((bf16[3,8,1536]{2,1,0:T(8,128)(2,1)S(1)}, bf16[3,8,1536]{2,1,0:T(8,128)(2,1)}, u32[]{:S(2)}, u32[]{:S(2)}) %collective-permute-start.18) | collective-permute-done | bytes 73760 | tf_op jit(solution)/shard_map/ppermute | solution.py:99
  263.0 2.5 collective-permute-start.26
  267.5 5.0 %collective-permute-done.25 = bf16[8,8,1536]{2,1,0:T(8,128)(2,1)S(1)} collective-permute-done((bf16[8,8,1536]{2,1,0:T(8,128)(2,1)S(1)}, bf16[8,8,1536]{2,1,0:T(8,128)(2,1)S(1)}, u32[]{:S(2)}, u32[]{:S(2)}) %collective-permute-start.25) | collective-permute-done | bytes 196640 | tf_op jit(solution)/shard_map/ppermute | solution.py:99
  274.4 2.6 collective-permute-start.28
  289.1 2.1 collective-permute-start.33
  292.0 4.8 %collective-permute-done.34 = bf16[1,4,8,1536]{3,2,1,0:T(8,128)(2,1)S(1)} collective-permute-done((bf16[1,4,8,1536]{3,2,1,0:T(8,128)(2,1)S(1)}, bf16[1,4,8,1536]{3,2,1,0:T(8,128)(2,1)S(1)}, u32[]{:S(2)}, u32[]{:S(2)}) %collective-permute-start.34) | collective-permute-done | bytes 98336 | tf_op jit(solution)/shard_map/ppermute | solution.py:99
  299.3 4.7 %collective-permute-start.38 = (bf16[2,4,8,1536]{3,2,1,0:T(8,128)(2,1)S(1)}, bf16[2,4,8,1536]{3,2,1,0:T(8,128)(2,1)S(1)}, u32[]{:S(2)}, u32[]{:S(2)}) collective-permute-start(bf16[2,4,8,1536]{3,2,1,0:T(8,128)(2,1)S(1)} %broadcast_select_fusion.1), channel_id=1, source_target_pairs={{0,2},{1,3},{2,0},{3,1},{4,6},{5,7},{6,4},{7,5},{8,10},{9,11},{10,... | collective-permute-start | bytes 589832 | tf_op jit(solution)/shard_map/ppermute | solution.py:99
  307.7 3.7 collective-permute-done.36
  311.8 2.6 collective-permute-start.40
  314.3 2.7 collective-permute-start.41
  317.5 7.9 %collective-permute-done.40 = bf16[4,4,8,1536]{3,2,1,0:T(8,128)(2,1)S(1)} collective-permute-done((bf16[4,4,8,1536]{3,2,1,0:T(8,128)(2,1)S(1)}, bf16[4,4,8,1536]{3,2,1,0:T(8,128)(2,1)S(1)}, u32[]{:S(2)}, u32[]{:S(2)}) %collective-permute-start.40) | collective-permute-done | bytes 393248 | tf_op jit(solution)/shard_map/ppermute | solution.py:99
  329.2 5.2 %collective-permute-start.42 = (bf16[8,5,8,1536]{3,2,1,0:T(8,128)(2,1)S(1)}, bf16[8,5,8,1536]{3,2,1,0:T(8,128)(2,1)}, u32[]{:S(2)}, u32[]{:S(2)}) collective-permute-start(bf16[8,5,8,1536]{3,2,1,0:T(8,128)(2,1)S(1)} %bitcast_select_fusion.5), channel_id=1, source_target_pairs={{0,2},{1,3},{2,0},{3,1},{4,6},{5,7},{6,4},{7,5},{8,10},{9,11},{10,... | collective-permute-start | bytes 2949128 | tf_op jit(solution)/shard_map/ppermute | solution.py:99
  336.4 2.3 collective-permute-start.44
  339.1 7.3 %collective-permute-done.43 = bf16[8,4,8,1536]{3,2,1,0:T(8,128)(2,1)} collective-permute-done((bf16[8,4,8,1536]{3,2,1,0:T(8,128)(2,1)S(1)}, bf16[8,4,8,1536]{3,2,1,0:T(8,128)(2,1)}, u32[]{:S(2)}, u32[]{:S(2)}) %collective-permute-start.43) | collective-permute-done | bytes 786464 | tf_op jit(solution)/shard_map/ppermute | solution.py:99
  346.4 2.3 collective-permute-done.44
  358.9 2.6 copy.58
  363.1 3.0 collective-permute-done.46
  367.3 3.3 slice.105
  371.7 2.4 copy.60
  375.3 9.3 %fusion = (f32[1536,1536]{1,0:T(8,128)}, f32[1536,1536]{1,0:T(8,128)}) fusion(pred[1536]{0:T(1024)(128)(4,1)S(1)} %iota.145, bf16[96,8,1536]{2,1,0:T(8,128)(2,1)} %slice.105, bf16[96,8,1536]{2,1,0:T(8,128)(2,1)S(1)} %copy-done.4, bf16[96,8,1536]{2,1,0:T(8,128)(2,1)} %collective-permute-done.46, bf16[96,8,1536]{2,1,0:T(8,128)(2,1)} %pad_maximum_fusion.2), kind=kLoop, calls=%fused_computation.2 | loop fusion | flops 9437184 | bytes 28313088 | tf_op jit(solution)/shard_map/convert_element_type | solution.py:294
  (309 shorter events, 125.0 us)
Async XLA Ops:
  0.7 15.9 %collective-permute-start.1 = (bf16[1536,512]{1,0:T(8,128)(2,1)}, bf16[1536,512]{1,0:T(8,128)(2,1)}, u32[]{:S(2)}, u32[]{:S(2)}) collective-permute-start(bf16[1536,512]{1,0:T(8,128)(2,1)} %param.9), channel_id=1, source_target_pairs={{0,1},{1,0},{2,3},{3,2},{4,5},{5,4},{6,7},{7,6},{8,9},{9,8},{10,11... | collective-permute-start | bytes 4718600 | tf_op jit(solution)/shard_map/ppermute | solution.py:99
  18.4 45.1 %all-to-all-start = ((bf16[32,2,8,1536]{3,2,1,0:T(8,128)(2,1)}), bf16[32,2,8,1536]{3,2,1,0:T(8,128)(2,1)}, u32[]{:S(2)}, u32[]{:S(2)}) async-start(bf16[32,2,8,1536]{3,2,1,0:T(8,128)(2,1)} %bitcast.177), calls=%async_computation | async-start | bytes 3145728 | tf_op jit(solution)/shard_map/all_to_all | solution.py:217
  67.2 46.6 %all-to-all-start.1 = ((bf16[32,2,8,1536]{3,2,1,0:T(8,128)(2,1)}), bf16[32,2,8,1536]{3,2,1,0:T(8,128)(2,1)}, u32[]{:S(2)}, u32[]{:S(2)}) async-start(bf16[32,2,8,1536]{3,2,1,0:T(8,128)(2,1)} %bitcast.184), calls=%async_computation.1 | async-start | bytes 3145728 | tf_op jit(solution)/shard_map/all_to_all | solution.py:217
  73.4 11.6 %collective-permute-start.3 = (f32[128,128]{1,0:T(8,128)S(1)}, f32[128,128]{1,0:T(8,128)S(1)}, u32[]{:S(2)}, u32[]{:S(2)}) collective-permute-start(f32[128,128]{1,0:T(8,128)S(1)} %add.241), channel_id=1, source_target_pairs={{0,2},{1,3},{2,0},{3,1},{4,6},{5,7},{6,4},{7,5},{8,10},{9,11},{10,... | collective-permute-start | bytes 196616 | tf_op jit(solution)/shard_map/ppermute | solution.py:99
  85.0 5.2 %collective-permute-start.4 = (f32[128,128]{1,0:T(8,128)S(1)}, f32[128,128]{1,0:T(8,128)S(1)}, u32[]{:S(2)}, u32[]{:S(2)}) collective-permute-start(f32[128,128]{1,0:T(8,128)S(1)} %add.242), channel_id=1, source_target_pairs={{0,4},{1,5},{2,6},{3,7},{4,0},{5,1},{6,2},{7,3},{8,12},{9,13},{10,... | collective-permute-start | bytes 196616 | tf_op jit(solution)/shard_map/ppermute | solution.py:99
  90.2 8.5 %collective-permute-start.5 = (f32[128,128]{1,0:T(8,128)S(1)}, f32[128,128]{1,0:T(8,128)S(1)}, u32[]{:S(2)}, u32[]{:S(2)}) collective-permute-start(f32[128,128]{1,0:T(8,128)S(1)} %add.243), channel_id=1, source_target_pairs={{0,8},{1,9},{2,10},{3,11},{4,12},{5,13},{6,14},{7,15},{8,0},{9,1},... | collective-permute-start | bytes 196616 | tf_op jit(solution)/shard_map/ppermute | solution.py:99
  99.4 12.1 %collective-permute-start.6 = (f32[128,128]{1,0:T(8,128)}, f32[128,128]{1,0:T(8,128)}, u32[]{:S(2)}, u32[]{:S(2)}) collective-permute-start(f32[128,128]{1,0:T(8,128)} %add.244), channel_id=1, source_target_pairs={{0,16},{1,17},{2,18},{3,19},{4,20},{5,21},{6,22},{7,23},{8,24},{9,... | collective-permute-start | bytes 196616 | tf_op jit(solution)/shard_map/ppermute | solution.py:99
  117.2 7.9 %collective-permute-start.8 = (bf16[512,768]{1,0:T(8,128)(2,1)}, bf16[512,768]{1,0:T(8,128)(2,1)}, u32[]{:S(2)}, u32[]{:S(2)}) collective-permute-start(bf16[512,768]{1,0:T(8,128)(2,1)} %get-tuple-element.220), channel_id=1, source_target_pairs={{0,1},{1,0},{2,3},{3,2},{4,5},{5,4},{6,7},{7,6},{8,9},{9,8},{10,11... | collective-permute-start | bytes 2359304 | tf_op jit(solution)/shard_map/ppermute | solution.py:99
  120.8 52.0 %all-to-all-start.2 = ((bf16[32,2,8,1536]{3,2,1,0:T(8,128)(2,1)}), bf16[32,2,8,1536]{3,2,1,0:T(8,128)(2,1)}, u32[]{:S(2)}, u32[]{:S(2)}) async-start(bf16[32,2,8,1536]{3,2,1,0:T(8,128)(2,1)} %bitcast.176), calls=%async_computation.2 | async-start | bytes 3145728 | tf_op jit(solution)/shard_map/all_to_all | solution.py:217
  133.7 26.1 %collective-permute-start.9 = (bf16[24,8,1536]{2,1,0:T(8,128)(2,1)}, bf16[24,8,1536]{2,1,0:T(8,128)(2,1)}, u32[]{:S(2)}, u32[]{:S(2)}) collective-permute-start(bf16[24,8,1536]{2,1,0:T(8,128)(2,1)} %dynamic-slice_convert_fusion), channel_id=1, source_target_pairs={{0,2},{1,3},{2,0},{3,1},{4,6},{5,7},{6,4},{7,5},{8,10},{9,11},{10,... | collective-permute-start | bytes 1769480 | tf_op jit(solution)/shard_map/ppermute | solution.py:99
  135.2 17.4 %collective-permute-start.10 = (bf16[16,8,1536]{2,1,0:T(8,128)(2,1)}, bf16[16,8,1536]{2,1,0:T(8,128)(2,1)}, u32[]{:S(2)}, u32[]{:S(2)}) collective-permute-start(bf16[16,8,1536]{2,1,0:T(8,128)(2,1)} %dynamic-slice_convert_fusion.5), channel_id=1, source_target_pairs={{0,4},{1,5},{2,6},{3,7},{4,0},{5,1},{6,2},{7,3},{8,12},{9,13},{10,... | collective-permute-start | bytes 1179656 | tf_op jit(solution)/shard_map/ppermute | solution.py:99
  136.7 23.1 %collective-permute-start.11 = (bf16[16,8,1536]{2,1,0:T(8,128)(2,1)}, bf16[16,8,1536]{2,1,0:T(8,128)(2,1)}, u32[]{:S(2)}, u32[]{:S(2)}) collective-permute-start(bf16[16,8,1536]{2,1,0:T(8,128)(2,1)} %dynamic-slice_convert_fusion.4), channel_id=1, source_target_pairs={{0,8},{1,9},{2,10},{3,11},{4,12},{5,13},{6,14},{7,15},{8,0},{9,1},... | collective-permute-start | bytes 1179656 | tf_op jit(solution)/shard_map/ppermute | solution.py:99
  166.8 16.5 %collective-permute-start.13 = (bf16[8,8,1536]{2,1,0:T(8,128)(2,1)}, bf16[8,8,1536]{2,1,0:T(8,128)(2,1)}, u32[]{:S(2)}, u32[]{:S(2)}) collective-permute-start(bf16[8,8,1536]{2,1,0:T(8,128)(2,1)} %dynamic-slice_convert_fusion.11), channel_id=1, source_target_pairs={{0,8},{1,9},{2,10},{3,11},{4,12},{5,13},{6,14},{7,15},{8,0},{9,1},... | collective-permute-start | bytes 589832 | tf_op jit(solution)/shard_map/ppermute | solution.py:99
  169.4 13.9 %collective-permute-start.14 = (bf16[8,8,1536]{2,1,0:T(8,128)(2,1)}, bf16[8,8,1536]{2,1,0:T(8,128)(2,1)}, u32[]{:S(2)}, u32[]{:S(2)}) collective-permute-start(bf16[8,8,1536]{2,1,0:T(8,128)(2,1)} %dynamic-slice_convert_fusion.10), channel_id=1, source_target_pairs={{0,16},{1,17},{2,18},{3,19},{4,20},{5,21},{6,22},{7,23},{8,24},{9,... | collective-permute-start | bytes 589832 | tf_op jit(solution)/shard_map/ppermute | solution.py:99
  171.1 12.2 %collective-permute-start.12 = (bf16[12,8,1536]{2,1,0:T(8,128)(2,1)S(1)}, bf16[12,8,1536]{2,1,0:T(8,128)(2,1)}, u32[]{:S(2)}, u32[]{:S(2)}) collective-permute-start(bf16[12,8,1536]{2,1,0:T(8,128)(2,1)S(1)} %dynamic-slice_convert_fusion.6), channel_id=1, source_target_pairs={{0,4},{1,5},{2,6},{3,7},{4,0},{5,1},{6,2},{7,3},{8,12},{9,13},{10,... | collective-permute-start | bytes 884744 | tf_op jit(solution)/shard_map/ppermute | solution.py:99
  176.5 46.7 %all-to-all-start.3 = ((bf16[32,2,8,1536]{3,2,1,0:T(8,128)(2,1)}), bf16[32,2,8,1536]{3,2,1,0:T(8,128)(2,1)}, u32[]{:S(2)}, u32[]{:S(2)}) async-start(bf16[32,2,8,1536]{3,2,1,0:T(8,128)(2,1)} %bitcast.185), calls=%async_computation.3 | async-start | bytes 3145728 | tf_op jit(solution)/shard_map/all_to_all | solution.py:217
  187.3 34.5 %collective-permute-start.16 = (bf16[4,8,1536]{2,1,0:T(8,128)(2,1)S(1)}, bf16[4,8,1536]{2,1,0:T(8,128)(2,1)S(1)}, u32[]{:S(2)}, u32[]{:S(2)}) collective-permute-start(bf16[4,8,1536]{2,1,0:T(8,128)(2,1)S(1)} %dynamic-slice_convert_fusion.17), channel_id=1, source_target_pairs={{0,16},{1,17},{2,18},{3,19},{4,20},{5,21},{6,22},{7,23},{8,24},{9,... | collective-permute-start | bytes 294920 | tf_op jit(solution)/shard_map/ppermute | solution.py:99
  190.0 31.8 %collective-permute-start.17 = (bf16[4,8,1536]{2,1,0:T(8,128)(2,1)S(1)}, bf16[4,8,1536]{2,1,0:T(8,128)(2,1)S(1)}, u32[]{:S(2)}, u32[]{:S(2)}) collective-permute-start(bf16[4,8,1536]{2,1,0:T(8,128)(2,1)S(1)} %dynamic-slice_convert_fusion.16), channel_id=1, source_target_pairs={{0,2},{1,3},{2,0},{3,1},{4,6},{5,7},{6,4},{7,5},{8,10},{9,11},{10,... | collective-permute-start | bytes 294920 | tf_op jit(solution)/shard_map/ppermute | solution.py:99
  191.5 30.4 %collective-permute-start.15 = (bf16[6,8,1536]{2,1,0:T(8,128)(2,1)S(1)}, bf16[6,8,1536]{2,1,0:T(8,128)(2,1)}, u32[]{:S(2)}, u32[]{:S(2)}) collective-permute-start(bf16[6,8,1536]{2,1,0:T(8,128)(2,1)S(1)} %dynamic-slice_convert_fusion.12), channel_id=1, source_target_pairs={{0,8},{1,9},{2,10},{3,11},{4,12},{5,13},{6,14},{7,15},{8,0},{9,1},... | collective-permute-start | bytes 442376 | tf_op jit(solution)/shard_map/ppermute | solution.py:99
  240.4 17.8 %collective-permute-start.21 = (bf16[16,8,1536]{2,1,0:T(8,128)(2,1)}, bf16[16,8,1536]{2,1,0:T(8,128)(2,1)}, u32[]{:S(2)}, u32[]{:S(2)}) collective-permute-start(bf16[16,8,1536]{2,1,0:T(8,128)(2,1)} %dynamic-slice_convert_fusion.3), channel_id=1, source_target_pairs={{0,2},{1,3},{2,0},{3,1},{4,6},{5,7},{6,4},{7,5},{8,10},{9,11},{10,... | collective-permute-start | bytes 1179656 | tf_op jit(solution)/shard_map/ppermute | solution.py:99
  241.5 16.6 %collective-permute-start.22 = (bf16[16,8,1536]{2,1,0:T(8,128)(2,1)}, bf16[16,8,1536]{2,1,0:T(8,128)(2,1)}, u32[]{:S(2)}, u32[]{:S(2)}) collective-permute-start(bf16[16,8,1536]{2,1,0:T(8,128)(2,1)} %dynamic-slice_convert_fusion.2), channel_id=1, source_target_pairs={{0,4},{1,5},{2,6},{3,7},{4,0},{5,1},{6,2},{7,3},{8,12},{9,13},{10,... | collective-permute-start | bytes 1179656 | tf_op jit(solution)/shard_map/ppermute | solution.py:99
  243.1 15.1 %collective-permute-start.23 = (bf16[16,8,1536]{2,1,0:T(8,128)(2,1)}, bf16[16,8,1536]{2,1,0:T(8,128)(2,1)}, u32[]{:S(2)}, u32[]{:S(2)}) collective-permute-start(bf16[16,8,1536]{2,1,0:T(8,128)(2,1)} %dynamic-slice_convert_fusion.1), channel_id=1, source_target_pairs={{0,8},{1,9},{2,10},{3,11},{4,12},{5,13},{6,14},{7,15},{8,0},{9,1},... | collective-permute-start | bytes 1179656 | tf_op jit(solution)/shard_map/ppermute | solution.py:99
  244.6 8.2 %collective-permute-start.19 = (bf16[2,8,1536]{2,1,0:T(8,128)(2,1)S(1)}, bf16[2,8,1536]{2,1,0:T(8,128)(2,1)S(1)}, u32[]{:S(2)}, u32[]{:S(2)}) collective-permute-start(bf16[2,8,1536]{2,1,0:T(8,128)(2,1)S(1)} %dynamic-slice_convert_fusion.23), channel_id=1, source_target_pairs={{0,2},{1,3},{2,0},{3,1},{4,6},{5,7},{6,4},{7,5},{8,10},{9,11},{10,... | collective-permute-start | bytes 147464 | tf_op jit(solution)/shard_map/ppermute | solution.py:99
  245.1 8.6 %collective-permute-start.20 = (bf16[2,8,1536]{2,1,0:T(8,128)(2,1)}, bf16[2,8,1536]{2,1,0:T(8,128)(2,1)}, u32[]{:S(2)}, u32[]{:S(2)}) collective-permute-start(bf16[2,8,1536]{2,1,0:T(8,128)(2,1)} %dynamic-slice_convert_fusion.22), channel_id=1, source_target_pairs={{0,4},{1,5},{2,6},{3,7},{4,0},{5,1},{6,2},{7,3},{8,12},{9,13},{10,... | collective-permute-start | bytes 147464 | tf_op jit(solution)/shard_map/ppermute | solution.py:99
  252.8 5.4 %collective-permute-start.18 = (bf16[3,8,1536]{2,1,0:T(8,128)(2,1)S(1)}, bf16[3,8,1536]{2,1,0:T(8,128)(2,1)}, u32[]{:S(2)}, u32[]{:S(2)}) collective-permute-start(bf16[3,8,1536]{2,1,0:T(8,128)(2,1)S(1)} %dynamic-slice_convert_fusion.18), channel_id=1, source_target_pairs={{0,16},{1,17},{2,18},{3,19},{4,20},{5,21},{6,22},{7,23},{8,24},{9,... | collective-permute-start | bytes 221192 | tf_op jit(solution)/shard_map/ppermute | solution.py:99
  261.8 5.7 %collective-permute-start.24 = (bf16[8,8,1536]{2,1,0:T(8,128)(2,1)S(1)}, bf16[8,8,1536]{2,1,0:T(8,128)(2,1)S(1)}, u32[]{:S(2)}, u32[]{:S(2)}) collective-permute-start(bf16[8,8,1536]{2,1,0:T(8,128)(2,1)S(1)} %dynamic-slice_convert_fusion.9), channel_id=1, source_target_pairs={{0,4},{1,5},{2,6},{3,7},{4,0},{5,1},{6,2},{7,3},{8,12},{9,13},{10,... | collective-permute-start | bytes 589832 | tf_op jit(solution)/shard_map/ppermute | solution.py:99
  263.0 9.5 %collective-permute-start.25 = (bf16[8,8,1536]{2,1,0:T(8,128)(2,1)S(1)}, bf16[8,8,1536]{2,1,0:T(8,128)(2,1)S(1)}, u32[]{:S(2)}, u32[]{:S(2)}) collective-permute-start(bf16[8,8,1536]{2,1,0:T(8,128)(2,1)S(1)} %dynamic-slice_convert_fusion.8), channel_id=1, source_target_pairs={{0,8},{1,9},{2,10},{3,11},{4,12},{5,13},{6,14},{7,15},{8,0},{9,1},... | collective-permute-start | bytes 589832 | tf_op jit(solution)/shard_map/ppermute | solution.py:99
  263.0 10.8 %collective-permute-start.26 = (bf16[8,8,1536]{2,1,0:T(8,128)(2,1)S(1)}, bf16[8,8,1536]{2,1,0:T(8,128)(2,1)S(1)}, u32[]{:S(2)}, u32[]{:S(2)}) collective-permute-start(bf16[8,8,1536]{2,1,0:T(8,128)(2,1)S(1)} %dynamic-slice_convert_fusion.7), channel_id=1, source_target_pairs={{0,16},{1,17},{2,18},{3,19},{4,20},{5,21},{6,22},{7,23},{8,24},{9,... | collective-permute-start | bytes 589832 | tf_op jit(solution)/shard_map/ppermute | solution.py:99
  274.0 6.3 %collective-permute-start.27 = (bf16[4,8,1536]{2,1,0:T(8,128)(2,1)S(1)}, bf16[4,8,1536]{2,1,0:T(8,128)(2,1)S(1)}, u32[]{:S(2)}, u32[]{:S(2)}) collective-permute-start(bf16[4,8,1536]{2,1,0:T(8,128)(2,1)S(1)} %dynamic-slice_convert_fusion.15), channel_id=1, source_target_pairs={{0,8},{1,9},{2,10},{3,11},{4,12},{5,13},{6,14},{7,15},{8,0},{9,1},... | collective-permute-start | bytes 294920 | tf_op jit(solution)/shard_map/ppermute | solution.py:99
  274.4 5.9 %collective-permute-start.28 = (bf16[4,8,1536]{2,1,0:T(8,128)(2,1)S(1)}, bf16[4,8,1536]{2,1,0:T(8,128)(2,1)S(1)}, u32[]{:S(2)}, u32[]{:S(2)}) collective-permute-start(bf16[4,8,1536]{2,1,0:T(8,128)(2,1)S(1)} %dynamic-slice_convert_fusion.14), channel_id=1, source_target_pairs={{0,16},{1,17},{2,18},{3,19},{4,20},{5,21},{6,22},{7,23},{8,24},{9,... | collective-permute-start | bytes 294920 | tf_op jit(solution)/shard_map/ppermute | solution.py:99
  277.0 4.7 %collective-permute-start.29 = (bf16[4,8,1536]{2,1,0:T(8,128)(2,1)S(1)}, bf16[4,8,1536]{2,1,0:T(8,128)(2,1)S(1)}, u32[]{:S(2)}, u32[]{:S(2)}) collective-permute-start(bf16[4,8,1536]{2,1,0:T(8,128)(2,1)S(1)} %dynamic-slice_convert_fusion.13), channel_id=1, source_target_pairs={{0,2},{1,3},{2,0},{3,1},{4,6},{5,7},{6,4},{7,5},{8,10},{9,11},{10,... | collective-permute-start | bytes 294920 | tf_op jit(solution)/shard_map/ppermute | solution.py:99
  281.9 5.2 %collective-permute-start.30 = (bf16[2,8,1536]{2,1,0:T(8,128)(2,1)S(1)}, bf16[2,8,1536]{2,1,0:T(8,128)(2,1)S(1)}, u32[]{:S(2)}, u32[]{:S(2)}) collective-permute-start(bf16[2,8,1536]{2,1,0:T(8,128)(2,1)S(1)} %dynamic-slice_convert_fusion.21), channel_id=1, source_target_pairs={{0,16},{1,17},{2,18},{3,19},{4,20},{5,21},{6,22},{7,23},{8,24},{9,... | collective-permute-start | bytes 147464 | tf_op jit(solution)/shard_map/ppermute | solution.py:99
  282.8 4.2 %collective-permute-start.31 = (bf16[2,8,1536]{2,1,0:T(8,128)(2,1)S(1)}, bf16[2,8,1536]{2,1,0:T(8,128)(2,1)S(1)}, u32[]{:S(2)}, u32[]{:S(2)}) collective-permute-start(bf16[2,8,1536]{2,1,0:T(8,128)(2,1)S(1)} %dynamic-slice_convert_fusion.20), channel_id=1, source_target_pairs={{0,2},{1,3},{2,0},{3,1},{4,6},{5,7},{6,4},{7,5},{8,10},{9,11},{10,... | collective-permute-start | bytes 147464 | tf_op jit(solution)/shard_map/ppermute | solution.py:99
  284.4 4.6 %collective-permute-start.32 = (bf16[2,8,1536]{2,1,0:T(8,128)(2,1)S(1)}, bf16[2,8,1536]{2,1,0:T(8,128)(2,1)S(1)}, u32[]{:S(2)}, u32[]{:S(2)}) collective-permute-start(bf16[2,8,1536]{2,1,0:T(8,128)(2,1)S(1)} %dynamic-slice_convert_fusion.19), channel_id=1, source_target_pairs={{0,4},{1,5},{2,6},{3,7},{4,0},{5,1},{6,2},{7,3},{8,12},{9,13},{10,... | collective-permute-start | bytes 147464 | tf_op jit(solution)/shard_map/ppermute | solution.py:99
  289.1 8.3 %collective-permute-start.33 = (bf16[1,5,8,1536]{3,2,1,0:T(8,128)(2,1)S(1)}, bf16[1,5,8,1536]{3,2,1,0:T(8,128)(2,1)S(1)}, u32[]{:S(2)}, u32[]{:S(2)}) collective-permute-start(bf16[1,5,8,1536]{3,2,1,0:T(8,128)(2,1)S(1)} %maximum_bitcast_fusion), channel_id=1, source_target_pairs={{0,16},{1,17},{2,18},{3,19},{4,20},{5,21},{6,22},{7,23},{8,24},{9,... | collective-permute-start | bytes 368648 | tf_op jit(solution)/shard_map/ppermute | solution.py:99
  291.2 5.6 %collective-permute-start.34 = (bf16[1,4,8,1536]{3,2,1,0:T(8,128)(2,1)S(1)}, bf16[1,4,8,1536]{3,2,1,0:T(8,128)(2,1)S(1)}, u32[]{:S(2)}, u32[]{:S(2)}) collective-permute-start(bf16[1,4,8,1536]{3,2,1,0:T(8,128)(2,1)S(1)} %maximum_bitcast_fusion.1), channel_id=1, source_target_pairs={{0,2},{1,3},{2,0},{3,1},{4,6},{5,7},{6,4},{7,5},{8,10},{9,11},{10,... | collective-permute-start | bytes 294920 | tf_op jit(solution)/shard_map/ppermute | solution.py:99
  291.7 5.1 %collective-permute-start.35 = (bf16[1,4,8,1536]{3,2,1,0:T(8,128)(2,1)S(1)}, bf16[1,4,8,1536]{3,2,1,0:T(8,128)(2,1)S(1)}, u32[]{:S(2)}, u32[]{:S(2)}) collective-permute-start(bf16[1,4,8,1536]{3,2,1,0:T(8,128)(2,1)S(1)} %maximum_bitcast_fusion.2), channel_id=1, source_target_pairs={{0,4},{1,5},{2,6},{3,7},{4,0},{5,1},{6,2},{7,3},{8,12},{9,13},{10,... | collective-permute-start | bytes 294920 | tf_op jit(solution)/shard_map/ppermute | solution.py:99
  297.7 13.6 %collective-permute-start.36 = (bf16[2,5,8,1536]{3,2,1,0:T(8,128)(2,1)S(1)}, bf16[2,5,8,1536]{3,2,1,0:T(8,128)(2,1)S(1)}, u32[]{:S(2)}, u32[]{:S(2)}) collective-permute-start(bf16[2,5,8,1536]{3,2,1,0:T(8,128)(2,1)S(1)} %broadcast_select_fusion), channel_id=1, source_target_pairs={{0,8},{1,9},{2,10},{3,11},{4,12},{5,13},{6,14},{7,15},{8,0},{9,1},... | collective-permute-start | bytes 737288 | tf_op jit(solution)/shard_map/ppermute | solution.py:99
  298.1 8.4 %collective-permute-start.37 = (bf16[2,4,8,1536]{3,2,1,0:T(8,128)(2,1)S(1)}, bf16[2,4,8,1536]{3,2,1,0:T(8,128)(2,1)S(1)}, u32[]{:S(2)}, u32[]{:S(2)}) collective-permute-start(bf16[2,4,8,1536]{3,2,1,0:T(8,128)(2,1)S(1)} %broadcast_select_fusion.2), channel_id=1, source_target_pairs={{0,16},{1,17},{2,18},{3,19},{4,20},{5,21},{6,22},{7,23},{8,24},{9,... | collective-permute-start | bytes 589832 | tf_op jit(solution)/shard_map/ppermute | solution.py:99
  299.3 8.3 %collective-permute-start.38 = (bf16[2,4,8,1536]{3,2,1,0:T(8,128)(2,1)S(1)}, bf16[2,4,8,1536]{3,2,1,0:T(8,128)(2,1)S(1)}, u32[]{:S(2)}, u32[]{:S(2)}) collective-permute-start(bf16[2,4,8,1536]{3,2,1,0:T(8,128)(2,1)S(1)} %broadcast_select_fusion.1), channel_id=1, source_target_pairs={{0,2},{1,3},{2,0},{3,1},{4,6},{5,7},{6,4},{7,5},{8,10},{9,11},{10,... | collective-permute-start | bytes 589832 | tf_op jit(solution)/shard_map/ppermute | solution.py:99
  311.7 16.0 %collective-permute-start.39 = (bf16[4,5,8,1536]{3,2,1,0:T(8,128)(2,1)S(1)}, bf16[4,5,8,1536]{3,2,1,0:T(8,128)(2,1)S(1)}, u32[]{:S(2)}, u32[]{:S(2)}) collective-permute-start(bf16[4,5,8,1536]{3,2,1,0:T(8,128)(2,1)S(1)} %bitcast_select_fusion.8), channel_id=1, source_target_pairs={{0,4},{1,5},{2,6},{3,7},{4,0},{5,1},{6,2},{7,3},{8,12},{9,13},{10,... | collective-permute-start | bytes 1474568 | tf_op jit(solution)/shard_map/ppermute | solution.py:99
  311.8 13.6 %collective-permute-start.40 = (bf16[4,4,8,1536]{3,2,1,0:T(8,128)(2,1)S(1)}, bf16[4,4,8,1536]{3,2,1,0:T(8,128)(2,1)S(1)}, u32[]{:S(2)}, u32[]{:S(2)}) collective-permute-start(bf16[4,4,8,1536]{3,2,1,0:T(8,128)(2,1)S(1)} %bitcast_select_fusion.12), channel_id=1, source_target_pairs={{0,8},{1,9},{2,10},{3,11},{4,12},{5,13},{6,14},{7,15},{8,0},{9,1},... | collective-permute-start | bytes 1179656 | tf_op jit(solution)/shard_map/ppermute | solution.py:99
  314.3 12.6 %collective-permute-start.41 = (bf16[4,4,8,1536]{3,2,1,0:T(8,128)(2,1)S(1)}, bf16[4,4,8,1536]{3,2,1,0:T(8,128)(2,1)S(1)}, u32[]{:S(2)}, u32[]{:S(2)}) collective-permute-start(bf16[4,4,8,1536]{3,2,1,0:T(8,128)(2,1)S(1)} %bitcast_select_fusion.11), channel_id=1, source_target_pairs={{0,16},{1,17},{2,18},{3,19},{4,20},{5,21},{6,22},{7,23},{8,24},{9,... | collective-permute-start | bytes 1179656 | tf_op jit(solution)/shard_map/ppermute | solution.py:99
  329.2 19.5 %collective-permute-start.42 = (bf16[8,5,8,1536]{3,2,1,0:T(8,128)(2,1)S(1)}, bf16[8,5,8,1536]{3,2,1,0:T(8,128)(2,1)}, u32[]{:S(2)}, u32[]{:S(2)}) collective-permute-start(bf16[8,5,8,1536]{3,2,1,0:T(8,128)(2,1)S(1)} %bitcast_select_fusion.5), channel_id=1, source_target_pairs={{0,2},{1,3},{2,0},{3,1},{4,6},{5,7},{6,4},{7,5},{8,10},{9,11},{10,... | collective-permute-start | bytes 2949128 | tf_op jit(solution)/shard_map/ppermute | solution.py:99
  334.3 12.1 %collective-permute-start.43 = (bf16[8,4,8,1536]{3,2,1,0:T(8,128)(2,1)S(1)}, bf16[8,4,8,1536]{3,2,1,0:T(8,128)(2,1)}, u32[]{:S(2)}, u32[]{:S(2)}) collective-permute-start(bf16[8,4,8,1536]{3,2,1,0:T(8,128)(2,1)S(1)} %bitcast_select_fusion.7), channel_id=1, source_target_pairs={{0,4},{1,5},{2,6},{3,7},{4,0},{5,1},{6,2},{7,3},{8,12},{9,13},{10,... | collective-permute-start | bytes 2359304 | tf_op jit(solution)/shard_map/ppermute | solution.py:99
  336.4 12.3 %collective-permute-start.44 = (bf16[8,4,8,1536]{3,2,1,0:T(8,128)(2,1)S(1)}, bf16[8,4,8,1536]{3,2,1,0:T(8,128)(2,1)}, u32[]{:S(2)}, u32[]{:S(2)}) collective-permute-start(bf16[8,4,8,1536]{3,2,1,0:T(8,128)(2,1)S(1)} %bitcast_select_fusion.6), channel_id=1, source_target_pairs={{0,8},{1,9},{2,10},{3,11},{4,12},{5,13},{6,14},{7,15},{8,0},{9,1},... | collective-permute-start | bytes 2359304 | tf_op jit(solution)/shard_map/ppermute | solution.py:99
  357.7 8.6 %collective-permute-start.45 = (bf16[112,8,1536]{2,1,0:T(8,128)(2,1)S(1)}, bf16[112,8,1536]{2,1,0:T(8,128)(2,1)}, u32[]{:S(2)}, u32[]{:S(2)}) collective-permute-start(bf16[112,8,1536]{2,1,0:T(8,128)(2,1)S(1)} %pad_maximum_fusion.1), channel_id=1, source_target_pairs={{0,1},{1,0},{2,3},{3,2},{4,5},{5,4},{6,7},{7,6},{8,9},{9,8},{10,11... | collective-permute-start | bytes 8257544 | tf_op jit(solution)/shard_map/ppermute | solution.py:99
  357.7 8.4 %collective-permute-start.46 = (bf16[96,8,1536]{2,1,0:T(8,128)(2,1)}, bf16[96,8,1536]{2,1,0:T(8,128)(2,1)}, u32[]{:S(2)}, u32[]{:S(2)}) collective-permute-start(bf16[96,8,1536]{2,1,0:T(8,128)(2,1)} %pad_maximum_fusion.2), channel_id=1, source_target_pairs={{0,1},{1,0},{2,3},{3,2},{4,5},{5,4},{6,7},{7,6},{8,9},{9,8},{10,11... | collective-permute-start | bytes 7077896 | tf_op jit(solution)/shard_map/ppermute | solution.py:99
  (52 other events, 240.6 us)
